TPU v7x, 32 devices: a whole 2x2x4 slice. The times are simulated.
32 devices in a mesh: section: 4 (over y, core), expert: 8 (over z, x).
Axes of the slice: x: 2, y: 2, z: 4, core: 2. Of those that a mesh axis runs over, the one named last changes fastest.
Arguments:
- saved_inputs: bfloat16 [4, 2, 64, 2048], P('section', None, 'expert'), may hold values from -6 to 6
- top_grad: bfloat16 [2, 64, 2048], P(None, 'expert'), may hold values from -6 to 6
- expert_ids: int32 [4, 2, 64, 2], P('section', None, 'expert'), may hold values from 0 to 7, all different within a row; in each aligned block of 8 rows (0 to 7, 8 to 15, ..., all dimensions but the last counted through in order) at most 3 rows name the same one
- route_weights: bfloat16 [4, 2, 64, 2], P('section', None, 'expert'), may hold values from 0.099609375 to 0.59765625
- example_ids: int32 [2, 64], P(None, 'expert'), may hold values from 0 to 3, never falling along the last dimension, each value on 1 to 32 neighbouring positions
- gate_weight: bfloat16 [4, 12288, 2048], P('section', 'expert'), may hold values from -0.125 to 0.125
- up_weight: bfloat16 [4, 12288, 2048], P('section', 'expert'), may hold values from -0.125 to 0.125
- down_weight: bfloat16 [4, 12288, 2048], P('section', 'expert'), may hold values from -0.15625 to 0.15625
- left_proj: bfloat16 [4, 12288, 64], P('section', 'expert'), may hold values from -0.15625 to 0.15625
- right_proj: bfloat16 [4, 2048, 64], P('section'), may hold values from -0.125 to 0.125
Outputs:
- input_grads: bfloat16 [4, 2, 64, 2048], P('section', None, 'expert')
- sketches: float32 [4, 64, 4096], P('section', 'expert')
Inputs may be any that keep to these rules, and one draw needn't show every extreme that they name: `expert_ids`: each row names 2 different experts; in each aligned block of 8 rows (one device's tokens of one layer and micro-batch) no expert is named by more than 3 rows, and some block reaches 3. `example_ids`: along each micro-batch the example number never falls and every example has a token.
All inputs are finite; a program needn't handle non-finite values.
Results may differ from a plain program's by a relative error of at most 0.028.
Values may be sent and summed in bfloat16 or wider, within the bound.
No kernel may reach another device: no remote copies, remote signals or barrier semaphores. Data moves between devices by JAX's collectives and lax.ppermute only.
A program may use at most 64 MiB of HBM per device.

v0:
```python
import jax
import jax.numpy as jnp
from jax import lax
from jax.sharding import PartitionSpec as P

EXPERTS = 8
EXM = 4
CAP = 3


def from_behind(block, axis, distance):
    devices = range(lax.axis_size(axis))
    route = [(i - distance, i) for i in devices if i - distance in devices]
    return lax.ppermute(block, axis, route)


def on_device(
    saved_inputs,
    top_grad,
    expert_ids,
    route_weights,
    example_ids,
    gate_weight,
    up_weight,
    down_weight,
    left_proj,
    right_proj,
):
    n_section = lax.axis_size("section")
    n_expert = lax.axis_size("expert")
    section_id = lax.axis_index("section")
    groups = EXPERTS
    hsplit = n_expert // groups
    n_micro = saved_inputs.shape[1]
    tok_dev = saved_inputs.shape[2]
    feat_dim = saved_inputs.shape[3]
    top_k = expert_ids.shape[3]
    n_pairs = tok_dev * top_k
    n_slots = groups * CAP
    n_rows = n_expert * CAP
    sketch_dim = left_proj.shape[2]
    q_total = n_micro * EXM * groups
    inputs = saved_inputs[0]
    ids_flat = expert_ids[0].reshape(n_micro, n_pairs)
    weights_flat = route_weights[0].reshape(n_micro, n_pairs).astype(jnp.float32)
    onehot = (ids_flat[:, :, None] == jnp.arange(groups, dtype=jnp.int32)[None, None, :]).astype(
        jnp.int32
    )
    before = jnp.cumsum(onehot, axis=1) - onehot
    position = jnp.sum(before * onehot, axis=2)
    slot_of = ids_flat * CAP + position
    select = (slot_of[:, None, :] == jnp.arange(n_slots, dtype=jnp.int32)[None, :, None]).astype(
        jnp.float32
    )
    token_select = select.reshape(n_micro, n_slots, tok_dev, top_k).sum(axis=3)
    token_select_b = token_select.astype(jnp.bfloat16)
    slot_weight = jnp.einsum("msp,mp->ms", select, weights_flat, precision=lax.Precision.HIGHEST)
    slot_rows = jnp.einsum(
        "mst,mtd->msd", token_select_b, inputs, preferred_element_type=jnp.float32
    ).astype(jnp.bfloat16)
    send_rows = jnp.repeat(slot_rows.reshape(n_micro, groups, CAP, feat_dim), hsplit, axis=1)
    send_weight = jnp.repeat(
        slot_weight.reshape(n_micro, groups, CAP).astype(jnp.bfloat16), hsplit, axis=1
    )
    recv_rows, recv_weight = (
        lax.all_to_all(send_rows, "expert", split_axis=1, concat_axis=1, tiled=True),
        lax.all_to_all(send_weight, "expert", split_axis=1, concat_axis=1, tiled=True),
    )
    expert_rows = recv_rows.reshape(n_micro, n_rows, feat_dim)
    expert_weight = recv_weight.reshape(n_micro, n_rows).astype(jnp.float32)
    w_gate = gate_weight[0]
    w_up = up_weight[0]
    w_down = down_weight[0]
    pre_gate = jnp.einsum("mrd,hd->mrh", expert_rows, w_gate, preferred_element_type=jnp.float32)
    pre_up = jnp.einsum("mrd,hd->mrh", expert_rows, w_up, preferred_element_type=jnp.float32)
    hidden = (pre_gate * jax.nn.sigmoid(pre_gate) * pre_up).astype(jnp.bfloat16)
    left_part = jnp.einsum(
        "mrh,hq->mrq", hidden, left_proj[0], preferred_element_type=jnp.float32
    ).astype(jnp.bfloat16)
    proj_right = right_proj[0]
    lag = n_section - 1 - section_id
    n_steps = n_section + n_micro - 1

    def one_step(step_num, loop_state):
        sending, grads_out, sketch = loop_state
        incoming = from_behind(sending, "section", -1)
        micro_idx = step_num - lag
        is_live = (micro_idx >= 0) & (micro_idx < n_micro)
        current = jnp.clip(micro_idx, 0, n_micro - 1)
        top_rows = lax.dynamic_index_in_dim(top_grad, current, 0, keepdims=False)
        out_grad = jnp.where(section_id == n_section - 1, top_rows, incoming)
        chosen = lax.dynamic_index_in_dim(token_select_b, current, 0, keepdims=False)
        grad_rows = jnp.dot(chosen, out_grad, preferred_element_type=jnp.float32).astype(
            jnp.bfloat16
        )
        spread_rows = jnp.repeat(grad_rows.reshape(groups, CAP, feat_dim), hsplit, axis=0)
        arrived = lax.all_to_all(spread_rows, "expert", split_axis=0, concat_axis=0, tiled=True)
        rows_weight = lax.dynamic_index_in_dim(expert_weight, current, 0, keepdims=False)
        gate_now = lax.dynamic_index_in_dim(pre_gate, current, 0, keepdims=False)
        up_now = lax.dynamic_index_in_dim(pre_up, current, 0, keepdims=False)
        left_now = lax.dynamic_index_in_dim(left_part, current, 0, keepdims=False)

        def backward(arrived_rows):
            grad_in = arrived_rows.reshape(n_rows, feat_dim)
            grad_hidden = (
                jnp.einsum("rd,hd->rh", grad_in, w_down, preferred_element_type=jnp.float32)
                * rows_weight[:, None]
            )
            sigmoid_g = jax.nn.sigmoid(gate_now)
            grad_gate = (
                grad_hidden * up_now * sigmoid_g * (1.0 + gate_now * (1.0 - sigmoid_g))
            ).astype(jnp.bfloat16)
            grad_up = (grad_hidden * gate_now * sigmoid_g).astype(jnp.bfloat16)
            part_grad = jnp.dot(grad_gate, w_gate, preferred_element_type=jnp.float32)
            part_grad = part_grad + jnp.dot(grad_up, w_up, preferred_element_type=jnp.float32)
            return part_grad.astype(jnp.bfloat16)

        part_grad = lax.cond(
            is_live,
            backward,
            lambda arrived_rows: jnp.zeros((n_rows, feat_dim), jnp.bfloat16),
            arrived,
        )
        back_part, back_left = (
            lax.all_to_all(
                part_grad.reshape(n_expert, CAP, feat_dim),
                "expert",
                split_axis=0,
                concat_axis=0,
                tiled=True,
            ),
            lax.all_to_all(
                left_now.reshape(n_expert, CAP, sketch_dim),
                "expert",
                split_axis=0,
                concat_axis=0,
                tiled=True,
            ),
        )
        summed = back_part.reshape(groups, hsplit, CAP, feat_dim).astype(jnp.float32).sum(axis=1)
        summed = summed.reshape(n_slots, feat_dim)
        left_slots = (
            back_left.reshape(groups, hsplit, CAP, sketch_dim).astype(jnp.float32).sum(axis=1)
        )
        left_slots = left_slots.reshape(n_slots, sketch_dim)
        moe_grad = jnp.einsum(
            "st,sd->td", chosen.astype(jnp.float32), summed, precision=lax.Precision.HIGHEST
        )
        new_grad = (out_grad.astype(jnp.float32) + moe_grad).astype(jnp.bfloat16)
        right_tok = jnp.dot(out_grad, proj_right, preferred_element_type=jnp.float32)
        select_now = lax.dynamic_index_in_dim(select, current, 0, keepdims=False)
        weight_now = lax.dynamic_index_in_dim(weights_flat, current, 0, keepdims=False)
        ids_now = lax.dynamic_index_in_dim(ids_flat, current, 0, keepdims=False)
        example_now = lax.dynamic_index_in_dim(example_ids, current, 0, keepdims=False)
        left_pairs = jnp.einsum(
            "sp,sr->pr", select_now, left_slots, precision=lax.Precision.HIGHEST
        )
        right_pairs = jnp.repeat(right_tok, top_k, axis=0) * weight_now[:, None]
        example_pairs = jnp.repeat(example_now, top_k, axis=0)
        query = (current * EXM + example_pairs) * groups + ids_now
        query_hot = (query[:, None] == jnp.arange(q_total, dtype=jnp.int32)[None, :]).astype(
            jnp.float32
        )
        outer_rows = (query_hot[:, :, None] * left_pairs[:, None, :]).reshape(
            n_pairs, q_total * sketch_dim
        )
        contrib = jnp.einsum("pa,pb->ab", outer_rows, right_pairs, precision=lax.Precision.HIGHEST)
        sketch = sketch + jnp.where(
            is_live, contrib.reshape(q_total, sketch_dim * sketch_dim), jnp.float32(0.0)
        )
        updated = lax.dynamic_update_index_in_dim(grads_out, new_grad, current, 0)
        grads_out = jnp.where(is_live, updated, grads_out)
        return (new_grad, grads_out, sketch)

    start_state = (
        jnp.zeros((tok_dev, feat_dim), jnp.bfloat16),
        jnp.zeros((n_micro, tok_dev, feat_dim), jnp.bfloat16),
        jnp.zeros((q_total, sketch_dim * sketch_dim), jnp.float32),
    )
    final_state = lax.fori_loop(0, n_steps, one_step, start_state)
    sketch_share = lax.psum_scatter(final_state[2], "expert", scatter_dimension=0, tiled=True)
    return (final_state[1][None], sketch_share[None])


def solution(mesh):
    placed = (
        P("section", None, "expert", None),
        P(None, "expert", None),
        P("section", None, "expert", None),
        P("section", None, "expert", None),
        P(None, "expert"),
        P("section", "expert", None),
        P("section", "expert", None),
        P("section", "expert", None),
        P("section", "expert", None),
        P("section", None, None),
    )
    return jax.shard_map(
        on_device,
        mesh=mesh,
        in_specs=placed,
        out_specs=(P("section", None, "expert", None), P("section", "expert", None)),
        check_vma=False,
    )
```

profile of v0, /device:TPU:0, one launch (start us, length us, event | category | flops | bytes accessed | tf_op | source)
XLA Modules:
  0.0 330.3 jit_solution(18071408338495752994)
XLA Ops:
  13.6 7.3 %all-to-all-start.3 = ((bf16[2,8,3]{2,0,1:T(2,128)(2,1)}), bf16[2,8,3]{2,0,1:T(2,128)(2,1)S(1)}, u32[]{:S(2)}, u32[]{:S(2)}) async-start(bf16[2,8,3]{2,0,1:T(2,128)(2,1)} %copy.51), calls=%async_computation.3 | async-start | bytes 8192 | tf_op jit(solution)/shard_map/all_to_all | solution.py:67
  20.8 1.1 convolution_convert_fusion.1
  22.8 4.4 %all-to-all-done.3 = bf16[2,8,3]{2,0,1:T(2,128)(2,1)S(1)} async-done(((bf16[2,8,3]{2,0,1:T(2,128)(2,1)}), bf16[2,8,3]{2,0,1:T(2,128)(2,1)S(1)}, u32[]{:S(2)}, u32[]{:S(2)}) %all-to-all-start.3) | async-done | bytes 128 | tf_op jit(solution)/shard_map/all_to_all | solution.py:67
  27.2 3.4 %all-to-all-start.4 = ((bf16[2,8,3,2048]{3,0,2,1:T(2,128)(2,1)}), bf16[2,8,3,2048]{3,0,2,1:T(2,128)(2,1)S(1)}, u32[]{:S(2)}, u32[]{:S(2)}) async-start(bf16[2,8,3,2048]{3,0,2,1:T(2,128)(2,1)} %bitcast.8), calls=%async_computation.4 | async-start | bytes 393216 | tf_op jit(solution)/shard_map/all_to_all | solution.py:66
  31.3 1.2 copy.57
  34.1 4.3 %all-to-all-done.4 = bf16[2,8,3,2048]{3,0,2,1:T(2,128)(2,1)S(1)} async-done(((bf16[2,8,3,2048]{3,0,2,1:T(2,128)(2,1)}), bf16[2,8,3,2048]{3,0,2,1:T(2,128)(2,1)S(1)}, u32[]{:S(2)}, u32[]{:S(2)}) %all-to-all-start.4) | async-done | bytes 196640 | tf_op jit(solution)/shard_map/all_to_all | solution.py:66
  38.4 4.9 %fusion.38 = f32[2,24,1536]{2,1,0:T(8,128)S(1)} fusion(bf16[1,1536,2048]{2,1,0:T(8,128)(2,1)} %param.19, bf16[2,24,2048]{2,0,1:T(2,128)(2,1)S(1)} %bitcast.139), kind=kOutput, calls=%fused_computation.54 | convolution fusion | flops 301989888 | bytes 6782976 | tf_op jit(solution)/shard_map/mrd,hd->mrh/dot_general | solution.py:74
  43.3 2.0 fusion.40
  46.2 216.8 %while.20 = (s32[]{:T(128)}, bf16[8,2048]{1,0:T(8,128)(2,1)S(1)}, bf16[2,8,2048]{2,1,0:T(8,128)(2,1)}, f32[64,4096]{1,0:T(8,128)}, pred[]{:T(512)}, /*index=5*/s...) while((s32[]{:T(128)}, bf16[8,2048]{1,0:T(8,128)(2,1)S(1)}, ...), condition=%wide.region_6.7_spmd.clone, body=%wide.region_3.6_spmd.clone.sunk | while | flops 509008896 | bytes 86463120 | solution.py:180
  46.9 3.3 %all-to-all-start.2 = ((bf16[8,3,64]{2,1,0:T(4,128)(2,1)}), bf16[8,3,64]{2,1,0:T(4,128)(2,1)S(1)}, u32[]{:S(2)}, u32[]{:S(2)}) async-start(bf16[8,3,64]{2,1,0:T(4,128)(2,1)} %reshape.243), calls=%async_computation.2 | async-start | bytes 16384 | tf_op jit(solution)/shard_map/while/body/eval_jaxpr/all_to_all | solution.py:132
  50.3 1.3 collective-permute-start
  53.9 2.8 all-to-all-done.2
  59.9 3.4 %all-to-all-start = ((bf16[8,3,2048]{2,1,0:T(4,128)(2,1)}), bf16[8,3,2048]{2,1,0:T(4,128)(2,1)S(1)}, u32[]{:S(2)}, u32[]{:S(2)}) async-start(bf16[8,3,2048]{2,1,0:T(4,128)(2,1)} %reshape.240), calls=%async_computation | async-start | bytes 262144 | tf_op jit(solution)/shard_map/while/body/eval_jaxpr/all_to_all | solution.py:97
  63.3 1.0 convolution_select_fusion.2
  65.6 5.6 %all-to-all-done = bf16[8,3,2048]{2,1,0:T(4,128)(2,1)S(1)} async-done(((bf16[8,3,2048]{2,1,0:T(4,128)(2,1)}), bf16[8,3,2048]{2,1,0:T(4,128)(2,1)S(1)}, u32[]{:S(2)}, u32[]{:S(2)}) %all-to-all-start) | async-done | bytes 98336 | tf_op jit(solution)/shard_map/while/body/eval_jaxpr/all_to_all | solution.py:97
  72.0 3.4 %all-to-all-start.1 = ((bf16[8,3,2048]{2,1,0:T(4,128)(2,1)}), bf16[8,3,2048]{2,1,0:T(4,128)(2,1)S(1)}, u32[]{:S(2)}, u32[]{:S(2)}) async-start(bf16[8,3,2048]{2,1,0:T(4,128)(2,1)} %reshape.241), calls=%async_computation.1 | async-start | bytes 262144 | tf_op jit(solution)/shard_map/while/body/eval_jaxpr/all_to_all | solution.py:125
  75.4 1.1 select_add_fusion.2
  76.5 6.2 %all-to-all-done.1 = bf16[8,3,2048]{2,1,0:T(4,128)(2,1)S(1)} async-done(((bf16[8,3,2048]{2,1,0:T(4,128)(2,1)}), bf16[8,3,2048]{2,1,0:T(4,128)(2,1)S(1)}, u32[]{:S(2)}, u32[]{:S(2)}) %all-to-all-start.1) | async-done | bytes 98336 | tf_op jit(solution)/shard_map/while/body/eval_jaxpr/all_to_all | solution.py:125
  84.3 3.3 %all-to-all-start.2 = ((bf16[8,3,64]{2,1,0:T(4,128)(2,1)}), bf16[8,3,64]{2,1,0:T(4,128)(2,1)S(1)}, u32[]{:S(2)}, u32[]{:S(2)}) async-start(bf16[8,3,64]{2,1,0:T(4,128)(2,1)} %reshape.243), calls=%async_computation.2 | async-start | bytes 16384 | tf_op jit(solution)/shard_map/while/body/eval_jaxpr/all_to_all | solution.py:132
  87.6 1.3 collective-permute-start
  91.3 2.8 all-to-all-done.2
  97.2 3.4 %all-to-all-start = ((bf16[8,3,2048]{2,1,0:T(4,128)(2,1)}), bf16[8,3,2048]{2,1,0:T(4,128)(2,1)S(1)}, u32[]{:S(2)}, u32[]{:S(2)}) async-start(bf16[8,3,2048]{2,1,0:T(4,128)(2,1)} %reshape.240), calls=%async_computation | async-start | bytes 262144 | tf_op jit(solution)/shard_map/while/body/eval_jaxpr/all_to_all | solution.py:97
  100.7 1.0 convolution_select_fusion.2
  103.0 5.6 %all-to-all-done = bf16[8,3,2048]{2,1,0:T(4,128)(2,1)S(1)} async-done(((bf16[8,3,2048]{2,1,0:T(4,128)(2,1)}), bf16[8,3,2048]{2,1,0:T(4,128)(2,1)S(1)}, u32[]{:S(2)}, u32[]{:S(2)}) %all-to-all-start) | async-done | bytes 98336 | tf_op jit(solution)/shard_map/while/body/eval_jaxpr/all_to_all | solution.py:97
  109.4 3.4 %all-to-all-start.1 = ((bf16[8,3,2048]{2,1,0:T(4,128)(2,1)}), bf16[8,3,2048]{2,1,0:T(4,128)(2,1)S(1)}, u32[]{:S(2)}, u32[]{:S(2)}) async-start(bf16[8,3,2048]{2,1,0:T(4,128)(2,1)} %reshape.241), calls=%async_computation.1 | async-start | bytes 262144 | tf_op jit(solution)/shard_map/while/body/eval_jaxpr/all_to_all | solution.py:125
  112.8 2.3 select_add_fusion.2
  115.1 5.0 %all-to-all-done.1 = bf16[8,3,2048]{2,1,0:T(4,128)(2,1)S(1)} async-done(((bf16[8,3,2048]{2,1,0:T(4,128)(2,1)}), bf16[8,3,2048]{2,1,0:T(4,128)(2,1)S(1)}, u32[]{:S(2)}, u32[]{:S(2)}) %all-to-all-start.1) | async-done | bytes 98336 | tf_op jit(solution)/shard_map/while/body/eval_jaxpr/all_to_all | solution.py:125
  121.6 3.3 %all-to-all-start.2 = ((bf16[8,3,64]{2,1,0:T(4,128)(2,1)}), bf16[8,3,64]{2,1,0:T(4,128)(2,1)S(1)}, u32[]{:S(2)}, u32[]{:S(2)}) async-start(bf16[8,3,64]{2,1,0:T(4,128)(2,1)} %reshape.243), calls=%async_computation.2 | async-start | bytes 16384 | tf_op jit(solution)/shard_map/while/body/eval_jaxpr/all_to_all | solution.py:132
  125.0 1.3 collective-permute-start
  128.6 2.8 all-to-all-done.2
  134.5 3.4 %all-to-all-start = ((bf16[8,3,2048]{2,1,0:T(4,128)(2,1)}), bf16[8,3,2048]{2,1,0:T(4,128)(2,1)S(1)}, u32[]{:S(2)}, u32[]{:S(2)}) async-start(bf16[8,3,2048]{2,1,0:T(4,128)(2,1)} %reshape.240), calls=%async_computation | async-start | bytes 262144 | tf_op jit(solution)/shard_map/while/body/eval_jaxpr/all_to_all | solution.py:97
  138.0 1.0 convolution_select_fusion.2
  140.3 4.9 %all-to-all-done = bf16[8,3,2048]{2,1,0:T(4,128)(2,1)S(1)} async-done(((bf16[8,3,2048]{2,1,0:T(4,128)(2,1)}), bf16[8,3,2048]{2,1,0:T(4,128)(2,1)S(1)}, u32[]{:S(2)}, u32[]{:S(2)}) %all-to-all-start) | async-done | bytes 98336 | tf_op jit(solution)/shard_map/while/body/eval_jaxpr/all_to_all | solution.py:97
  146.0 3.4 %all-to-all-start.1 = ((bf16[8,3,2048]{2,1,0:T(4,128)(2,1)}), bf16[8,3,2048]{2,1,0:T(4,128)(2,1)S(1)}, u32[]{:S(2)}, u32[]{:S(2)}) async-start(bf16[8,3,2048]{2,1,0:T(4,128)(2,1)} %reshape.241), calls=%async_computation.1 | async-start | bytes 262144 | tf_op jit(solution)/shard_map/while/body/eval_jaxpr/all_to_all | solution.py:125
  149.3 2.3 select_add_fusion.2
  151.7 5.0 %all-to-all-done.1 = bf16[8,3,2048]{2,1,0:T(4,128)(2,1)S(1)} async-done(((bf16[8,3,2048]{2,1,0:T(4,128)(2,1)}), bf16[8,3,2048]{2,1,0:T(4,128)(2,1)S(1)}, u32[]{:S(2)}, u32[]{:S(2)}) %all-to-all-start.1) | async-done | bytes 98336 | tf_op jit(solution)/shard_map/while/body/eval_jaxpr/all_to_all | solution.py:125
  158.2 3.3 %all-to-all-start.2 = ((bf16[8,3,64]{2,1,0:T(4,128)(2,1)}), bf16[8,3,64]{2,1,0:T(4,128)(2,1)S(1)}, u32[]{:S(2)}, u32[]{:S(2)}) async-start(bf16[8,3,64]{2,1,0:T(4,128)(2,1)} %reshape.243), calls=%async_computation.2 | async-start | bytes 16384 | tf_op jit(solution)/shard_map/while/body/eval_jaxpr/all_to_all | solution.py:132
  161.5 1.3 collective-permute-start
  165.2 2.8 all-to-all-done.2
  169.2 12.5 %collective-permute-done = bf16[8,2048]{1,0:T(8,128)(2,1)S(1)} collective-permute-done((bf16[8,2048]{1,0:T(8,128)(2,1)S(1)}, bf16[8,2048]{1,0:T(8,128)(2,1)S(1)}, u32[]{:S(2)}, u32[]{:S(2)}) %collective-permute-start) | collective-permute-done | bytes 32800 | tf_op jit(solution)/shard_map/while/body/eval_jaxpr/ppermute | solution.py:14
  183.6 5.6 %all-to-all-start = ((bf16[8,3,2048]{2,1,0:T(4,128)(2,1)}), bf16[8,3,2048]{2,1,0:T(4,128)(2,1)S(1)}, u32[]{:S(2)}, u32[]{:S(2)}) async-start(bf16[8,3,2048]{2,1,0:T(4,128)(2,1)} %reshape.240), calls=%async_computation | async-start | bytes 262144 | tf_op jit(solution)/shard_map/while/body/eval_jaxpr/all_to_all | solution.py:97
  189.4 1.0 convolution_select_fusion.2
  191.7 5.0 %all-to-all-done = bf16[8,3,2048]{2,1,0:T(4,128)(2,1)S(1)} async-done(((bf16[8,3,2048]{2,1,0:T(4,128)(2,1)}), bf16[8,3,2048]{2,1,0:T(4,128)(2,1)S(1)}, u32[]{:S(2)}, u32[]{:S(2)}) %all-to-all-start) | async-done | bytes 98336 | tf_op jit(solution)/shard_map/while/body/eval_jaxpr/all_to_all | solution.py:97
  196.6 8.5 %conditional.3 = (bf16[24,2048]{1,0:T(8,128)(2,1)S(1)}) conditional(s32[]{:T(128)} %convert_element_type.150, () %tuple.61, (bf16[8,3,2048]{2,1,0:T(4,128)(2,1)S(1)}, bf16[1536,2048]{1,0:T(8,128)(2,1)}, f32[2,24]{1,0:T(2,128)S(1)}, s32[]{:T(128)}, f32[2,24,1536]{2,1,0:T(8,128)}, /*index=5*/f32[2,24,1536]{2,1,0:T(8,128)}, ...), branch_computations={%region_4.4_spmd, %region_5.5_spmd} | conditional | flops 453709824 | bytes 72057736 | solution.py:118
  196.8 4.7 %convolution_multiply_fusion = f32[24,1536]{1,0:T(8,128)S(1)} fusion(bf16[24,2048]{1,0:T(8,128)(2,1)S(1)} %reshape.207, bf16[1536,2048]{1,0:T(8,128)(2,1)} %get-tuple-element.496, f32[24]{0:T(128)S(1)} %fusion.17), kind=kOutput, calls=%fused_computation | convolution fusion | flops 151031808 | bytes 6537312 | tf_op jit(solution)/shard_map/while/body/eval_jaxpr/cond/branch_1_fun/rd,hd->rh/dot_general | solution.py:106
  201.5 2.7 fusion.11
  204.2 0.9 fusion
  205.9 3.4 %all-to-all-start.1 = ((bf16[8,3,2048]{2,1,0:T(4,128)(2,1)}), bf16[8,3,2048]{2,1,0:T(4,128)(2,1)S(1)}, u32[]{:S(2)}, u32[]{:S(2)}) async-start(bf16[8,3,2048]{2,1,0:T(4,128)(2,1)} %reshape.241), calls=%async_computation.1 | async-start | bytes 262144 | tf_op jit(solution)/shard_map/while/body/eval_jaxpr/all_to_all | solution.py:125
  209.3 2.3 select_add_fusion.2
  211.6 5.0 %all-to-all-done.1 = bf16[8,3,2048]{2,1,0:T(4,128)(2,1)S(1)} async-done(((bf16[8,3,2048]{2,1,0:T(4,128)(2,1)}), bf16[8,3,2048]{2,1,0:T(4,128)(2,1)S(1)}, u32[]{:S(2)}, u32[]{:S(2)}) %all-to-all-start.1) | async-done | bytes 98336 | tf_op jit(solution)/shard_map/while/body/eval_jaxpr/all_to_all | solution.py:125
  218.2 3.3 %all-to-all-start.2 = ((bf16[8,3,64]{2,1,0:T(4,128)(2,1)}), bf16[8,3,64]{2,1,0:T(4,128)(2,1)S(1)}, u32[]{:S(2)}, u32[]{:S(2)}) async-start(bf16[8,3,64]{2,1,0:T(4,128)(2,1)} %reshape.243), calls=%async_computation.2 | async-start | bytes 16384 | tf_op jit(solution)/shard_map/while/body/eval_jaxpr/all_to_all | solution.py:132
  221.6 1.3 collective-permute-start
  225.2 2.8 all-to-all-done.2
  231.2 3.7 %all-to-all-start = ((bf16[8,3,2048]{2,1,0:T(4,128)(2,1)}), bf16[8,3,2048]{2,1,0:T(4,128)(2,1)S(1)}, u32[]{:S(2)}, u32[]{:S(2)}) async-start(bf16[8,3,2048]{2,1,0:T(4,128)(2,1)} %reshape.240), calls=%async_computation | async-start | bytes 262144 | tf_op jit(solution)/shard_map/while/body/eval_jaxpr/all_to_all | solution.py:97
  234.9 1.0 convolution_select_fusion.2
  237.2 5.0 %all-to-all-done = bf16[8,3,2048]{2,1,0:T(4,128)(2,1)S(1)} async-done(((bf16[8,3,2048]{2,1,0:T(4,128)(2,1)}), bf16[8,3,2048]{2,1,0:T(4,128)(2,1)S(1)}, u32[]{:S(2)}, u32[]{:S(2)}) %all-to-all-start) | async-done | bytes 98336 | tf_op jit(solution)/shard_map/while/body/eval_jaxpr/all_to_all | solution.py:97
  242.2 8.5 %conditional.3 = (bf16[24,2048]{1,0:T(8,128)(2,1)S(1)}) conditional(s32[]{:T(128)} %convert_element_type.150, () %tuple.61, (bf16[8,3,2048]{2,1,0:T(4,128)(2,1)S(1)}, bf16[1536,2048]{1,0:T(8,128)(2,1)}, f32[2,24]{1,0:T(2,128)S(1)}, s32[]{:T(128)}, f32[2,24,1536]{2,1,0:T(8,128)}, /*index=5*/f32[2,24,1536]{2,1,0:T(8,128)}, ...), branch_computations={%region_4.4_spmd, %region_5.5_spmd} | conditional | flops 453709824 | bytes 72057736 | solution.py:118
  242.3 4.7 %convolution_multiply_fusion = f32[24,1536]{1,0:T(8,128)S(1)} fusion(bf16[24,2048]{1,0:T(8,128)(2,1)S(1)} %reshape.207, bf16[1536,2048]{1,0:T(8,128)(2,1)} %get-tuple-element.496, f32[24]{0:T(128)S(1)} %fusion.17), kind=kOutput, calls=%fused_computation | convolution fusion | flops 151031808 | bytes 6537312 | tf_op jit(solution)/shard_map/while/body/eval_jaxpr/cond/branch_1_fun/rd,hd->rh/dot_general | solution.py:106
  247.0 2.7 fusion.11
  249.8 0.9 fusion
  251.5 3.4 %all-to-all-start.1 = ((bf16[8,3,2048]{2,1,0:T(4,128)(2,1)}), bf16[8,3,2048]{2,1,0:T(4,128)(2,1)S(1)}, u32[]{:S(2)}, u32[]{:S(2)}) async-start(bf16[8,3,2048]{2,1,0:T(4,128)(2,1)} %reshape.241), calls=%async_computation.1 | async-start | bytes 262144 | tf_op jit(solution)/shard_map/while/body/eval_jaxpr/all_to_all | solution.py:125
  254.9 2.3 select_add_fusion.2
  257.2 5.0 %all-to-all-done.1 = bf16[8,3,2048]{2,1,0:T(4,128)(2,1)S(1)} async-done(((bf16[8,3,2048]{2,1,0:T(4,128)(2,1)}), bf16[8,3,2048]{2,1,0:T(4,128)(2,1)S(1)}, u32[]{:S(2)}, u32[]{:S(2)}) %all-to-all-start.1) | async-done | bytes 98336 | tf_op jit(solution)/shard_map/while/body/eval_jaxpr/all_to_all | solution.py:125
  263.0 60.4 %reduce-scatter.2.cloned.1.call-done = f32[8,4096]{1,0:T(8,128)} async-done(((f32[64,4096]{1,0:T(8,128)}), f32[8,4096]{1,0:T(8,128)}) %reduce-scatter.2.cloned.1.call-update) | async-done | bytes 131088 | tf_op jit(solution)/shard_map/reduce_scatter | solution.py:181
  (236 shorter events, 56.1 us)
Async XLA Ops:
  7.2 38.2 %copy-start = (bf16[1,1536,64]{1,2,0:T(8,128)(2,1)S(1)}, bf16[1,1536,64]{1,2,0:T(8,128)(2,1)}, u32[]{:S(2)}) copy-start(bf16[1,1536,64]{1,2,0:T(8,128)(2,1)} %param.22) | copy-start | bytes 589828
  13.6 13.6 %all-to-all-start.3 = ((bf16[2,8,3]{2,0,1:T(2,128)(2,1)}), bf16[2,8,3]{2,0,1:T(2,128)(2,1)S(1)}, u32[]{:S(2)}, u32[]{:S(2)}) async-start(bf16[2,8,3]{2,0,1:T(2,128)(2,1)} %copy.51), calls=%async_computation.3 | async-start | bytes 8192 | tf_op jit(solution)/shard_map/all_to_all | solution.py:67
  21.9 21.4 %slice-start = ((s8[6291456]{0:T(1024)(128)(4,1)}), s8[2097152]{0:T(1024)(128)(4,1)S(1)}, s32[]{:S(2)}) async-start(s8[6291456]{0:T(1024)(128)(4,1)} %bitcast.134), calls=%async_computation.7 | async-start | bytes 4194304
  27.2 11.1 %all-to-all-start.4 = ((bf16[2,8,3,2048]{3,0,2,1:T(2,128)(2,1)}), bf16[2,8,3,2048]{3,0,2,1:T(2,128)(2,1)S(1)}, u32[]{:S(2)}, u32[]{:S(2)}) async-start(bf16[2,8,3,2048]{3,0,2,1:T(2,128)(2,1)} %bitcast.8), calls=%async_computation.4 | async-start | bytes 393216 | tf_op jit(solution)/shard_map/all_to_all | solution.py:66
  30.6 292.8 %reduce-scatter.2.cloned.1.call-start = ((), (), s32[]{:S(2)}) async-start(), calls=%async_computation.6 | async-start | bytes 1179648 | tf_op jit(solution)/shard_map/reduce_scatter | solution.py:181
  38.4 5.0 %slice-start.1 = ((s8[6291456]{0:T(1024)(128)(4,1)}), s8[4194304]{0:T(1024)(128)(4,1)S(1)}, s32[]{:S(2)}) async-start(s8[6291456]{0:T(1024)(128)(4,1)} %bitcast.134), calls=%async_computation.8 | async-start | bytes 8388608
  43.3 2.9 copy-start.5
  45.3 0.9 copy-start.7
  46.2 17.1 %copy-start.3 = (bf16[2048,64]{1,0:T(8,128)(2,1)}, bf16[2048,64]{1,0:T(8,128)(2,1)S(1)}, u32[]{:S(2)}) copy-start(bf16[2048,64]{1,0:T(8,128)(2,1)S(1)} %get-tuple-element.826) | copy-start | bytes 786436 | tf_op jit(solution)/shard_map/while
  46.9 9.8 %all-to-all-start.2 = ((bf16[8,3,64]{2,1,0:T(4,128)(2,1)}), bf16[8,3,64]{2,1,0:T(4,128)(2,1)S(1)}, u32[]{:S(2)}, u32[]{:S(2)}) async-start(bf16[8,3,64]{2,1,0:T(4,128)(2,1)} %reshape.243), calls=%async_computation.2 | async-start | bytes 16384 | tf_op jit(solution)/shard_map/while/body/eval_jaxpr/all_to_all | solution.py:132
  50.3 21.0 %copy-start.10 = (f32[2,24]{1,0:T(2,128)S(1)}, f32[2,24]{1,0:T(2,128)}, u32[]{:S(2)}) copy-start(f32[2,24]{1,0:T(2,128)} %get-tuple-element.817) | copy-start | bytes 580 | tf_op jit(solution)/shard_map/while
  50.3 7.7 %collective-permute-start = (bf16[8,2048]{1,0:T(8,128)(2,1)S(1)}, bf16[8,2048]{1,0:T(8,128)(2,1)S(1)}, u32[]{:S(2)}, u32[]{:S(2)}) collective-permute-start(bf16[8,2048]{1,0:T(8,128)(2,1)S(1)} %broadcast_select_fusion.2), channel_id=1, source_target_pairs={{8,0},{16,8},{24,16},{9,1},{17,9},{25,17},{10,2},{18,10},{26,18},{... | collective-permute-start | bytes 98312 | tf_op jit(solution)/shard_map/while/body/eval_jaxpr/ppermute | solution.py:14
  59.9 11.4 %all-to-all-start = ((bf16[8,3,2048]{2,1,0:T(4,128)(2,1)}), bf16[8,3,2048]{2,1,0:T(4,128)(2,1)S(1)}, u32[]{:S(2)}, u32[]{:S(2)}) async-start(bf16[8,3,2048]{2,1,0:T(4,128)(2,1)} %reshape.240), calls=%async_computation | async-start | bytes 262144 | tf_op jit(solution)/shard_map/while/body/eval_jaxpr/all_to_all | solution.py:97
  71.3 11.5 %copy-start.8 = (bf16[2,8,2048]{2,1,0:T(8,128)(2,1)S(1)}, bf16[2,8,2048]{2,1,0:T(8,128)(2,1)}, u32[]{:S(2)}) copy-start(bf16[2,8,2048]{2,1,0:T(8,128)(2,1)} %get-tuple-element.786) | copy-start | bytes 196612 | tf_op jit(solution)/shard_map/while
  71.3 12.3 %copy-start.4 = (bf16[2048,64]{1,0:T(8,128)(2,1)S(1)}, bf16[2048,64]{1,0:T(8,128)(2,1)}, u32[]{:S(2)}) copy-start(bf16[2048,64]{1,0:T(8,128)(2,1)} %copy-done.3) | copy-start | bytes 786436 | tf_op jit(solution)/shard_map/while
  72.0 10.7 %all-to-all-start.1 = ((bf16[8,3,2048]{2,1,0:T(4,128)(2,1)}), bf16[8,3,2048]{2,1,0:T(4,128)(2,1)S(1)}, u32[]{:S(2)}, u32[]{:S(2)}) async-start(bf16[8,3,2048]{2,1,0:T(4,128)(2,1)} %reshape.241), calls=%async_computation.1 | async-start | bytes 262144 | tf_op jit(solution)/shard_map/while/body/eval_jaxpr/all_to_all | solution.py:125
  83.0 0.6 copy-start.9
  83.6 17.1 %copy-start.3 = (bf16[2048,64]{1,0:T(8,128)(2,1)}, bf16[2048,64]{1,0:T(8,128)(2,1)S(1)}, u32[]{:S(2)}) copy-start(bf16[2048,64]{1,0:T(8,128)(2,1)S(1)} %get-tuple-element.826) | copy-start | bytes 786436 | tf_op jit(solution)/shard_map/while
  84.3 9.8 %all-to-all-start.2 = ((bf16[8,3,64]{2,1,0:T(4,128)(2,1)}), bf16[8,3,64]{2,1,0:T(4,128)(2,1)S(1)}, u32[]{:S(2)}, u32[]{:S(2)}) async-start(bf16[8,3,64]{2,1,0:T(4,128)(2,1)} %reshape.243), calls=%async_computation.2 | async-start | bytes 16384 | tf_op jit(solution)/shard_map/while/body/eval_jaxpr/all_to_all | solution.py:132
  87.6 21.0 %copy-start.10 = (f32[2,24]{1,0:T(2,128)S(1)}, f32[2,24]{1,0:T(2,128)}, u32[]{:S(2)}) copy-start(f32[2,24]{1,0:T(2,128)} %get-tuple-element.817) | copy-start | bytes 580 | tf_op jit(solution)/shard_map/while
  87.6 7.7 %collective-permute-start = (bf16[8,2048]{1,0:T(8,128)(2,1)S(1)}, bf16[8,2048]{1,0:T(8,128)(2,1)S(1)}, u32[]{:S(2)}, u32[]{:S(2)}) collective-permute-start(bf16[8,2048]{1,0:T(8,128)(2,1)S(1)} %broadcast_select_fusion.2), channel_id=1, source_target_pairs={{8,0},{16,8},{24,16},{9,1},{17,9},{25,17},{10,2},{18,10},{26,18},{... | collective-permute-start | bytes 98312 | tf_op jit(solution)/shard_map/while/body/eval_jaxpr/ppermute | solution.py:14
  97.2 11.4 %all-to-all-start = ((bf16[8,3,2048]{2,1,0:T(4,128)(2,1)}), bf16[8,3,2048]{2,1,0:T(4,128)(2,1)S(1)}, u32[]{:S(2)}, u32[]{:S(2)}) async-start(bf16[8,3,2048]{2,1,0:T(4,128)(2,1)} %reshape.240), calls=%async_computation | async-start | bytes 262144 | tf_op jit(solution)/shard_map/while/body/eval_jaxpr/all_to_all | solution.py:97
  108.6 11.5 %copy-start.8 = (bf16[2,8,2048]{2,1,0:T(8,128)(2,1)S(1)}, bf16[2,8,2048]{2,1,0:T(8,128)(2,1)}, u32[]{:S(2)}) copy-start(bf16[2,8,2048]{2,1,0:T(8,128)(2,1)} %get-tuple-element.786) | copy-start | bytes 196612 | tf_op jit(solution)/shard_map/while
  108.6 12.3 %copy-start.4 = (bf16[2048,64]{1,0:T(8,128)(2,1)S(1)}, bf16[2048,64]{1,0:T(8,128)(2,1)}, u32[]{:S(2)}) copy-start(bf16[2048,64]{1,0:T(8,128)(2,1)} %copy-done.3) | copy-start | bytes 786436 | tf_op jit(solution)/shard_map/while
  109.4 10.7 %all-to-all-start.1 = ((bf16[8,3,2048]{2,1,0:T(4,128)(2,1)}), bf16[8,3,2048]{2,1,0:T(4,128)(2,1)S(1)}, u32[]{:S(2)}, u32[]{:S(2)}) async-start(bf16[8,3,2048]{2,1,0:T(4,128)(2,1)} %reshape.241), calls=%async_computation.1 | async-start | bytes 262144 | tf_op jit(solution)/shard_map/while/body/eval_jaxpr/all_to_all | solution.py:125
  120.3 0.6 copy-start.9
  120.9 17.1 %copy-start.3 = (bf16[2048,64]{1,0:T(8,128)(2,1)}, bf16[2048,64]{1,0:T(8,128)(2,1)S(1)}, u32[]{:S(2)}) copy-start(bf16[2048,64]{1,0:T(8,128)(2,1)S(1)} %get-tuple-element.826) | copy-start | bytes 786436 | tf_op jit(solution)/shard_map/while
  121.6 9.8 %all-to-all-start.2 = ((bf16[8,3,64]{2,1,0:T(4,128)(2,1)}), bf16[8,3,64]{2,1,0:T(4,128)(2,1)S(1)}, u32[]{:S(2)}, u32[]{:S(2)}) async-start(bf16[8,3,64]{2,1,0:T(4,128)(2,1)} %reshape.243), calls=%async_computation.2 | async-start | bytes 16384 | tf_op jit(solution)/shard_map/while/body/eval_jaxpr/all_to_all | solution.py:132
  125.0 20.2 %copy-start.10 = (f32[2,24]{1,0:T(2,128)S(1)}, f32[2,24]{1,0:T(2,128)}, u32[]{:S(2)}) copy-start(f32[2,24]{1,0:T(2,128)} %get-tuple-element.817) | copy-start | bytes 580 | tf_op jit(solution)/shard_map/while
  125.0 7.7 %collective-permute-start = (bf16[8,2048]{1,0:T(8,128)(2,1)S(1)}, bf16[8,2048]{1,0:T(8,128)(2,1)S(1)}, u32[]{:S(2)}, u32[]{:S(2)}) collective-permute-start(bf16[8,2048]{1,0:T(8,128)(2,1)S(1)} %broadcast_select_fusion.2), channel_id=1, source_target_pairs={{8,0},{16,8},{24,16},{9,1},{17,9},{25,17},{10,2},{18,10},{26,18},{... | collective-permute-start | bytes 98312 | tf_op jit(solution)/shard_map/while/body/eval_jaxpr/ppermute | solution.py:14
  134.5 10.7 %all-to-all-start = ((bf16[8,3,2048]{2,1,0:T(4,128)(2,1)}), bf16[8,3,2048]{2,1,0:T(4,128)(2,1)S(1)}, u32[]{:S(2)}, u32[]{:S(2)}) async-start(bf16[8,3,2048]{2,1,0:T(4,128)(2,1)} %reshape.240), calls=%async_computation | async-start | bytes 262144 | tf_op jit(solution)/shard_map/while/body/eval_jaxpr/all_to_all | solution.py:97
  145.2 11.5 %copy-start.8 = (bf16[2,8,2048]{2,1,0:T(8,128)(2,1)S(1)}, bf16[2,8,2048]{2,1,0:T(8,128)(2,1)}, u32[]{:S(2)}) copy-start(bf16[2,8,2048]{2,1,0:T(8,128)(2,1)} %get-tuple-element.786) | copy-start | bytes 196612 | tf_op jit(solution)/shard_map/while
  145.2 12.3 %copy-start.4 = (bf16[2048,64]{1,0:T(8,128)(2,1)S(1)}, bf16[2048,64]{1,0:T(8,128)(2,1)}, u32[]{:S(2)}) copy-start(bf16[2048,64]{1,0:T(8,128)(2,1)} %copy-done.3) | copy-start | bytes 786436 | tf_op jit(solution)/shard_map/while
  146.0 10.7 %all-to-all-start.1 = ((bf16[8,3,2048]{2,1,0:T(4,128)(2,1)}), bf16[8,3,2048]{2,1,0:T(4,128)(2,1)S(1)}, u32[]{:S(2)}, u32[]{:S(2)}) async-start(bf16[8,3,2048]{2,1,0:T(4,128)(2,1)} %reshape.241), calls=%async_computation.1 | async-start | bytes 262144 | tf_op jit(solution)/shard_map/while/body/eval_jaxpr/all_to_all | solution.py:125
  156.9 0.6 copy-start.9
  157.5 31.9 %copy-start.3 = (bf16[2048,64]{1,0:T(8,128)(2,1)}, bf16[2048,64]{1,0:T(8,128)(2,1)S(1)}, u32[]{:S(2)}) copy-start(bf16[2048,64]{1,0:T(8,128)(2,1)S(1)} %get-tuple-element.826) | copy-start | bytes 786436 | tf_op jit(solution)/shard_map/while
  158.2 9.8 %all-to-all-start.2 = ((bf16[8,3,64]{2,1,0:T(4,128)(2,1)}), bf16[8,3,64]{2,1,0:T(4,128)(2,1)S(1)}, u32[]{:S(2)}, u32[]{:S(2)}) async-start(bf16[8,3,64]{2,1,0:T(4,128)(2,1)} %reshape.243), calls=%async_computation.2 | async-start | bytes 16384 | tf_op jit(solution)/shard_map/while/body/eval_jaxpr/all_to_all | solution.py:132
  161.5 35.1 %copy-start.10 = (f32[2,24]{1,0:T(2,128)S(1)}, f32[2,24]{1,0:T(2,128)}, u32[]{:S(2)}) copy-start(f32[2,24]{1,0:T(2,128)} %get-tuple-element.817) | copy-start | bytes 580 | tf_op jit(solution)/shard_map/while
  161.5 20.2 %collective-permute-start = (bf16[8,2048]{1,0:T(8,128)(2,1)S(1)}, bf16[8,2048]{1,0:T(8,128)(2,1)S(1)}, u32[]{:S(2)}, u32[]{:S(2)}) collective-permute-start(bf16[8,2048]{1,0:T(8,128)(2,1)S(1)} %broadcast_select_fusion.2), channel_id=1, source_target_pairs={{8,0},{16,8},{24,16},{9,1},{17,9},{25,17},{10,2},{18,10},{26,18},{... | collective-permute-start | bytes 98312 | tf_op jit(solution)/shard_map/while/body/eval_jaxpr/ppermute | solution.py:14
  183.6 13.0 %all-to-all-start = ((bf16[8,3,2048]{2,1,0:T(4,128)(2,1)}), bf16[8,3,2048]{2,1,0:T(4,128)(2,1)S(1)}, u32[]{:S(2)}, u32[]{:S(2)}) async-start(bf16[8,3,2048]{2,1,0:T(4,128)(2,1)} %reshape.240), calls=%async_computation | async-start | bytes 262144 | tf_op jit(solution)/shard_map/while/body/eval_jaxpr/all_to_all | solution.py:97
  196.6 20.1 %copy-start.8 = (bf16[2,8,2048]{2,1,0:T(8,128)(2,1)S(1)}, bf16[2,8,2048]{2,1,0:T(8,128)(2,1)}, u32[]{:S(2)}) copy-start(bf16[2,8,2048]{2,1,0:T(8,128)(2,1)} %get-tuple-element.786) | copy-start | bytes 196612 | tf_op jit(solution)/shard_map/while
  196.6 20.9 %copy-start.4 = (bf16[2048,64]{1,0:T(8,128)(2,1)S(1)}, bf16[2048,64]{1,0:T(8,128)(2,1)}, u32[]{:S(2)}) copy-start(bf16[2048,64]{1,0:T(8,128)(2,1)} %copy-done.3) | copy-start | bytes 786436 | tf_op jit(solution)/shard_map/while
  196.7 4.7 %copy-start.2 = (bf16[1536,2048]{1,0:T(8,128)(2,1)S(1)}, bf16[1536,2048]{1,0:T(8,128)(2,1)}, u32[]{:S(2)}) copy-start(bf16[1536,2048]{1,0:T(8,128)(2,1)} %get-tuple-element.501) | copy-start | bytes 18874372 | tf_op jit(solution)/shard_map/while/body/eval_jaxpr/cond
  196.8 7.5 %copy-start.1 = (bf16[1536,2048]{1,0:T(8,128)(2,1)S(1)}, bf16[1536,2048]{1,0:T(8,128)(2,1)}, u32[]{:S(2)}) copy-start(bf16[1536,2048]{1,0:T(8,128)(2,1)} %get-tuple-element.502) | copy-start | bytes 18874372 | tf_op jit(solution)/shard_map/while/body/eval_jaxpr/cond
  196.8 7.4 %copy-start.6 = (f32[2,24,1536]{2,1,0:T(8,128)S(1)}, f32[2,24,1536]{2,1,0:T(8,128)}, u32[]{:S(2)}) copy-start(f32[2,24,1536]{2,1,0:T(8,128)} %get-tuple-element.500) | copy-start | bytes 884740 | tf_op jit(solution)/shard_map/while/body/eval_jaxpr/cond
  205.9 10.7 %all-to-all-start.1 = ((bf16[8,3,2048]{2,1,0:T(4,128)(2,1)}), bf16[8,3,2048]{2,1,0:T(4,128)(2,1)S(1)}, u32[]{:S(2)}, u32[]{:S(2)}) async-start(bf16[8,3,2048]{2,1,0:T(4,128)(2,1)} %reshape.241), calls=%async_computation.1 | async-start | bytes 262144 | tf_op jit(solution)/shard_map/while/body/eval_jaxpr/all_to_all | solution.py:125
  216.9 0.6 copy-start.9
  217.5 17.4 %copy-start.3 = (bf16[2048,64]{1,0:T(8,128)(2,1)}, bf16[2048,64]{1,0:T(8,128)(2,1)S(1)}, u32[]{:S(2)}) copy-start(bf16[2048,64]{1,0:T(8,128)(2,1)S(1)} %get-tuple-element.826) | copy-start | bytes 786436 | tf_op jit(solution)/shard_map/while
  218.2 9.8 %all-to-all-start.2 = ((bf16[8,3,64]{2,1,0:T(4,128)(2,1)}), bf16[8,3,64]{2,1,0:T(4,128)(2,1)S(1)}, u32[]{:S(2)}, u32[]{:S(2)}) async-start(bf16[8,3,64]{2,1,0:T(4,128)(2,1)} %reshape.243), calls=%async_computation.2 | async-start | bytes 16384 | tf_op jit(solution)/shard_map/while/body/eval_jaxpr/all_to_all | solution.py:132
  221.6 20.6 %copy-start.10 = (f32[2,24]{1,0:T(2,128)S(1)}, f32[2,24]{1,0:T(2,128)}, u32[]{:S(2)}) copy-start(f32[2,24]{1,0:T(2,128)} %get-tuple-element.817) | copy-start | bytes 580 | tf_op jit(solution)/shard_map/while
  221.6 7.7 %collective-permute-start = (bf16[8,2048]{1,0:T(8,128)(2,1)S(1)}, bf16[8,2048]{1,0:T(8,128)(2,1)S(1)}, u32[]{:S(2)}, u32[]{:S(2)}) collective-permute-start(bf16[8,2048]{1,0:T(8,128)(2,1)S(1)} %broadcast_select_fusion.2), channel_id=1, source_target_pairs={{8,0},{16,8},{24,16},{9,1},{17,9},{25,17},{10,2},{18,10},{26,18},{... | collective-permute-start | bytes 98312 | tf_op jit(solution)/shard_map/while/body/eval_jaxpr/ppermute | solution.py:14
  231.2 11.0 %all-to-all-start = ((bf16[8,3,2048]{2,1,0:T(4,128)(2,1)}), bf16[8,3,2048]{2,1,0:T(4,128)(2,1)S(1)}, u32[]{:S(2)}, u32[]{:S(2)}) async-start(bf16[8,3,2048]{2,1,0:T(4,128)(2,1)} %reshape.240), calls=%async_computation | async-start | bytes 262144 | tf_op jit(solution)/shard_map/while/body/eval_jaxpr/all_to_all | solution.py:97
  242.2 20.0 %copy-start.8 = (bf16[2,8,2048]{2,1,0:T(8,128)(2,1)S(1)}, bf16[2,8,2048]{2,1,0:T(8,128)(2,1)}, u32[]{:S(2)}) copy-start(bf16[2,8,2048]{2,1,0:T(8,128)(2,1)} %get-tuple-element.786) | copy-start | bytes 196612 | tf_op jit(solution)/shard_map/while
  242.2 20.8 %copy-start.4 = (bf16[2048,64]{1,0:T(8,128)(2,1)S(1)}, bf16[2048,64]{1,0:T(8,128)(2,1)}, u32[]{:S(2)}) copy-start(bf16[2048,64]{1,0:T(8,128)(2,1)} %copy-done.3) | copy-start | bytes 786436 | tf_op jit(solution)/shard_map/while
  242.3 4.7 %copy-start.2 = (bf16[1536,2048]{1,0:T(8,128)(2,1)S(1)}, bf16[1536,2048]{1,0:T(8,128)(2,1)}, u32[]{:S(2)}) copy-start(bf16[1536,2048]{1,0:T(8,128)(2,1)} %get-tuple-element.501) | copy-start | bytes 18874372 | tf_op jit(solution)/shard_map/while/body/eval_jaxpr/cond
  242.3 7.5 %copy-start.1 = (bf16[1536,2048]{1,0:T(8,128)(2,1)S(1)}, bf16[1536,2048]{1,0:T(8,128)(2,1)}, u32[]{:S(2)}) copy-start(bf16[1536,2048]{1,0:T(8,128)(2,1)} %get-tuple-element.502) | copy-start | bytes 18874372 | tf_op jit(solution)/shard_map/while/body/eval_jaxpr/cond
  242.3 7.4 %copy-start.6 = (f32[2,24,1536]{2,1,0:T(8,128)S(1)}, f32[2,24,1536]{2,1,0:T(8,128)}, u32[]{:S(2)}) copy-start(f32[2,24,1536]{2,1,0:T(8,128)} %get-tuple-element.500) | copy-start | bytes 884740 | tf_op jit(solution)/shard_map/while/body/eval_jaxpr/cond
  251.5 10.7 %all-to-all-start.1 = ((bf16[8,3,2048]{2,1,0:T(4,128)(2,1)}), bf16[8,3,2048]{2,1,0:T(4,128)(2,1)S(1)}, u32[]{:S(2)}, u32[]{:S(2)}) async-start(bf16[8,3,2048]{2,1,0:T(4,128)(2,1)} %reshape.241), calls=%async_computation.1 | async-start | bytes 262144 | tf_op jit(solution)/shard_map/while/body/eval_jaxpr/all_to_all | solution.py:125
  262.4 0.6 copy-start.9
Sparse Core Ops, SparseCore 0:
  263.2 60.2 reduce-scatter.1
where the time goes:
time: 333 us; the launch traced here: 330 us
  waiting for transfers between devices  148 us (44%)
  starting transfers between devices  70.1 us (21%)
  matrix products  37.1 us (11%)
  local copies, waits for them, and re-layouts  33.3 us (10%)
  other arithmetic  27.1 us (8%)
  between operations  14.2 us (4%)
    reduce_scatter x1, waiting for transfers between devices, on_device(): lax.psum_scatter(final_state[2], 'expert', scatter_dimension=0, tiled=True)  60.4 us
    all_to_all x5, waiting for transfers between devices, one_step(): lax.all_to_all(spread_rows, 'expert', split_axis=0, concat_axis=0, tiled=...  26.2 us
    all_to_all x5, waiting for transfers between devices, one_step(): lax.all_to_all(part_grad.reshape(n_expert, CAP, feat_dim), 'expert', spli...  26.1 us
    all_to_all x5, starting transfers between devices, one_step(): lax.all_to_all(spread_rows, 'expert', split_axis=0, concat_axis=0, tiled=...  19.4 us
    all_to_all x5, starting transfers between devices, one_step(): lax.all_to_all(part_grad.reshape(n_expert, CAP, feat_dim), 'expert', spli...  16.9 us
    all_to_all x5, starting transfers between devices, one_step(): lax.all_to_all(left_now.reshape(n_expert, CAP, sketch_dim), 'expert', spl...  16.7 us
    all_to_all x5, waiting for transfers between devices, one_step(): lax.all_to_all(left_now.reshape(n_expert, CAP, sketch_dim), 'expert', spl...  14 us
    ppermute x5, waiting for transfers between devices, from_behind(): return lax.ppermute(block, axis, route)  12.5 us
  transfers between devices with their start and end apart: 23, of which 19 were waited for; matrix products, arithmetic and copies ran while one was open for 14% of the time, Pallas kernels for 0%

commit v1 on v0

v1 whole, which is shorter than its diff:
```python
import functools

import jax
import jax.numpy as jnp
from jax import lax
from jax.experimental import pallas as pl
from jax.experimental.pallas import tpu as pltpu
from jax.sharding import PartitionSpec as P

EXPERTS = 8
EXM = 4
CAP = 3
META = 128

F32 = jnp.float32
BF16 = jnp.bfloat16


def contract(a, b, dim_a, dim_b):
    return lax.dot_general(a, b, (((dim_a,), (dim_b,)), ((), ())), preferred_element_type=F32)


def iota(shape, dim):
    return lax.broadcasted_iota(jnp.int32, shape, dim)


def slots_of(ids, n_micro, tok_dev, n_expert, block):
    tokens = n_micro * tok_dev
    lanes = n_expert * block
    hsplit = n_expert // EXPERTS
    group = iota((tokens, lanes), 1) // (block * hsplit)
    hit = ids[:, 0:1] == group
    for k in range(1, ids.shape[1]):
        hit = hit | (ids[:, k : k + 1] == group)
    row, col = iota((tokens, tokens), 0), iota((tokens, tokens), 1)
    earlier = ((row // tok_dev == col // tok_dev) & (col < row)).astype(F32)
    position = contract(earlier, hit.astype(F32), 1, 0)
    slot = iota((tokens, lanes), 1) % block - (iota((tokens, lanes), 0) // tok_dev) * CAP
    return hit & (slot >= 0) & (slot < CAP) & (position.astype(jnp.int32) == slot), group


def prepare(n_expert, block, ids_ref, w_ref, ex_ref, x_ref, top_ref, send_ref, sel_ref, comb_ref):
    n_micro, tok_dev = x_ref.shape[1], x_ref.shape[2]
    tokens = n_micro * tok_dev
    feat = x_ref.shape[3]
    ids = jnp.concatenate([ids_ref[0, m] for m in range(n_micro)], axis=0)
    weights = jnp.concatenate([w_ref[0, m].astype(F32) for m in range(n_micro)], axis=0)
    mask, group = slots_of(ids, n_micro, tok_dev, n_expert, block)
    weight = jnp.where(ids[:, 0:1] == group, weights[:, 0:1], 0.0)
    for k in range(1, ids.shape[1]):
        weight = weight + jnp.where(ids[:, k : k + 1] == group, weights[:, k : k + 1], 0.0)
    comb = jnp.where(mask, weight, 0.0)
    sel_ref[...] = mask.astype(BF16)
    comb_ref[...] = comb.astype(BF16)
    twice = n_expert * 2 * block
    wide, _ = slots_of(ids, n_micro, tok_dev, n_expert, 2 * block)
    lane = iota((tokens, twice), 1) % (2 * block)
    late = slots_of_late(ids, n_micro, tok_dev, n_expert, block)
    sel_saved = jnp.where(wide & (lane < block), 1.0, 0.0)
    sel_top = jnp.where(late, 1.0, 0.0)
    chosen = jnp.concatenate([sel_saved, sel_top], axis=0).astype(BF16)
    rows = jnp.concatenate(
        [x_ref[0, m] for m in range(n_micro)] + [top_ref[m] for m in range(n_micro)], axis=0
    )
    send_ref[:, 0:feat] = contract(chosen, rows, 0, 0).astype(BF16)
    examples = []
    for m in range(n_micro):
        diagonal = iota((tok_dev, tok_dev), 0) == iota((tok_dev, tok_dev), 1)
        own = jnp.where(diagonal, jnp.broadcast_to(ex_ref[m : m + 1, :], (tok_dev, tok_dev)), 0)
        examples.append(jnp.sum(own, axis=1, keepdims=True) + m * EXM)
    example = jnp.concatenate(examples, axis=0)
    onehot = (example == iota((tokens, META), 1)).astype(BF16)
    group_wide = iota((tokens, twice), 1) // (2 * block * (n_expert // EXPERTS))
    weight_wide = jnp.where(ids[:, 0:1] == group_wide, weights[:, 0:1], 0.0)
    for k in range(1, ids.shape[1]):
        weight_wide = weight_wide + jnp.where(
            ids[:, k : k + 1] == group_wide, weights[:, k : k + 1], 0.0
        )
    comb_wide = (sel_saved * weight_wide).astype(BF16)
    send_ref[:, feat:] = contract(comb_wide, onehot, 0, 0).astype(BF16)


def slots_of_late(ids, n_micro, tok_dev, n_expert, block):
    tokens = n_micro * tok_dev
    lanes = n_expert * 2 * block
    hsplit = n_expert // EXPERTS
    group = iota((tokens, lanes), 1) // (2 * block * hsplit)
    hit = ids[:, 0:1] == group
    for k in range(1, ids.shape[1]):
        hit = hit | (ids[:, k : k + 1] == group)
    row, col = iota((tokens, tokens), 0), iota((tokens, tokens), 1)
    earlier = ((row // tok_dev == col // tok_dev) & (col < row)).astype(F32)
    position = contract(earlier, hit.astype(F32), 1, 0)
    slot = iota((tokens, lanes), 1) % (2 * block) - block
    slot = slot - (iota((tokens, lanes), 0) // tok_dev) * CAP
    return hit & (slot >= 0) & (slot < CAP) & (position.astype(jnp.int32) == slot)


def on_device(
    saved_inputs,
    top_grad,
    expert_ids,
    route_weights,
    example_ids,
    gate_weight,
    up_weight,
    down_weight,
    left_proj,
    right_proj,
):
    n_section = lax.axis_size("section")
    n_expert = lax.axis_size("expert")
    section_id = lax.axis_index("section")
    expert_id = lax.axis_index("expert")
    hsplit = n_expert // EXPERTS
    n_micro, tok_dev, feat = saved_inputs.shape[1:]
    tokens = n_micro * tok_dev
    sketch_dim = left_proj.shape[2]
    flat = sketch_dim * sketch_dim
    used = n_micro * CAP
    extra = -(-flat // feat)
    block = -(-(used + extra) // 8) * 8
    n_rows = n_expert * block
    q_dev = n_micro * EXM * EXPERTS // n_expert

    vmem = pl.BlockSpec(memory_space=pltpu.VMEM)
    send, sel, comb = pl.pallas_call(
        functools.partial(prepare, n_expert, block),
        out_shape=(
            jax.ShapeDtypeStruct((2 * n_rows, feat + META), BF16),
            jax.ShapeDtypeStruct((tokens, n_rows), BF16),
            jax.ShapeDtypeStruct((tokens, n_rows), BF16),
        ),
        in_specs=[vmem] * 5,
        out_specs=(vmem, vmem, vmem),
    )(expert_ids, route_weights, example_ids, saved_inputs, top_grad)
    first = lax.all_to_all(
        send.reshape(n_expert, 2 * block, feat + META),
        "expert",
        split_axis=0,
        concat_axis=0,
        tiled=True,
    )
    x_rows = first[:, :block, :feat].reshape(n_rows, feat)
    meta = first[:, :block, feat:].reshape(n_rows, META)
    rows = first[:, block:, :feat].reshape(n_rows, feat)
    w_gate, w_up, w_down = gate_weight[0], up_weight[0], down_weight[0]
    pre_gate = contract(x_rows, w_gate, 1, 1)
    pre_up = contract(x_rows, w_up, 1, 1)
    sigmoid = jax.nn.sigmoid(pre_gate)
    to_up = pre_gate * sigmoid
    to_gate = pre_up * sigmoid * (1.0 + pre_gate * (1.0 - sigmoid))
    hidden = (to_up * pre_up).astype(BF16)
    left = contract(hidden, left_proj[0], 1, 0).astype(BF16)

    out_grad = top_grad.reshape(tokens, feat)
    right = jnp.zeros((n_rows, sketch_dim), F32)
    own_grad = jnp.zeros((tokens, feat), BF16)
    sketch_rows = None
    for stage in range(n_section):
        mine = section_id == n_section - 1 - stage
        if stage > 0:
            out_grad = lax.ppermute(
                new_grad, "section", [(n_section - stage, n_section - 1 - stage)]
            )
            spread = contract(sel, out_grad, 0, 0).astype(BF16)
            rows = lax.all_to_all(
                spread.reshape(n_expert, block, feat),
                "expert",
                split_axis=0,
                concat_axis=0,
                tiled=True,
            ).reshape(n_rows, feat)
        grad_hidden = contract(rows, w_down, 1, 1)
        grad_gate = (grad_hidden * to_gate).astype(BF16)
        grad_up = (grad_hidden * to_up).astype(BF16)
        part = contract(grad_gate, w_gate, 1, 0) + contract(grad_up, w_up, 1, 0)
        right = jnp.where(mine, contract(rows, right_proj[0], 1, 0), right)
        if stage == n_section - 1:
            lane = jnp.arange(flat, dtype=jnp.int32)
            axis = jnp.arange(sketch_dim, dtype=jnp.int32)
            spread_left = (axis[:, None] == lane[None, :] // sketch_dim).astype(BF16)
            spread_right = (axis[:, None] == lane[None, :] % sketch_dim).astype(BF16)
            right_high = right.astype(BF16)
            right_low = (right - right_high.astype(F32)).astype(BF16)
            outer = contract(left, spread_left, 1, 0) * (
                contract(right_high, spread_right, 1, 0) + contract(right_low, spread_right, 1, 0)
            )
            place = jnp.arange(n_rows, dtype=jnp.int32)
            target = (place // block) * q_dev
            here = (expert_id // hsplit >= target % EXPERTS) & (
                expert_id // hsplit < target % EXPERTS + q_dev
            )
            wanted = jnp.where(here, target // EXPERTS, -1)
            picks = (wanted[:, None] == jnp.arange(META, dtype=jnp.int32)[None, :]).astype(BF16)
            terms = contract(picks, meta, 1, 1)
            for part_no in range(extra):
                at_row = (place % block == used + part_no)[:, None]
                chosen = jnp.where(at_row, terms, 0.0).astype(BF16)
                part = part + contract(
                    chosen, outer[:, part_no * feat : (part_no + 1) * feat].astype(BF16), 1, 0
                )
        back = lax.all_to_all(
            part.astype(BF16).reshape(n_expert, block, feat),
            "expert",
            split_axis=0,
            concat_axis=0,
            tiled=True,
        )
        summed = contract(comb, back.reshape(n_rows, feat), 1, 0)
        new_grad = (out_grad.astype(F32) + summed).astype(BF16)
        own_grad = jnp.where(mine, new_grad, own_grad)
        sketch_rows = back[:, used : used + extra]
    sketch = sketch_rows.reshape(EXPERTS, hsplit, extra * feat).astype(F32).sum(axis=1)[:, :flat]
    start = (expert_id * q_dev) % EXPERTS
    sketch = lax.dynamic_slice_in_dim(sketch, start, q_dev, 0)
    return own_grad.reshape(1, n_micro, tok_dev, feat), sketch[None]


def solution(mesh):
    placed = (
        P("section", None, "expert", None),
        P(None, "expert", None),
        P("section", None, "expert", None),
        P("section", None, "expert", None),
        P(None, "expert"),
        P("section", "expert", None),
        P("section", "expert", None),
        P("section", "expert", None),
        P("section", "expert", None),
        P("section", None, None),
    )
    return jax.shard_map(
        on_device,
        mesh=mesh,
        in_specs=placed,
        out_specs=(P("section", None, "expert", None), P("section", "expert", None)),
        check_vma=False,
    )
```

time: 333 us -> 170 us (0.51)
  waiting for transfers between devices: 148 us -> 23.8 us
  blocking collectives: 0 us -> 71.3 us
  starting transfers between devices: 70.1 us -> 13.7 us
  local copies, waits for them, and re-layouts: 33.3 us -> 3.67 us
  other arithmetic: 27.1 us -> 1.16 us
  matrix products: 37.1 us -> 51.8 us
  between operations: 14.2 us -> 1.23 us
    all_to_all x0 -> x5, blocking collectives: none -> 71.3 us  [the longest x3 35.9 us: on_device(): lax.all_to_all(part.astype(BF16).reshape(n_expert, block, feat), 'expert'...]
    reduce_scatter x1 -> x0, waiting for transfers between devices: 60.4 us -> none  [on_device(): lax.psum_scatter(final_state[2], 'expert', scatter_dimension=0, tiled=True)]
    all_to_all x17 -> x3, waiting for transfers between devices: 74.9 us -> 19.6 us  [the longest x2 14.1 us: on_device(): lax.all_to_all(spread.reshape(n_expert, block, feat), 'expert', split_axi...]
    all_to_all x17 -> x3, starting transfers between devices: 63.6 us -> 11 us  [the longest x2 7.63 us: on_device(): lax.all_to_all(spread.reshape(n_expert, block, feat), 'expert', split_axi...]
    add x12 -> x0, other arithmetic: 15.1 us -> none  [the longest x5 10.4 us: one_step(): sketch + jnp.where(is_live, contrib.reshape(q_total, sketch_dim * sketch_...]
    dot_general x36 -> x31, matrix products: 37.1 us -> 51.8 us  [contract(): lax.dot_general(a, b, (((dim_a,), (dim_b,)), ((), ())), preferred_element...]
    reshape x27 -> x0, local copies, waits for them, and re-layouts: 11.4 us -> none  [the longest x5 3.69 us: one_step(): jnp.repeat(grad_rows.reshape(groups, CAP, feat_dim), hsplit, axis=0)]
    ppermute x5 -> x3, waiting for transfers between devices: 12.5 us -> 4.13 us  [on_device(): lax.ppermute(new_grad, 'section', [(n_section - stage, n_section - 1 - st...]
  transfers between devices with their start and end apart: 23 -> 6, of which waited for: 19 -> 4; matrix products, arithmetic and copies ran while one was open for 14% -> 5% of each run, Pallas kernels for 0% -> 0%
where the time goes in v1:
time: 170 us; the launch traced here: 169 us
  blocking collectives  71.3 us (42%)
  matrix products  51.8 us (30%)
  waiting for transfers between devices  23.8 us (14%)
  starting transfers between devices  13.7 us (8%)
  local copies, waits for them, and re-layouts  3.67 us (2%)
  Pallas kernels  2.26 us (1%)
    dot_general x31, matrix products, contract(): lax.dot_general(a, b, (((dim_a,), (dim_b,)), ((), ())), preferred_element...  51.8 us
    all_to_all x3, blocking collectives, on_device(): lax.all_to_all(part.astype(BF16).reshape(n_expert, block, feat), 'expert'...  35.9 us
    all_to_all x1, blocking collectives, on_device(): lax.all_to_all(send.reshape(n_expert, 2 * block, feat + META), 'expert',...  23.5 us
    all_to_all x2, waiting for transfers between devices, on_device(): lax.all_to_all(spread.reshape(n_expert, block, feat), 'expert', split_axi...  14.1 us
    all_to_all x1, blocking collectives, on_device(): lax.all_to_all(spread.reshape(n_expert, block, feat), 'expert', split_axi...  11.9 us
    all_to_all x2, starting transfers between devices, on_device(): lax.all_to_all(spread.reshape(n_expert, block, feat), 'expert', split_axi...  7.63 us
    all_to_all x1, waiting for transfers between devices, on_device(): lax.all_to_all(part.astype(BF16).reshape(n_expert, block, feat), 'expert'...  5.52 us
    ppermute x3, waiting for transfers between devices, on_device(): lax.ppermute(new_grad, 'section', [(n_section - stage, n_section - 1 - st...  4.13 us
  transfers between devices with their start and end apart: 6, of which 4 were waited for; matrix products, arithmetic and copies ran while one was open for 5% of the time, Pallas kernels for 0%

profile of v1, /device:TPU:0, one launch (start us, length us, event | category | flops | bytes accessed | tf_op | source)
XLA Modules:
  0.0 168.9 jit_solution(13056192900857380344)
XLA Ops:
  0.6 0.0 copy-start
  0.6 1.4 copy.13.w_ref
  2.0 1.4 copy.12.ids_ref
  3.4 2.3 %shard_map.113 = (bf16[128,2176]{1,0:T(8,128)(2,1)}, bf16[16,64]{1,0:T(8,128)(2,1)}, bf16[16,64]{1,0:T(8,128)(2,1)}) custom-call(s32[1,2,8,2]{3,2,1,0:T(8,128)} %copy.12.ids_ref, bf16[1,2,8,2]{3,2,1,0:T(8,128)(2,1)} %copy.13.w_ref, s32[2,8]{1,0:T(2,128)} %ex_ref.1, bf16[1,2,8,2048]{3,2,1,0:T(8,128)(2,1)} %x_ref.1, bf16[2,8,2048]{2,1,0:T(8,128)(2,1)} %top_ref.1), custom_call_target="tpu_custom_call" | custom-call | tf_op jit(solution)/shard_map/pallas_call | solution.py:127
  5.7 23.5 %all_to_all.40 = bf16[8,16,2176]{2,1,0:T(8,128)(2,1)S(1)} all-to-all(bf16[8,16,2176]{2,1,0:T(8,128)(2,1)} %bitcast.150), channel_id=1, replica_groups=mesh['section'=4,'expert'=8] {'expert'}, dimensions={0} | all-to-all | bytes 1114112 | tf_op jit(solution)/shard_map/all_to_all | solution.py:137
  29.2 5.1 %fusion.18 = f32[64,1536]{1,0:T(8,128)S(1)} fusion(bf16[1,1536,2048]{2,1,0:T(8,128)(2,1)} %param.16, bf16[8,16,2176]{2,1,0:T(8,128)(2,1)S(1)} %all_to_all.40), kind=kOutput, calls=%fused_computation.18 | convolution fusion | flops 402653184 | bytes 6946816 | tf_op jit(solution)/shard_map/dot_general | solution.py:20
  34.3 0.0 slice-start.2
  34.3 2.0 %fusion.26 = f32[64,1536]{1,0:T(8,128)S(1)} fusion(bf16[1,1536,2048]{2,1,0:T(8,128)(2,1)S(1)} %copy-done.1, bf16[8,16,2176]{2,1,0:T(8,128)(2,1)S(1)} %all_to_all.40), kind=kOutput, calls=%fused_computation.26 | convolution fusion | flops 402653184 | bytes 6946816 | tf_op jit(solution)/shard_map/dot_general | solution.py:20
  36.3 0.0 slice-start.3
  36.3 2.1 %add_multiply_fusion = (f32[64,1536]{1,0:T(8,128)S(1)}, f32[64,1536]{1,0:T(8,128)S(1)}) fusion(f32[64,1536]{1,0:T(8,128)S(1)} %fusion.18, bf16[1,1536,2048]{2,1,0:T(8,128)(2,1)S(1)} %bitcast.143, bf16[8,16,2176]{2,1,0:T(8,128)(2,1)S(1)} %all_to_all.40), kind=kOutput, calls=%fused_computation.74 | convolution fusion | flops 403439616 | bytes 7733248 | tf_op jit(solution)/shard_map/dot_general | solution.py:20
  38.4 0.0 copy-start.8
  38.5 1.2 fusion.6
  39.7 1.2 fusion.52
  41.0 11.4 %all_to_all.41 = bf16[8,8,2048]{2,1,0:T(8,128)(2,1)S(1)} all-to-all(bf16[8,8,2048]{2,1,0:T(8,128)(2,1)S(1)} %fusion.52), channel_id=1, replica_groups=mesh['section'=4,'expert'=8] {'expert'}, dimensions={0} | all-to-all | bytes 524288 | tf_op jit(solution)/shard_map/all_to_all | solution.py:203
  52.3 0.2 fusion.65
  52.5 0.7 collective-permute-start
  53.2 0.0 collective-permute-done
  53.2 0.2 fusion.61
  53.4 11.9 %all_to_all.42 = bf16[8,8,2048]{2,1,0:T(8,128)(2,1)S(1)} all-to-all(bf16[8,8,2048]{2,1,0:T(8,128)(2,1)S(1)} %fusion.61), channel_id=1, replica_groups=mesh['section'=4,'expert'=8] {'expert'}, dimensions={0} | all-to-all | bytes 524288 | tf_op jit(solution)/shard_map/all_to_all | solution.py:167
  65.4 2.0 %fusion.24 = f32[64,1536]{1,0:T(8,128)S(1)} fusion(bf16[1,1536,2048]{2,1,0:T(8,128)(2,1)S(1)} %copy-done.1, bf16[8,8,2048]{2,1,0:T(8,128)(2,1)S(1)} %all_to_all.42), kind=kOutput, calls=%fused_computation.24 | convolution fusion | flops 402653184 | bytes 6946816 | tf_op jit(solution)/shard_map/dot_general | solution.py:20
  67.4 1.2 fusion.4
  68.7 1.2 fusion.55
  69.9 11.9 %all_to_all.43 = bf16[8,8,2048]{2,1,0:T(8,128)(2,1)S(1)} all-to-all(bf16[8,8,2048]{2,1,0:T(8,128)(2,1)S(1)} %fusion.55), channel_id=1, replica_groups=mesh['section'=4,'expert'=8] {'expert'}, dimensions={0} | all-to-all | bytes 524288 | tf_op jit(solution)/shard_map/all_to_all | solution.py:203
  81.8 0.2 add_convert_fusion.2
  82.0 0.7 collective-permute-start.1
  82.6 0.0 collective-permute-done.1
  82.6 0.0 copy-start.11
  82.7 1.0 fusion.62
  83.6 3.6 %all-to-all-start.4 = ((bf16[8,8,2048]{2,1,0:T(8,128)(2,1)}), bf16[8,8,2048]{2,1,0:T(8,128)(2,1)S(1)}, u32[]{:S(2)}, u32[]{:S(2)}) async-start(bf16[8,8,2048]{2,1,0:T(8,128)(2,1)} %fusion.62), calls=%async_computation.4 | async-start | bytes 524288 | tf_op jit(solution)/shard_map/all_to_all | solution.py:167
  87.2 0.6 broadcast_compare_fusion.1
  87.8 0.5 broadcast_compare_fusion
  88.3 7.0 %all-to-all-done.4 = bf16[8,8,2048]{2,1,0:T(8,128)(2,1)S(1)} async-done(((bf16[8,8,2048]{2,1,0:T(8,128)(2,1)}), bf16[8,8,2048]{2,1,0:T(8,128)(2,1)S(1)}, u32[]{:S(2)}, u32[]{:S(2)}) %all-to-all-start.4) | async-done | bytes 262176 | tf_op jit(solution)/shard_map/all_to_all | solution.py:167
  95.3 4.8 %fusion.22 = f32[64,1536]{1,0:T(8,128)S(1)} fusion(bf16[1,1536,2048]{2,1,0:T(8,128)(2,1)} %param.17, bf16[8,8,2048]{2,1,0:T(8,128)(2,1)S(1)} %all-to-all-done.4), kind=kOutput, calls=%fused_computation.22 | convolution fusion | flops 402653184 | bytes 6946816 | tf_op jit(solution)/shard_map/dot_general | solution.py:20
  100.1 0.0 slice-start.5
  100.1 4.2 %fusion.2 = f32[64,2048]{1,0:T(8,128)S(1)} fusion(bf16[1,1536,2048]{2,1,0:T(8,128)(2,1)} %param.15, f32[64,1536]{1,0:T(8,128)S(1)} %fusion.22, f32[64,1536]{1,0:T(8,128)S(1)} %get-tuple-element.8), kind=kOutput, calls=%fused_computation.2 | convolution fusion | flops 402849792 | bytes 7602176 | tf_op jit(solution)/shard_map/dot_general | solution.py:20
  104.3 1.9 %fusion.58 = bf16[8,8,2048]{2,1,0:T(8,128)(2,1)} fusion(f32[64,2048]{1,0:T(8,128)S(1)} %fusion.2, bf16[1,1536,2048]{2,1,0:T(8,128)(2,1)S(1)} %bitcast.147, f32[64,1536]{1,0:T(8,128)S(1)} %fusion.22, f32[64,1536]{1,0:T(8,128)S(1)} %get-tuple-element.9), kind=kOutput, calls=%fused_computation.46 | convolution fusion | flops 403505152 | bytes 7864320 | tf_op jit(solution)/shard_map/dot_general | solution.py:20
  106.3 3.4 %all-to-all-start.5 = ((bf16[8,8,2048]{2,1,0:T(8,128)(2,1)}), bf16[8,8,2048]{2,1,0:T(8,128)(2,1)S(1)}, u32[]{:S(2)}, u32[]{:S(2)}) async-start(bf16[8,8,2048]{2,1,0:T(8,128)(2,1)} %fusion.58), calls=%async_computation.5 | async-start | bytes 524288 | tf_op jit(solution)/shard_map/all_to_all | solution.py:203
  109.7 2.6 %fusion.68 = f32[64,4096]{1,0:T(8,128)} fusion(s32[4096]{0:T(1024)S(1)} %add_select_fusion, f32[64,1536]{1,0:T(8,128)} %copy-done.4, bf16[1,1536,64]{1,2,0:T(8,128)(2,1)} %param.18, f32[64,1536]{1,0:T(8,128)S(1)} %get-tuple-element.9), kind=kOutput, calls=%fused_computation.58 | convolution fusion | flops 46993408 | bytes 2048000 | tf_op jit(solution)/shard_map/dot_general | solution.py:20
  112.3 5.5 %all-to-all-done.5 = bf16[8,8,2048]{2,1,0:T(8,128)(2,1)S(1)} async-done(((bf16[8,8,2048]{2,1,0:T(8,128)(2,1)}), bf16[8,8,2048]{2,1,0:T(8,128)(2,1)S(1)}, u32[]{:S(2)}, u32[]{:S(2)}) %all-to-all-start.5) | async-done | bytes 262176 | tf_op jit(solution)/shard_map/all_to_all | solution.py:203
  117.9 1.0 add_convert_fusion.1
  118.9 1.3 collective-permute-start.2
  120.2 1.5 fusion.103
  121.7 4.1 %collective-permute-done.2 = bf16[16,2048]{1,0:T(8,128)(2,1)S(1)} collective-permute-done((bf16[16,2048]{1,0:T(8,128)(2,1)S(1)}, bf16[16,2048]{1,0:T(8,128)(2,1)S(1)}, u32[]{:S(2)}, u32[]{:S(2)}) %collective-permute-start.2) | collective-permute-done | bytes 65568 | tf_op jit(solution)/shard_map/ppermute | solution.py:163
  125.8 1.6 fusion.63
  127.4 4.0 %all-to-all-start.6 = ((bf16[8,8,2048]{2,1,0:T(8,128)(2,1)}), bf16[8,8,2048]{2,1,0:T(8,128)(2,1)}, u32[]{:S(2)}, u32[]{:S(2)}) async-start(bf16[8,8,2048]{2,1,0:T(8,128)(2,1)} %fusion.63), calls=%async_computation.6 | async-start | bytes 524288 | tf_op jit(solution)/shard_map/all_to_all | solution.py:167
  131.5 1.2 fusion.79
  132.7 1.8 %fusion.66 = f32[64,64]{1,0:T(8,128)} fusion(f32[64,64]{1,0:T(8,128)S(1)} %fusion.79, bf16[1,2048,64]{1,2,0:T(8,128)(2,1)S(1)} %copy-done, bf16[8,16,2176]{2,1,0:T(8,128)(2,1)} %copy-done.2, pred[]{:T(512)S(6)} %eq.95, pred[]{:T(512)S(6)} %eq.94), kind=kOutput, calls=%fused_computation.54 | convolution fusion | flops 16785408 | bytes 557058 | tf_op jit(solution)/shard_map/dot_general | solution.py:20
  134.5 7.1 %all-to-all-done.6 = bf16[8,8,2048]{2,1,0:T(8,128)(2,1)} async-done(((bf16[8,8,2048]{2,1,0:T(8,128)(2,1)}), bf16[8,8,2048]{2,1,0:T(8,128)(2,1)}, u32[]{:S(2)}, u32[]{:S(2)}) %all-to-all-start.6) | async-done | bytes 262176 | tf_op jit(solution)/shard_map/all_to_all | solution.py:167
  141.6 4.9 %fusion.20 = f32[64,1536]{1,0:T(8,128)S(1)} fusion(bf16[1,1536,2048]{2,1,0:T(8,128)(2,1)} %param.17, bf16[8,8,2048]{2,1,0:T(8,128)(2,1)} %all-to-all-done.6), kind=kOutput, calls=%fused_computation.20 | convolution fusion | flops 402653184 | bytes 6946816 | tf_op jit(solution)/shard_map/dot_general | solution.py:20
  146.5 0.0 slice-start.7
  146.5 0.0 copy-start.12
  146.5 4.2 %fusion = f32[64,2048]{1,0:T(8,128)S(1)} fusion(bf16[1,1536,2048]{2,1,0:T(8,128)(2,1)} %param.15, f32[64,1536]{1,0:T(8,128)S(1)} %fusion.20, f32[64,1536]{1,0:T(8,128)S(1)} %get-tuple-element.8), kind=kOutput, calls=%fused_computation | convolution fusion | flops 402849792 | bytes 7602176 | tf_op jit(solution)/shard_map/dot_general | solution.py:20
  150.7 0.0 copy-start.10
  150.8 1.2 fusion.39
  152.0 1.2 fusion.82
  153.2 0.2 fusion.67
  153.4 0.3 fusion.69
  153.7 0.4 fusion.29
  154.1 0.3 convolution_add_fusion.2
  154.4 0.3 fusion.64
  154.7 12.6 %all_to_all.44 = bf16[8,8,2048]{2,1,0:T(8,128)(2,1)S(1)} all-to-all(bf16[8,8,2048]{2,1,0:T(8,128)(2,1)S(1)} %fusion.64), channel_id=1, replica_groups=mesh['section'=4,'expert'=8] {'expert'}, dimensions={0} | all-to-all | bytes 524288 | tf_op jit(solution)/shard_map/all_to_all | solution.py:203
  167.2 0.1 slice_convert_fusion
  167.3 0.8 reshape.212
  168.1 0.8 fusion.98
  (52 shorter events, 0.1 us)
Async XLA Ops:
  0.6 130.8 %copy-start = (bf16[1,2048,64]{1,2,0:T(8,128)(2,1)S(1)}, bf16[1,2048,64]{1,2,0:T(8,128)(2,1)}, u32[]{:S(2)}) copy-start(bf16[1,2048,64]{1,2,0:T(8,128)(2,1)} %param.19) | copy-start | bytes 786436
  5.7 28.6 %copy-start.1 = (bf16[1,1536,2048]{2,1,0:T(8,128)(2,1)S(1)}, bf16[1,1536,2048]{2,1,0:T(8,128)(2,1)}, u32[]{:S(2)}) copy-start(bf16[1,1536,2048]{2,1,0:T(8,128)(2,1)} %param.17) | copy-start | bytes 18874372
  5.7 30.6 %slice-start = ((s8[6291456]{0:T(1024)(128)(4,1)}), s8[4194304]{0:T(1024)(128)(4,1)S(1)}, s32[]{:S(2)}) async-start(s8[6291456]{0:T(1024)(128)(4,1)} %bitcast.142), calls=%async_computation.8 | async-start | bytes 8388608
  29.2 23.3 %copy-start.2 = (bf16[8,16,2176]{2,1,0:T(8,128)(2,1)}, bf16[8,16,2176]{2,1,0:T(8,128)(2,1)S(1)}, u32[]{:S(2)}) copy-start(bf16[8,16,2176]{2,1,0:T(8,128)(2,1)S(1)} %all_to_all.40) | copy-start | bytes 1671172
  29.2 7.1 %slice-start.1 = ((s8[6291456]{0:T(1024)(128)(4,1)}), s8[2097152]{0:T(1024)(128)(4,1)S(1)}, s32[]{:S(2)}) async-start(s8[6291456]{0:T(1024)(128)(4,1)} %bitcast.142), calls=%async_computation.9 | async-start | bytes 4194304
  34.3 4.2 %copy-start.4 = (f32[64,1536]{1,0:T(8,128)}, f32[64,1536]{1,0:T(8,128)S(1)}, u32[]{:S(2)}) copy-start(f32[64,1536]{1,0:T(8,128)S(1)} %fusion.18) | copy-start | bytes 1179652
  34.3 5.4 %slice-start.2 = ((s8[6291456]{0:T(1024)(128)(4,1)}), s8[4194304]{0:T(1024)(128)(4,1)S(1)}, s32[]{:S(2)}) async-start(s8[6291456]{0:T(1024)(128)(4,1)} %bitcast.144), calls=%async_computation.10 | async-start | bytes 8388608
  36.3 3.4 %slice-start.3 = ((s8[6291456]{0:T(1024)(128)(4,1)}), s8[2097152]{0:T(1024)(128)(4,1)S(1)}, s32[]{:S(2)}) async-start(s8[6291456]{0:T(1024)(128)(4,1)} %bitcast.144), calls=%async_computation.11 | async-start | bytes 4194304
  38.4 13.9 %copy-start.8 = (bf16[2,8,2048]{2,1,0:T(8,128)(2,1)S(1)}, bf16[2,8,2048]{2,1,0:T(8,128)(2,1)}, u32[]{:S(2)}) copy-start(bf16[2,8,2048]{2,1,0:T(8,128)(2,1)} %top_ref.1) | copy-start | bytes 196612
  38.5 13.9 %copy-start.14 = (bf16[16,64]{1,0:T(8,128)(2,1)S(1)}, bf16[16,64]{1,0:T(8,128)(2,1)}, u32[]{:S(2)}) copy-start(bf16[16,64]{1,0:T(8,128)(2,1)} %get-tuple-element.5) | copy-start | bytes 6148
  39.7 13.5 %copy-start.16 = (bf16[16,64]{1,0:T(8,128)(2,1)S(1)}, bf16[16,64]{1,0:T(8,128)(2,1)}, u32[]{:S(2)}) copy-start(bf16[16,64]{1,0:T(8,128)(2,1)} %get-tuple-element.7) | copy-start | bytes 6148
  52.5 0.7 collective-permute-start
  65.4 3.3 %copy-start.3 = (bf16[8,8,2048]{2,1,0:T(8,128)(2,1)}, bf16[8,8,2048]{2,1,0:T(8,128)(2,1)S(1)}, u32[]{:S(2)}) copy-start(bf16[8,8,2048]{2,1,0:T(8,128)(2,1)S(1)} %all_to_all.42) | copy-start | bytes 786436
  82.0 0.7 collective-permute-start.1
  82.6 1.0 copy-start.11
  83.6 11.7 %all-to-all-start.4 = ((bf16[8,8,2048]{2,1,0:T(8,128)(2,1)}), bf16[8,8,2048]{2,1,0:T(8,128)(2,1)S(1)}, u32[]{:S(2)}, u32[]{:S(2)}) async-start(bf16[8,8,2048]{2,1,0:T(8,128)(2,1)} %fusion.62), calls=%async_computation.4 | async-start | bytes 524288 | tf_op jit(solution)/shard_map/all_to_all | solution.py:167
  88.3 16.0 %slice-start.4 = ((s8[6291456]{0:T(1024)(128)(4,1)}), s8[2097152]{0:T(1024)(128)(4,1)S(1)}, s32[]{:S(2)}) async-start(s8[6291456]{0:T(1024)(128)(4,1)} %bitcast.146), calls=%async_computation.12 | async-start | bytes 4194304
  100.1 4.2 %slice-start.5 = ((s8[6291456]{0:T(1024)(128)(4,1)}), s8[4194304]{0:T(1024)(128)(4,1)S(1)}, s32[]{:S(2)}) async-start(s8[6291456]{0:T(1024)(128)(4,1)} %bitcast.146), calls=%async_computation.13 | async-start | bytes 8388608
  106.3 11.6 %all-to-all-start.5 = ((bf16[8,8,2048]{2,1,0:T(8,128)(2,1)}), bf16[8,8,2048]{2,1,0:T(8,128)(2,1)S(1)}, u32[]{:S(2)}, u32[]{:S(2)}) async-start(bf16[8,8,2048]{2,1,0:T(8,128)(2,1)} %fusion.58), calls=%async_computation.5 | async-start | bytes 524288 | tf_op jit(solution)/shard_map/all_to_all | solution.py:203
  118.9 13.8 %copy-start.6 = (bf16[16,2048]{1,0:T(8,128)(2,1)}, bf16[16,2048]{1,0:T(8,128)(2,1)S(1)}, u32[]{:S(2)}) copy-start(bf16[16,2048]{1,0:T(8,128)(2,1)S(1)} %add_convert_fusion.1) | copy-start | bytes 196612
  118.9 6.9 %collective-permute-start.2 = (bf16[16,2048]{1,0:T(8,128)(2,1)S(1)}, bf16[16,2048]{1,0:T(8,128)(2,1)S(1)}, u32[]{:S(2)}, u32[]{:S(2)}) collective-permute-start(bf16[16,2048]{1,0:T(8,128)(2,1)S(1)} %add_convert_fusion.1), channel_id=1, source_target_pairs={{8,0},{9,1},{10,2},{11,3},{12,4},{13,5},{14,6},{15,7}} | collective-permute-start | bytes 196616 | tf_op jit(solution)/shard_map/ppermute | solution.py:163
  125.8 6.9 %copy-start.9 = (bf16[16,2048]{1,0:T(8,128)(2,1)}, bf16[16,2048]{1,0:T(8,128)(2,1)S(1)}, u32[]{:S(2)}) copy-start(bf16[16,2048]{1,0:T(8,128)(2,1)S(1)} %collective-permute-done.2) | copy-start | bytes 196612
  127.4 14.1 %all-to-all-start.6 = ((bf16[8,8,2048]{2,1,0:T(8,128)(2,1)}), bf16[8,8,2048]{2,1,0:T(8,128)(2,1)}, u32[]{:S(2)}, u32[]{:S(2)}) async-start(bf16[8,8,2048]{2,1,0:T(8,128)(2,1)} %fusion.63), calls=%async_computation.6 | async-start | bytes 524288 | tf_op jit(solution)/shard_map/all_to_all | solution.py:167
  134.5 16.2 %slice-start.6 = ((s8[6291456]{0:T(1024)(128)(4,1)}), s8[2097152]{0:T(1024)(128)(4,1)S(1)}, s32[]{:S(2)}) async-start(s8[6291456]{0:T(1024)(128)(4,1)} %bitcast.148), calls=%async_computation.14 | async-start | bytes 4194304
  146.5 4.2 %slice-start.7 = ((s8[6291456]{0:T(1024)(128)(4,1)}), s8[4194304]{0:T(1024)(128)(4,1)S(1)}, s32[]{:S(2)}) async-start(s8[6291456]{0:T(1024)(128)(4,1)} %bitcast.148), calls=%async_computation.15 | async-start | bytes 8388608
  146.5 6.7 %copy-start.12 = (f32[64,64]{1,0:T(8,128)S(1)}, f32[64,64]{1,0:T(8,128)}, u32[]{:S(2)}) copy-start(f32[64,64]{1,0:T(8,128)} %fusion.66) | copy-start | bytes 49156
  150.7 3.0 %copy-start.5 = (f32[64,4096]{1,0:T(8,128)S(1)}, f32[64,4096]{1,0:T(8,128)}, u32[]{:S(2)}) copy-start(f32[64,4096]{1,0:T(8,128)} %fusion.68) | copy-start | bytes 3145732
  150.7 3.4 %copy-start.13 = (bf16[64,64]{1,0:T(8,128)(2,1)S(1)}, bf16[64,64]{1,0:T(8,128)(2,1)}, u32[]{:S(2)}) copy-start(bf16[64,64]{1,0:T(8,128)(2,1)} %fusion.103) | copy-start | bytes 24580
  150.7 3.4 %copy-start.17 = (pred[64]{0:T(512)(128)(4,1)S(1)}, pred[64]{0:T(512)(128)(4,1)}, u32[]{:S(2)}) copy-start(pred[64]{0:T(512)(128)(4,1)} %broadcast_compare_fusion) | copy-start | bytes 196
  150.7 3.7 %copy-start.18 = (pred[64]{0:T(512)(128)(4,1)S(1)}, pred[64]{0:T(512)(128)(4,1)}, u32[]{:S(2)}) copy-start(pred[64]{0:T(512)(128)(4,1)} %broadcast_compare_fusion.1) | copy-start | bytes 196
  150.7 17.4 %copy-start.7 = (bf16[16,2048]{1,0:T(8,128)(2,1)S(1)}, bf16[16,2048]{1,0:T(8,128)(2,1)}, u32[]{:S(2)}) copy-start(bf16[16,2048]{1,0:T(8,128)(2,1)} %copy-done.6) | copy-start | bytes 196612
  150.7 17.4 %copy-start.10 = (bf16[16,2048]{1,0:T(8,128)(2,1)S(1)}, bf16[16,2048]{1,0:T(8,128)(2,1)}, u32[]{:S(2)}) copy-start(bf16[16,2048]{1,0:T(8,128)(2,1)} %copy-done.9) | copy-start | bytes 196612
  150.7 17.3 %copy-start.15 = (bf16[16,64]{1,0:T(8,128)(2,1)S(1)}, bf16[16,64]{1,0:T(8,128)(2,1)}, u32[]{:S(2)}) copy-start(bf16[16,64]{1,0:T(8,128)(2,1)} %get-tuple-element.5) | copy-start | bytes 6148

commit v2 on v0

v2 whole, which is shorter than its diff:
```python
import functools
import math

import jax
import jax.numpy as jnp
from jax import lax
from jax.experimental import pallas as pl
from jax.experimental.pallas import tpu as pltpu
from jax.sharding import PartitionSpec as P

EXPERTS = 8
EXM = 4
CAP = 3
LANES = 128
TILE = 256
MOST_PERMUTES = 8

F32 = jnp.float32
BF16 = jnp.bfloat16
VMEM = pl.BlockSpec(memory_space=pltpu.VMEM)
HBM = pl.BlockSpec(memory_space=pltpu.HBM)


def contract(a, b, dim_a, dim_b):
    return lax.dot_general(a, b, (((dim_a,), (dim_b,)), ((), ())), preferred_element_type=F32)


def iota(shape, dim):
    return lax.broadcasted_iota(jnp.int32, shape, dim)


def ones_where(mask):
    return jnp.where(mask, 1.0, 0.0).astype(F32)


def partner(device, turn, amount):
    if amount & (amount - 1) == 0:
        return device ^ turn
    return (turn + 2 * amount - device) % amount


def size_of(arrays):
    return sum(a.dtype.itemsize * a.size for a in arrays)


def call(kernel, out_shape, inputs, spec=VMEM, scratch=(), limit=12 << 20):
    return pl.pallas_call(
        kernel,
        out_shape=out_shape,
        in_specs=[spec] * len(inputs),
        out_specs=tuple(VMEM for _ in out_shape),
        scratch_shapes=list(scratch),
        compiler_params=pltpu.CompilerParams(vmem_limit_bytes=limit),
    )(*inputs)


def copy_all(pairs, sems):
    copies = []
    for number, (source, target) in enumerate(pairs):
        copies.append(pltpu.make_async_copy(source, target, sems.at[number]))
        copies[-1].start()
    for copy in copies:
        copy.wait()


def names(fields, top_k, group):
    hit = fields[0:1, :] == group
    for k in range(1, top_k):
        hit = hit | (fields[k : k + 1, :] == group)
    return ones_where(hit)


def prepare(n_section, n_expert, block, ids_hbm, w_hbm, ex_hbm, x_hbm, top_hbm, *refs):
    saved_ref, top_send_ref, slots_ref = refs[:3]
    ids_ref, w_ref, ex_ref, x_ref, top_ref, sems = refs[3:]
    from_hbm = (ids_hbm, w_hbm, ex_hbm, x_hbm, top_hbm)
    copy_all(list(zip(from_hbm, (ids_ref, w_ref, ex_ref, x_ref, top_ref))), sems)
    n_micro, top_k, tok_dev = ids_ref.shape[1:]
    tokens = n_micro * tok_dev
    n_all = n_expert * tokens
    n_fields = 2 * top_k + 1
    feat = x_ref.shape[3]
    section, me = lax.axis_index("section"), lax.axis_index("expert")
    padded = -(-n_fields // 8) * 8
    local = jnp.zeros((padded, tokens), F32)
    packed = jnp.zeros((padded, n_all), F32)
    for m in range(n_micro):
        row = iota((padded, tok_dev), 0)
        example = ex_ref[m : m + 1, :] + m * EXM
        fields = jnp.where(row == 2 * top_k, example.astype(F32), 0.0)
        for k in range(top_k):
            fields = jnp.where(row == k, ids_ref[0, m, k : k + 1, :].astype(F32), fields)
            fields = jnp.where(row == top_k + k, w_ref[0, m, k : k + 1, :].astype(F32), fields)
        here = iota((tok_dev, tokens), 1) == m * tok_dev + iota((tok_dev, tokens), 0)
        local = local + contract(fields, ones_where(here), 1, 0)
        there = me * tokens + m * tok_dev + iota((tok_dev, n_all), 0)
        packed = packed + contract(fields, ones_where(iota((tok_dev, n_all), 1) == there), 1, 0)
    rows = n_expert * block
    group = (iota((rows, tokens), 0) // (block * (n_expert // EXPERTS))).astype(F32)
    hit = names(local, top_k, group)
    early, late = iota((tokens, tokens), 0), iota((tokens, tokens), 1)
    before = ones_where((early // tok_dev == late // tok_dev) & (early < late))
    position = contract(hit, before, 1, 0)
    slot = iota((rows, tokens), 0) % block - CAP * (iota((rows, tokens), 1) // tok_dev)
    fits = (hit > 0.5) & (slot >= 0) & (slot < CAP) & (position == slot.astype(F32))
    slots = ones_where(fits).astype(BF16)
    slots_ref[...] = slots
    saved = jnp.concatenate([x_ref[0, m] for m in range(n_micro)], axis=0)
    saved_ref[...] = contract(slots, saved, 1, 0).astype(BF16)
    for number, (at_row, lanes) in enumerate(field_places(n_fields, n_all, feat, n_micro * CAP)):
        spare = iota((rows, n_all), 0) % block == at_row
        field = jnp.broadcast_to(packed[number : number + 1, :], (rows, n_all))
        kept = saved_ref[:, lanes].astype(F32)
        saved_ref[:, lanes] = jnp.where(spare, field, kept).astype(BF16)
    top = jnp.concatenate([top_ref[m] for m in range(n_micro)], axis=0)
    used = jnp.where(section == n_section - 1, slots, jnp.zeros_like(slots))
    top_send_ref[...] = contract(used, top, 1, 0).astype(BF16)


def field_places(n_fields, n_all, feat, first_row):
    per_row = feat // n_all
    for number in range(n_fields):
        at = number % per_row * n_all
        yield first_row + number // per_row, slice(at, at + n_all)


def collect(block, used, n_fields, x_ref, fields_ref):
    n_all = fields_ref.shape[1]
    rows, feat = x_ref.shape
    total = jnp.zeros(fields_ref.shape, F32)
    for number, (at_row, lanes) in enumerate(field_places(n_fields, n_all, feat, used)):
        spare = iota((rows, n_all), 0) % block == at_row
        kept = jnp.where(spare, x_ref[:, lanes].astype(F32), 0.0)
        field = jnp.sum(kept, axis=0, keepdims=True)
        total = jnp.where(iota(fields_ref.shape, 0) == number, field, total)
    fields_ref[...] = total


def plan(
    n_section, n_expert, n_micro, tok_dev, top_k, block, share, q_dev, *refs
):
    around, refs = refs[:n_section], refs[n_section:]
    comp_ref, place_ref, cols_ref, sketch_ref, over_ref = refs
    n_all = around[0].shape[1]
    tokens = n_micro * tok_dev
    hsplit = n_expert // EXPERTS
    rows = n_expert * block
    section, me = lax.axis_index("section"), lax.axis_index("expert")
    mine, below, above = around[0][...], around[-1][...], around[1 % n_section][...]
    group = (me // hsplit).astype(F32)
    hit = names(mine, top_k, group)
    early, late = iota((n_all, n_all), 0), iota((n_all, n_all), 1)
    before = ones_where(early < late)
    near = ones_where((early // tok_dev == late // tok_dev) & (early < late))
    lane = iota((8, n_all), 1)
    count = contract(jnp.broadcast_to(hit, (8, n_all)), near, 1, 0)
    slot = (lane // tokens) * block + (lane // tok_dev) % n_micro * CAP
    slot = (slot.astype(F32) + count)[0:1, :]
    held = ones_where((iota((rows, n_all), 0).astype(F32) == slot) & (hit > 0.5))
    weight = jnp.zeros((1, n_all), F32)
    for k in range(top_k):
        weight = weight + jnp.where(
            mine[k : k + 1, :] == group, mine[top_k + k : top_k + k + 1, :], 0.0
        )
    first = ones_where((mine[0:1, :] == group) & (me % hsplit == 0))
    column = iota((rows, LANES), 1)
    weight_col = jnp.sum(held * weight, axis=1, keepdims=True)
    first_col = jnp.sum(held * first, axis=1, keepdims=True)
    cols_ref[...] = jnp.where(column == 0, weight_col, jnp.where(column == 1, first_col, 0.0))

    held_b = held.astype(BF16)
    peers = (partner(me, iota((n_expert, n_all), 0), n_expert) // hsplit).astype(F32)
    for other, to_row in ((below, True), (above, False)):
        both = names(other, top_k, peers) * hit
        position = contract(both, before, 1, 0)
        picks = []
        for turn in range(n_expert):
            chosen = position[turn : turn + 1, :] == iota((share, n_all), 0).astype(F32)
            picks.append(ones_where(chosen) * both[turn : turn + 1, :])
        picks = jnp.concatenate(picks, axis=0).astype(BF16)
        if to_row:
            comp_ref[...] = contract(picks, held_b, 1, 1).astype(BF16)
        else:
            place_ref[...] = contract(held_b, picks, 1, 1).astype(BF16)

    place = iota((rows, n_all), 0)
    target = (place // block) * q_dev
    local = me // hsplit
    inside = (local >= target % EXPERTS) & (local < target % EXPERTS + q_dev)
    example = mine[2 * top_k : 2 * top_k + 1, :]
    fits = inside & (example == (target // EXPERTS).astype(F32))
    for part_no in range(sketch_ref.shape[0]):
        at_row = place % block == n_micro * CAP + part_no
        terms = jnp.where(fits & at_row, weight, 0.0).astype(BF16)
        sketch_ref[part_no] = contract(terms, held_b, 1, 1).astype(BF16)

    expert = iota((EXPERTS, n_all), 0).astype(F32)
    most = jnp.zeros((1, 1), F32)
    upper = names(mine, top_k, expert)
    for turn in range(1, n_section + 1):
        lower, upper = upper, names(around[turn % n_section][...], top_k, expert)
        shared = jnp.max(contract(upper, lower, 1, 1), axis=(0, 1), keepdims=True)
        wraps = (section + turn) % n_section == 0
        most = jnp.maximum(most, jnp.where(wraps, 0.0, shared))
    over_ref[...] = jnp.broadcast_to(most, over_ref.shape)


def forward(
    x_ref, gate_hbm, up_hbm, down_hbm, left_hbm, right_hbm,
    to_gate_ref, to_up_ref, left_ref, gate_ref, up_ref, down_ref, left_map, right_map, sems,
):
    hidden = gate_ref.shape[1]
    tile = math.gcd(hidden, TILE)
    pairs = [(left_hbm, left_map)]
    for at in range(0, hidden, tile):
        part = pl.ds(at, tile)
        pairs.append((gate_hbm.at[:, part, :], gate_ref.at[:, part, :]))
        pairs.append((up_hbm.at[:, part, :], up_ref.at[:, part, :]))
    for at in range(0, hidden, tile):
        part = pl.ds(at, tile)
        pairs.append((down_hbm.at[:, part, :], down_ref.at[:, part, :]))
    pairs.append((right_hbm, right_map))
    copies = [pltpu.make_async_copy(a, b, sems.at[i]) for i, (a, b) in enumerate(pairs)]
    for copy in copies:
        copy.start()
    copies.pop(0).wait()
    left = jnp.zeros(left_ref.shape, F32)
    for at in range(0, hidden, tile):
        part = slice(at, at + tile)
        copies.pop(0).wait()
        gate = contract(x_ref[...], gate_ref[0, part, :], 1, 1)
        copies.pop(0).wait()
        up = contract(x_ref[...], up_ref[0, part, :], 1, 1)
        sigmoid = jax.nn.sigmoid(gate)
        silu = gate * sigmoid
        to_up_ref[:, part] = silu
        to_gate_ref[:, part] = up * sigmoid * (1.0 + gate * (1.0 - sigmoid))
        left = left + contract((silu * up).astype(BF16), left_map[0, :, part], 1, 1)
    left_ref[...] = left.astype(BF16)
    for copy in copies:
        copy.wait()


def layer(n_arrived, n_sent, n_before, stage, n_section, n_extra, *refs):
    refs = list(refs)
    take = lambda amount: [refs.pop(0) for _ in range(amount)]
    arrived = take(n_arrived)
    place = take(1)[0] if n_arrived > 1 else None
    to_gate, to_up, down, gate, up, cols = take(6)
    comp = take(1)[0] if n_sent else None
    rows_before, part_before = take(2) if n_before else (None, None)
    if not n_sent:
        left_ref, right_proj, sketch = take(3)
    sent = take(n_sent)
    part_ref, rows_ref = take(2) if n_sent else take(1) + [None]
    grad_gate, grad_up, rows_now = take(3)
    feat = rows_now.shape[1]
    live = lax.axis_index("section") == n_section - 1 - stage

    @pl.when(live)
    def _():
        if n_arrived > 1:
            pieces = jnp.concatenate([ref[...].astype(F32) for ref in arrived], axis=0)
            rows = contract(place[...], pieces.astype(BF16), 1, 0).astype(BF16)
        else:
            rows = arrived[0][...]
        rows_now[...] = rows
        tile = math.gcd(grad_gate.shape[1], TILE)
        for at in range(0, grad_gate.shape[1], tile):
            part = slice(at, at + tile)
            grad_hidden = contract(rows, down[0, part, :], 1, 1)
            grad_gate[:, part] = (grad_hidden * to_gate[:, part]).astype(BF16)
            grad_up[:, part] = (grad_hidden * to_up[:, part]).astype(BF16)
        weight, first = cols[:, 0:1], cols[:, 1:2]
        for at in range(0, feat, TILE):
            part = slice(at, at + TILE)
            total = contract(grad_gate[...], gate[0, :, part], 1, 0)
            total = total + contract(grad_up[...], up[0, :, part], 1, 0)
            total = total * weight + rows[:, part].astype(F32) * first
            total = total.astype(BF16)
            part_ref[:, part] = total
            if n_sent:
                chosen = contract(comp[...], total, 1, 0)
                share = chosen.shape[0] // n_sent
                for turn in range(n_sent):
                    sent[turn][:, part] = chosen[turn * share : (turn + 1) * share].astype(BF16)

    @pl.when(jnp.logical_not(live))
    def _():
        if n_before:
            rows_now[...] = rows_before[...]
            part_ref[...] = part_before[...]
        else:
            rows_now[...] = jnp.zeros(rows_now.shape, BF16)
            part_ref[...] = jnp.zeros(part_ref.shape, BF16)

    if n_sent:
        rows_ref[...] = rows_now[...]
        return
    right = contract(rows_now[...], right_proj[0], 1, 1)
    high = right.astype(BF16)
    low = (right - high.astype(F32)).astype(BF16)
    left = left_ref[...]
    size = left.shape[1]
    lane, axis = iota((size, TILE), 1), iota((size, TILE), 0)
    over_right = ones_where(axis == lane % size).astype(BF16)
    right = contract(high, over_right, 1, 0) + contract(low, over_right, 1, 0)
    for number in range(n_extra):
        for at in range(0, feat, TILE):
            part = slice(at, at + TILE)
            over_left = ones_where(axis == (number * feat + at + lane) // size).astype(BF16)
            outer = contract(left, over_left, 1, 0) * right
            terms = contract(sketch[number], outer.astype(BF16), 1, 0)
            part_ref[:, part] = (part_ref[:, part].astype(F32) + terms).astype(BF16)


def finish(n_expert, block, used, n_extra, q_dev, back_ref, slots_ref, grad_ref, sketch_ref):
    me = lax.axis_index("expert")
    hsplit = n_expert // EXPERTS
    n_micro, tok_dev, feat = grad_ref.shape[1:]
    rows = n_expert * block
    start = (me * q_dev) % EXPERTS
    group = iota((q_dev, rows), 1) // (block * hsplit)
    owner = group == start + iota((q_dev, rows), 0)
    back = back_ref[...]
    total = contract(slots_ref[...], back, 0, 0)
    for m in range(n_micro):
        grad_ref[0, m] = total[m * tok_dev : (m + 1) * tok_dev].astype(BF16)
    for number in range(n_extra):
        at_row = iota((q_dev, rows), 1) % block == used + number
        picks = ones_where(owner & at_row).astype(BF16)
        sketch_ref[0, :, number * feat : (number + 1) * feat] = contract(picks, back, 1, 0)


def send_down(blocks, section, n_expert):
    window = 5
    far, near = list(range(n_expert - 1, n_expert // 2 - 1, -1)), list(range(n_expert // 2))
    near[0:2] = near[1::-1]
    order = []
    while far or near:
        for some, amount in ((far, 1), (near, 1), (far, 1), (near, 1), (far, 2), (near, 2)):
            order += some[:amount]
            del some[:amount]
    freed = [3, 1, 0, 2, 4] + list(range(5, n_expert))
    arrived = [None] * n_expert
    for place, turn in enumerate(order):
        pairs = [
            (section * n_expert + e, (section - 1) * n_expert + partner(e, turn, n_expert))
            for e in range(n_expert)
        ]
        block = blocks[turn]
        if place >= window:
            earlier = order[freed[place - window]]
            block, arrived[earlier] = lax.optimization_barrier((block, arrived[earlier]))
        arrived[turn] = lax.ppermute(block, ("section", "expert"), pairs)
    return arrived


def by_owners(block, used, n_extra, q_dev, arrays, slots, x_rows, top_rows, cols, sketch):
    top_grad, gate_weight, up_weight, down_weight, left_proj, right_proj = arrays
    n_section, n_expert = lax.axis_size("section"), lax.axis_size("expert")
    section = lax.axis_index("section")
    n_micro, tok_dev, feat = top_grad.shape
    tokens = n_micro * tok_dev
    n_rows = n_expert * block

    def exchange(rows):
        blocks = rows.reshape(n_expert, block, feat)
        blocks = lax.all_to_all(blocks, "expert", split_axis=0, concat_axis=0, tiled=True)
        return blocks.reshape(n_rows, feat)

    gate, up, down = gate_weight[0], up_weight[0], down_weight[0]
    pre_gate = contract(x_rows, gate, 1, 1)
    pre_up = contract(x_rows, up, 1, 1)
    sigmoid = jax.nn.sigmoid(pre_gate)
    to_up = pre_gate * sigmoid
    to_gate = pre_up * sigmoid * (1.0 + pre_gate * (1.0 - sigmoid))
    left = contract((to_up * pre_up).astype(BF16), left_proj[0], 1, 0).astype(BF16)
    size = left.shape[1]
    rows = top_rows
    right = jnp.zeros((n_rows, size), F32)
    own = jnp.zeros((tokens, feat), BF16)
    for stage in range(n_section):
        live = section == n_section - 1 - stage
        if stage > 0:
            hop = [(n_section - stage, n_section - 1 - stage)]
            out_grad = lax.ppermute(new_grad, "section", hop)
            rows = exchange(contract(slots, out_grad, 1, 0).astype(BF16))
        grad_hidden = contract(rows, down, 1, 1)
        part = contract((grad_hidden * to_gate).astype(BF16), gate, 1, 0)
        part = part + contract((grad_hidden * to_up).astype(BF16), up, 1, 0)
        part = part * cols[:, 0:1] + rows.astype(F32) * cols[:, 1:2]
        right = right + jnp.where(live, contract(rows, right_proj[0], 1, 0), 0.0)
        back = exchange(part.astype(BF16))
        new_grad = contract(slots, back, 0, 0).astype(BF16)
        own = jnp.where(live, new_grad, own)
    outer = (left.astype(F32)[:, :, None] * right[:, None, :]).astype(BF16)
    outer = outer.reshape(n_rows, n_extra * feat)
    terms = jnp.zeros((n_rows, feat), F32)
    for number in range(n_extra):
        here = outer[:, number * feat : (number + 1) * feat]
        terms = terms + contract(sketch[number], here, 1, 0)
    back = exchange(terms.astype(BF16)).reshape(EXPERTS, n_expert // EXPERTS, block, feat)
    back = back[:, :, used : used + n_extra].astype(F32).sum(axis=1)
    back = back.reshape(EXPERTS, n_extra * feat)
    start = (lax.axis_index("expert") * q_dev) % EXPERTS
    found = lax.dynamic_slice_in_dim(back, start, q_dev, 0)
    return own.reshape(1, n_micro, tok_dev, feat), found[None]


def on_device(
    saved_inputs,
    top_grad,
    expert_ids,
    route_weights,
    example_ids,
    gate_weight,
    up_weight,
    down_weight,
    left_proj,
    right_proj,
):
    n_section = lax.axis_size("section")
    n_expert = lax.axis_size("expert")
    n_micro, tok_dev, feat = saved_inputs.shape[1:]
    top_k = expert_ids.shape[3]
    hidden = gate_weight.shape[1]
    tokens = n_micro * tok_dev
    sketch_dim = left_proj.shape[2]
    used = n_micro * CAP
    n_extra = sketch_dim * sketch_dim // feat
    block = -(-(used + n_extra) // 8) * 8
    n_rows = n_expert * block
    q_dev = n_micro * EXM * EXPERTS // n_expert
    share = -(-(n_expert * used // 2) // 8) * 8
    n_picks = n_expert * share

    def shape(*dims, dtype=BF16):
        return jax.ShapeDtypeStruct(dims, dtype)

    arrays = (
        expert_ids.transpose(0, 1, 3, 2),
        route_weights.transpose(0, 1, 3, 2),
        example_ids,
        saved_inputs,
        top_grad,
    )
    saved_send, top_send, slots = call(
        functools.partial(prepare, n_section, n_expert, block),
        (shape(n_rows, feat), shape(n_rows, feat), shape(n_rows, tokens)),
        arrays,
        HBM,
        [pltpu.VMEM(a.shape, a.dtype) for a in arrays] + [pltpu.SemaphoreType.DMA((5,))],
    )

    def exchange(rows):
        blocks = rows.reshape(n_expert, block, feat)
        blocks = lax.all_to_all(blocks, "expert", split_axis=0, concat_axis=0, tiled=True)
        return blocks.reshape(n_rows, feat)

    x_rows = exchange(saved_send)
    (fields,) = call(
        functools.partial(collect, block, used, 2 * top_k + 1),
        (shape(-(-(2 * top_k + 1) // 8) * 8, n_expert * tokens, dtype=F32),),
        (x_rows,),
    )
    around = [fields]
    for turn in range(1, n_section):
        pairs = [(i, (i - turn) % n_section) for i in range(n_section)]
        around.append(lax.ppermute(fields, "section", pairs))
    top_rows = exchange(top_send)
    kept = (
        gate_weight,
        up_weight,
        down_weight,
        left_proj.transpose(0, 2, 1),
        right_proj.transpose(0, 2, 1),
    )
    kept, top_rows = lax.optimization_barrier((kept, top_rows))
    to_gate, to_up, left, gate, up, down, left_map, right_map = pl.pallas_call(
        forward,
        out_shape=(
            shape(n_rows, hidden, dtype=F32),
            shape(n_rows, hidden, dtype=F32),
            shape(n_rows, sketch_dim),
        )
        + tuple(pltpu.VMEM(a.shape, a.dtype) for a in kept),
        in_specs=[VMEM] + [HBM] * len(kept),
        out_specs=(VMEM,) * (3 + len(kept)),
        scratch_shapes=[pltpu.SemaphoreType.DMA((2 + 3 * (hidden // math.gcd(hidden, TILE)),))],
        compiler_params=pltpu.CompilerParams(vmem_limit_bytes=40 << 20),
    )(x_rows, *kept)
    comp, place, cols, sketch, over = call(
        functools.partial(
            plan, n_section, n_expert, n_micro, tok_dev, top_k, block, share, q_dev
        ),
        (
            shape(n_picks, n_rows),
            shape(n_rows, n_picks),
            shape(n_rows, LANES, dtype=F32),
            shape(n_extra, n_rows, n_rows),
            shape(8, LANES, dtype=F32),
        ),
        around,
        limit=(12 << 20) + 16 * n_rows * n_picks,
    )

    raw = (top_grad, gate_weight, up_weight, down_weight, left_proj, right_proj)

    def crowded(*_):
        return by_owners(
            block, used, n_extra, q_dev, raw, slots, x_rows, top_rows, cols, sketch
        )

    if n_expert > MOST_PERMUTES:
        return crowded()

    rows, part = None, None
    arrived = [top_rows]
    for stage in range(n_section):
        last = stage == n_section - 1
        inputs = list(arrived)
        if stage > 0:
            inputs += [place]
        inputs += [to_gate, to_up, down, gate, up, cols]
        if last:
            inputs += [rows, part, left, right_map, sketch]
            out = (shape(n_rows, feat),)
        else:
            inputs += [comp] + ([rows, part] if stage > 0 else [])
            out = tuple(shape(share, feat) for _ in range(n_expert))
            out += (shape(n_rows, feat), shape(n_rows, feat))
        kernel = functools.partial(
            layer,
            len(arrived),
            0 if last else n_expert,
            stage > 0,
            stage,
            n_section,
            n_extra,
        )
        results = pl.pallas_call(
            kernel,
            out_shape=out,
            in_specs=[VMEM] * len(inputs),
            out_specs=tuple(VMEM for _ in out),
            scratch_shapes=[
                pltpu.VMEM((n_rows, hidden), BF16),
                pltpu.VMEM((n_rows, hidden), BF16),
                pltpu.VMEM((n_rows, feat), BF16),
            ],
            compiler_params=pltpu.CompilerParams(
                vmem_limit_bytes=(12 << 20) + 2 * size_of(out) + 2 * size_of(arrived)
            ),
        )(*inputs)
        if last:
            back = exchange(results[0])
            break
        part, rows = results[-2:]
        arrived = send_down(results[:n_expert], n_section - 1 - stage, n_expert)

    def direct(*_):
        return call(
            functools.partial(finish, n_expert, block, used, n_extra, q_dev),
            (
                shape(1, n_micro, tok_dev, feat),
                shape(1, q_dev, sketch_dim * sketch_dim, dtype=F32),
            ),
            (back, slots),
        )

    return lax.cond(over[0, 0] > share, crowded, direct)


def solution(mesh):
    placed = (
        P("section", None, "expert", None),
        P(None, "expert", None),
        P("section", None, "expert", None),
        P("section", None, "expert", None),
        P(None, "expert"),
        P("section", "expert", None),
        P("section", "expert", None),
        P("section", "expert", None),
        P("section", "expert", None),
        P("section", None, None),
    )
    return jax.shard_map(
        on_device,
        mesh=mesh,
        in_specs=placed,
        out_specs=(P("section", None, "expert", None), P("section", "expert", None)),
        check_vma=False,
    )
```

time: 333 us -> 154 us (0.46); the launches traced: 330 us -> 155 us
  waiting for transfers between devices: 148 us -> 62.2 us
  starting transfers between devices: 70.1 us -> 31.6 us
  matrix products: 37.1 us -> 0 us
  Pallas kernels: 0 us -> 36.7 us
  other arithmetic: 27.1 us -> 0 us
  local copies, waits for them, and re-layouts: 33.3 us -> 6.24 us
  blocking collectives: 0 us -> 16 us
  between operations: 14.2 us -> 1.93 us
    all_to_all x17 -> x2, waiting for transfers between devices: 74.9 us -> 12.5 us  [exchange(): lax.all_to_all(blocks, 'expert', split_axis=0, concat_axis=0, tiled=True)]
    reduce_scatter x1 -> x0, waiting for transfers between devices: 60.4 us -> none  [on_device(): lax.psum_scatter(final_state[2], 'expert', scatter_dimension=0, tiled=True)]
    all_to_all x17 -> x2, starting transfers between devices: 63.6 us -> 7.46 us  [exchange(): lax.all_to_all(blocks, 'expert', split_axis=0, concat_axis=0, tiled=True)]
    ppermute x5 -> x27, waiting for transfers between devices: 12.5 us -> 49.7 us  [the longest x24 49.7 us: send_down(): arrived[turn] = lax.ppermute(block, ('section', 'expert'), pairs)]
    dot_general x36 -> x0, matrix products: 37.1 us -> none  [the longest x2 9.34 us: backward(): jnp.einsum('rd,hd->rh', grad_in, w_down, preferred_element_type=jnp.float32)]
    pallas_call x0 -> x9, Pallas kernels: none -> 36.7 us  [the longest x4 23.3 us: on_device(): pl.pallas_call(kernel, out_shape=out, in_specs=[VMEM] * len(inputs), out_...]
    ppermute x5 -> x27, starting transfers between devices: 6.46 us -> 24.1 us  [the longest x24 21.1 us: send_down(): arrived[turn] = lax.ppermute(block, ('section', 'expert'), pairs)]
    all_to_all x0 -> x1, blocking collectives: none -> 16 us  [exchange(): lax.all_to_all(blocks, 'expert', split_axis=0, concat_axis=0, tiled=True)]
  transfers between devices with their start and end apart: 23 -> 29, of which waited for: 19 -> 8; matrix products, arithmetic and copies ran while one was open for 14% -> 0% of each run, Pallas kernels for 0% -> 7%
where the time goes in v2:
time: 154 us; the launch traced here: 155 us
  waiting for transfers between devices  62.2 us (40%)
  Pallas kernels  36.7 us (24%)
  starting transfers between devices  31.6 us (21%)
  blocking collectives  16 us (10%)
  local copies, waits for them, and re-layouts  6.24 us (4%)
  between operations  1.93 us (1%)
    ppermute x24, waiting for transfers between devices, send_down(): arrived[turn] = lax.ppermute(block, ('section', 'expert'), pairs)  49.7 us
    pallas_call x4, Pallas kernels, on_device(): pl.pallas_call(kernel, out_shape=out, in_specs=[VMEM] * len(inputs), out_...  23.3 us
    ppermute x24, starting transfers between devices, send_down(): arrived[turn] = lax.ppermute(block, ('section', 'expert'), pairs)  21.1 us
    all_to_all x1, blocking collectives, exchange(): lax.all_to_all(blocks, 'expert', split_axis=0, concat_axis=0, tiled=True)  16 us
    all_to_all x2, waiting for transfers between devices, exchange(): lax.all_to_all(blocks, 'expert', split_axis=0, concat_axis=0, tiled=True)  12.5 us
    pallas_call x1, Pallas kernels, on_device(): pl.pallas_call(forward, out_shape=(shape(n_rows, hidden, dtype=F32), shap...  10.7 us
    all_to_all x2, starting transfers between devices, exchange(): lax.all_to_all(blocks, 'expert', split_axis=0, concat_axis=0, tiled=True)  7.46 us
    unnamed x26, local copies, waits for them, and re-layouts  5.73 us
  transfers between devices with their start and end apart: 29, of which 8 were waited for; matrix products, arithmetic and copies ran while one was open for 0% of the time, Pallas kernels for 7%

profile of v2, /device:TPU:0, one launch (start us, length us, event | category | flops | bytes accessed | tf_op | source)
XLA Modules:
  0.0 154.7 jit_solution(17345350785194622319)
XLA Ops:
  0.6 0.8 copy-done.4
  1.5 0.8 copy-done.5
  2.3 0.7 copy-done.7
  3.0 0.7 copy-done.8
  3.7 0.7 copy-done.9
  4.4 1.4 shard_map.117
  5.8 16.0 %all_to_all.51 = bf16[8,8,2048]{2,1,0:T(8,128)(2,1)S(1)} all-to-all(bf16[8,8,2048]{2,1,0:T(8,128)(2,1)S(1)} %bitcast.196), channel_id=1, replica_groups=mesh['section'=4,'expert'=8] {'expert'}, dimensions={0} | all-to-all | bytes 524288 | tf_op jit(solution)/shard_map/all_to_all | solution.py:458
  21.8 3.6 %all-to-all-start.9 = ((bf16[8,8,2048]{2,1,0:T(8,128)(2,1)}), bf16[8,8,2048]{2,1,0:T(8,128)(2,1)S(1)}, u32[]{:S(2)}, u32[]{:S(2)}) async-start(bf16[8,8,2048]{2,1,0:T(8,128)(2,1)} %bitcast.42), calls=%async_computation.9 | async-start | bytes 524288 | tf_op jit(solution)/shard_map/all_to_all | solution.py:458
  25.4 0.1 collective-permute-start.5
  25.4 1.6 %collective-permute-start.4 = (f32[8,128]{1,0:T(8,128)S(1)}, f32[8,128]{1,0:T(8,128)S(1)}, u32[]{:S(2)}, u32[]{:S(2)}) collective-permute-start(f32[8,128]{1,0:T(8,128)S(1)} %shard_map.118.refs_0_), channel_id=1, source_target_pairs={{0,16},{8,24},{16,0},{24,8},{1,17},{9,25},{17,1},{25,9},{2,18},{10... | collective-permute-start | bytes 12296 | tf_op jit(solution)/shard_map/ppermute | solution.py:470
  27.0 1.4 collective-permute-start.3
  28.4 5.5 %all-to-all-done.9 = bf16[8,8,2048]{2,1,0:T(8,128)(2,1)S(1)} async-done(((bf16[8,8,2048]{2,1,0:T(8,128)(2,1)}), bf16[8,8,2048]{2,1,0:T(8,128)(2,1)S(1)}, u32[]{:S(2)}, u32[]{:S(2)}) %all-to-all-start.9) | async-done | bytes 262176 | tf_op jit(solution)/shard_map/all_to_all | solution.py:458
  33.9 10.7 %shard_map.120 = (f32[64,1536]{1,0:T(8,128)}, f32[64,1536]{1,0:T(8,128)}, bf16[64,64]{1,0:T(8,128)(2,1)}, bf16[1,1536,2048]{2,1,0:T(8,128)(2,1)S(1)}, bf16[1,153...) custom-call(bf16[64,2048]{1,0:T(8,128)(2,1)S(1)} %bitcast.209, ...), custom_call_target="tpu_custom_call" | custom-call | tf_op jit(solution)/shard_map/pallas_call | solution.py:480
  44.6 0.0 collective-permute-done.3.refs_1_
  44.6 0.4 shard_map.119
  45.1 1.0 copy-done
  46.1 1.0 copy-done.2
  47.1 0.1 shard_map.121
  47.1 0.8 collective-permute-start.6
  47.9 0.7 collective-permute-start.7
  48.6 0.7 collective-permute-start.9
  49.3 0.7 collective-permute-start.12
  50.0 0.7 collective-permute-start.13
  50.6 0.7 collective-permute-start.11
  51.3 0.0 collective-permute-done.7.refs_1_
  51.3 0.7 collective-permute-start.8
  52.0 0.0 collective-permute-done.9.refs_7_
  52.0 0.7 collective-permute-start.10
  52.7 0.0 collective-permute-done.12.refs_5_
  52.7 0.0 collective-permute-done.11.refs_4_
  52.7 0.0 collective-permute-done.8.refs_2_
  52.8 0.3 shard_map.122
  53.1 0.7 collective-permute-start.14
  53.8 0.7 collective-permute-start.15
  54.5 0.7 collective-permute-start.17
  55.1 0.7 collective-permute-start.20
  55.8 0.7 collective-permute-start.21
  56.5 0.0 collective-permute-done.14.refs_0_
  56.5 0.7 collective-permute-start.19
  57.2 0.7 collective-permute-start.16
  57.9 0.7 collective-permute-start.18
  58.6 0.0 collective-permute-done.21.refs_6_
  58.6 0.0 copy-start.6
  58.6 0.1 shard_map.123
  58.7 1.3 collective-permute-start.22
  60.0 1.3 collective-permute-start.23
  61.3 1.3 collective-permute-start.25
  62.6 1.3 collective-permute-start.28
  63.9 1.3 collective-permute-start.29
  65.2 36.9 %collective-permute-done.22.refs_0_ = bf16[24,2048]{1,0:T(8,128)(2,1)S(1)} collective-permute-done((bf16[24,2048]{1,0:T(8,128)(2,1)S(1)}, bf16[24,2048]{1,0:T(8,128)(2,1)S(1)}, u32[]{:S(2)}, u32[]{:S(2)}) %collective-permute-start.22) | collective-permute-done | bytes 98336 | tf_op jit(solution)/shard_map/ppermute | solution.py:355
  102.1 1.3 collective-permute-start.27
  103.4 2.5 %collective-permute-done.23.refs_1_ = bf16[24,2048]{1,0:T(8,128)(2,1)S(1)} collective-permute-done((bf16[24,2048]{1,0:T(8,128)(2,1)S(1)}, bf16[24,2048]{1,0:T(8,128)(2,1)S(1)}, u32[]{:S(2)}, u32[]{:S(2)}) %collective-permute-start.23) | collective-permute-done | bytes 98336 | tf_op jit(solution)/shard_map/ppermute | solution.py:355
  105.8 1.3 collective-permute-start.24
  107.1 1.0 collective-permute-done.25.refs_7_
  108.1 1.3 collective-permute-start.26
  109.4 2.4 %collective-permute-done.28.refs_5_ = bf16[24,2048]{1,0:T(8,128)(2,1)S(1)} collective-permute-done((bf16[24,2048]{1,0:T(8,128)(2,1)S(1)}, bf16[24,2048]{1,0:T(8,128)(2,1)S(1)}, u32[]{:S(2)}, u32[]{:S(2)}) %collective-permute-start.28) | collective-permute-done | bytes 98336 | tf_op jit(solution)/shard_map/ppermute | solution.py:355
  111.8 3.0 %collective-permute-done.27.refs_4_ = bf16[24,2048]{1,0:T(8,128)(2,1)S(1)} collective-permute-done((bf16[24,2048]{1,0:T(8,128)(2,1)S(1)}, bf16[24,2048]{1,0:T(8,128)(2,1)S(1)}, u32[]{:S(2)}, u32[]{:S(2)}) %collective-permute-start.27) | collective-permute-done | bytes 98336 | tf_op jit(solution)/shard_map/ppermute | solution.py:355
  114.8 3.9 %collective-permute-done.26.refs_3_ = bf16[24,2048]{1,0:T(8,128)(2,1)S(1)} collective-permute-done((bf16[24,2048]{1,0:T(8,128)(2,1)S(1)}, bf16[24,2048]{1,0:T(8,128)(2,1)S(1)}, u32[]{:S(2)}, u32[]{:S(2)}) %collective-permute-start.26) | collective-permute-done | bytes 98336 | tf_op jit(solution)/shard_map/ppermute | solution.py:355
  118.7 22.8 %shard_map.124 = bf16[64,2048]{1,0:T(8,128)(2,1)} custom-call(bf16[24,2048]{1,0:T(8,128)(2,1)S(1)} %collective-permute-done.22.refs_0_, bf16[24,2048]{1,0:T(8,128)(2,1)S(1)} %collective-permute-done.23.refs_1_, bf16[24,2048]{1,0:T(8,128)(2,1)S(1)} %collective-permute-done.24.refs_2_, bf16[24,2048]{1,0:T(8,128)(2,1)S(1)} %collective-permute-done.26.refs_3_, ...), custom_call_target="tpu_custom_call" | custom-call | tf_op jit(solution)/shard_map/pallas_call | solution.py:542
  141.5 3.9 %all-to-all-start.10 = ((bf16[8,8,2048]{2,1,0:T(8,128)(2,1)}), bf16[8,8,2048]{2,1,0:T(8,128)(2,1)S(1)}, u32[]{:S(2)}, u32[]{:S(2)}) async-start(bf16[8,8,2048]{2,1,0:T(8,128)(2,1)} %bitcast.44), calls=%async_computation.10 | async-start | bytes 524288 | tf_op jit(solution)/shard_map/all_to_all | solution.py:458
  145.4 0.5 slice.30
  146.5 7.1 %all-to-all-done.10 = bf16[8,8,2048]{2,1,0:T(8,128)(2,1)S(1)} async-done(((bf16[8,8,2048]{2,1,0:T(8,128)(2,1)}), bf16[8,8,2048]{2,1,0:T(8,128)(2,1)S(1)}, u32[]{:S(2)}, u32[]{:S(2)}) %all-to-all-start.10) | async-done | bytes 262176 | tf_op jit(solution)/shard_map/all_to_all | solution.py:458
  153.6 0.9 conditional.1
  153.6 0.9 branch_0_fun.1
  (32 shorter events, 0.1 us)
Async XLA Ops:
  0.6 0.8 copy-start.4
  1.5 0.8 copy-start.5
  2.3 0.7 copy-start.7
  3.0 0.7 copy-start.8
  3.7 0.7 copy-start.9
  21.8 12.2 %all-to-all-start.9 = ((bf16[8,8,2048]{2,1,0:T(8,128)(2,1)}), bf16[8,8,2048]{2,1,0:T(8,128)(2,1)S(1)}, u32[]{:S(2)}, u32[]{:S(2)}) async-start(bf16[8,8,2048]{2,1,0:T(8,128)(2,1)} %bitcast.42), calls=%async_computation.9 | async-start | bytes 524288 | tf_op jit(solution)/shard_map/all_to_all | solution.py:458
  25.4 19.2 %collective-permute-start.5 = (f32[8,128]{1,0:T(8,128)S(1)}, f32[8,128]{1,0:T(8,128)S(1)}, u32[]{:S(2)}, u32[]{:S(2)}) collective-permute-start(f32[8,128]{1,0:T(8,128)S(1)} %shard_map.118.refs_0_), channel_id=1, source_target_pairs={{0,8},{8,16},{16,24},{24,0},{1,9},{9,17},{17,25},{25,1},{2,10},{10... | collective-permute-start | bytes 12296 | tf_op jit(solution)/shard_map/ppermute | solution.py:470
  25.4 19.2 %collective-permute-start.4 = (f32[8,128]{1,0:T(8,128)S(1)}, f32[8,128]{1,0:T(8,128)S(1)}, u32[]{:S(2)}, u32[]{:S(2)}) collective-permute-start(f32[8,128]{1,0:T(8,128)S(1)} %shard_map.118.refs_0_), channel_id=1, source_target_pairs={{0,16},{8,24},{16,0},{24,8},{1,17},{9,25},{17,1},{25,9},{2,18},{10... | collective-permute-start | bytes 12296 | tf_op jit(solution)/shard_map/ppermute | solution.py:470
  27.0 17.6 %collective-permute-start.3 = (f32[8,128]{1,0:T(8,128)S(1)}, f32[8,128]{1,0:T(8,128)S(1)}, u32[]{:S(2)}, u32[]{:S(2)}) collective-permute-start(f32[8,128]{1,0:T(8,128)S(1)} %shard_map.118.refs_0_), channel_id=1, source_target_pairs={{0,24},{8,0},{16,8},{24,16},{1,25},{9,1},{17,9},{25,17},{2,26},{10... | collective-permute-start | bytes 12296 | tf_op jit(solution)/shard_map/ppermute | solution.py:470
  45.1 73.7 %copy-start.14 = (bf16[2,64,64]{2,1,0:T(8,128)(2,1)}, bf16[2,64,64]{2,1,0:T(8,128)(2,1)S(1)}, u32[]{:S(2)}) copy-start(bf16[2,64,64]{2,1,0:T(8,128)(2,1)S(1)} %get-tuple-element.175.refs_19_) | copy-start | bytes 49156
  45.1 1.0 copy-start
  46.1 1.0 copy-start.2
  47.1 5.7 %copy-start.1 = (f32[64,1536]{1,0:T(8,128)S(1)}, f32[64,1536]{1,0:T(8,128)}, u32[]{:S(2)}) copy-start(f32[64,1536]{1,0:T(8,128)} %get-tuple-element.117.refs_1_.refs_9_) | copy-start | bytes 1179652
  47.1 5.7 %copy-start.3 = (f32[64,1536]{1,0:T(8,128)S(1)}, f32[64,1536]{1,0:T(8,128)}, u32[]{:S(2)}) copy-start(f32[64,1536]{1,0:T(8,128)} %get-tuple-element.118.refs_2_.refs_10_) | copy-start | bytes 1179652
  47.1 3.5 %collective-permute-start.6 = (bf16[24,2048]{1,0:T(8,128)(2,1)S(1)}, bf16[24,2048]{1,0:T(8,128)(2,1)S(1)}, u32[]{:S(2)}, u32[]{:S(2)}) collective-permute-start(bf16[24,2048]{1,0:T(8,128)(2,1)S(1)} %get-tuple-element.125), channel_id=1, source_target_pairs={{24,16},{25,17},{26,18},{27,19},{28,20},{29,21},{30,22},{31,23}} | collective-permute-start | bytes 294920 | tf_op jit(solution)/shard_map/ppermute | solution.py:355
  47.9 3.4 %collective-permute-start.7 = (bf16[24,2048]{1,0:T(8,128)(2,1)S(1)}, bf16[24,2048]{1,0:T(8,128)(2,1)S(1)}, u32[]{:S(2)}, u32[]{:S(2)}) collective-permute-start(bf16[24,2048]{1,0:T(8,128)(2,1)S(1)} %get-tuple-element.128), channel_id=1, source_target_pairs={{24,17},{25,16},{26,19},{27,18},{28,21},{29,20},{30,23},{31,22}} | collective-permute-start | bytes 294920 | tf_op jit(solution)/shard_map/ppermute | solution.py:355
  48.6 3.4 %collective-permute-start.9 = (bf16[24,2048]{1,0:T(8,128)(2,1)S(1)}, bf16[24,2048]{1,0:T(8,128)(2,1)S(1)}, u32[]{:S(2)}, u32[]{:S(2)}) collective-permute-start(bf16[24,2048]{1,0:T(8,128)(2,1)S(1)} %get-tuple-element.132), channel_id=1, source_target_pairs={{24,23},{25,22},{26,21},{27,20},{28,19},{29,18},{30,17},{31,16}} | collective-permute-start | bytes 294920 | tf_op jit(solution)/shard_map/ppermute | solution.py:355
  49.3 3.4 %collective-permute-start.12 = (bf16[24,2048]{1,0:T(8,128)(2,1)S(1)}, bf16[24,2048]{1,0:T(8,128)(2,1)S(1)}, u32[]{:S(2)}, u32[]{:S(2)}) collective-permute-start(bf16[24,2048]{1,0:T(8,128)(2,1)S(1)} %get-tuple-element.135), channel_id=1, source_target_pairs={{24,21},{25,20},{26,23},{27,22},{28,17},{29,16},{30,19},{31,18}} | collective-permute-start | bytes 294920 | tf_op jit(solution)/shard_map/ppermute | solution.py:355
  50.0 2.7 %collective-permute-start.13 = (bf16[24,2048]{1,0:T(8,128)(2,1)S(1)}, bf16[24,2048]{1,0:T(8,128)(2,1)S(1)}, u32[]{:S(2)}, u32[]{:S(2)}) collective-permute-start(bf16[24,2048]{1,0:T(8,128)(2,1)S(1)} %get-tuple-element.136), channel_id=1, source_target_pairs={{24,22},{25,23},{26,20},{27,21},{28,18},{29,19},{30,16},{31,17}} | collective-permute-start | bytes 294920 | tf_op jit(solution)/shard_map/ppermute | solution.py:355
  50.6 2.1 %collective-permute-start.11 = (bf16[24,2048]{1,0:T(8,128)(2,1)S(1)}, bf16[24,2048]{1,0:T(8,128)(2,1)S(1)}, u32[]{:S(2)}, u32[]{:S(2)}) collective-permute-start(bf16[24,2048]{1,0:T(8,128)(2,1)S(1)} %get-tuple-element.134), channel_id=1, source_target_pairs={{24,20},{25,21},{26,22},{27,23},{28,16},{29,17},{30,18},{31,19}} | collective-permute-start | bytes 294920 | tf_op jit(solution)/shard_map/ppermute | solution.py:355
  51.3 1.4 collective-permute-start.8
  52.0 0.7 collective-permute-start.10
  53.1 3.4 %collective-permute-start.14 = (bf16[24,2048]{1,0:T(8,128)(2,1)S(1)}, bf16[24,2048]{1,0:T(8,128)(2,1)S(1)}, u32[]{:S(2)}, u32[]{:S(2)}) collective-permute-start(bf16[24,2048]{1,0:T(8,128)(2,1)S(1)} %get-tuple-element.142), channel_id=1, source_target_pairs={{16,8},{17,9},{18,10},{19,11},{20,12},{21,13},{22,14},{23,15}} | collective-permute-start | bytes 294920 | tf_op jit(solution)/shard_map/ppermute | solution.py:355
  53.8 3.4 %collective-permute-start.15 = (bf16[24,2048]{1,0:T(8,128)(2,1)S(1)}, bf16[24,2048]{1,0:T(8,128)(2,1)S(1)}, u32[]{:S(2)}, u32[]{:S(2)}) collective-permute-start(bf16[24,2048]{1,0:T(8,128)(2,1)S(1)} %get-tuple-element.145), channel_id=1, source_target_pairs={{16,9},{17,8},{18,11},{19,10},{20,13},{21,12},{22,15},{23,14}} | collective-permute-start | bytes 294920 | tf_op jit(solution)/shard_map/ppermute | solution.py:355
  54.5 3.4 %collective-permute-start.17 = (bf16[24,2048]{1,0:T(8,128)(2,1)S(1)}, bf16[24,2048]{1,0:T(8,128)(2,1)S(1)}, u32[]{:S(2)}, u32[]{:S(2)}) collective-permute-start(bf16[24,2048]{1,0:T(8,128)(2,1)S(1)} %get-tuple-element.149), channel_id=1, source_target_pairs={{16,15},{17,14},{18,13},{19,12},{20,11},{21,10},{22,9},{23,8}} | collective-permute-start | bytes 294920 | tf_op jit(solution)/shard_map/ppermute | solution.py:355
  55.1 3.4 %collective-permute-start.20 = (bf16[24,2048]{1,0:T(8,128)(2,1)S(1)}, bf16[24,2048]{1,0:T(8,128)(2,1)S(1)}, u32[]{:S(2)}, u32[]{:S(2)}) collective-permute-start(bf16[24,2048]{1,0:T(8,128)(2,1)S(1)} %get-tuple-element.152), channel_id=1, source_target_pairs={{16,13},{17,12},{18,15},{19,14},{20,9},{21,8},{22,11},{23,10}} | collective-permute-start | bytes 294920 | tf_op jit(solution)/shard_map/ppermute | solution.py:355
  55.8 2.7 %collective-permute-start.21 = (bf16[24,2048]{1,0:T(8,128)(2,1)S(1)}, bf16[24,2048]{1,0:T(8,128)(2,1)S(1)}, u32[]{:S(2)}, u32[]{:S(2)}) collective-permute-start(bf16[24,2048]{1,0:T(8,128)(2,1)S(1)} %get-tuple-element.153), channel_id=1, source_target_pairs={{16,14},{17,15},{18,12},{19,13},{20,10},{21,11},{22,8},{23,9}} | collective-permute-start | bytes 294920 | tf_op jit(solution)/shard_map/ppermute | solution.py:355
  56.5 2.1 %collective-permute-start.19 = (bf16[24,2048]{1,0:T(8,128)(2,1)S(1)}, bf16[24,2048]{1,0:T(8,128)(2,1)S(1)}, u32[]{:S(2)}, u32[]{:S(2)}) collective-permute-start(bf16[24,2048]{1,0:T(8,128)(2,1)S(1)} %get-tuple-element.151), channel_id=1, source_target_pairs={{16,12},{17,13},{18,14},{19,15},{20,8},{21,9},{22,10},{23,11}} | collective-permute-start | bytes 294920 | tf_op jit(solution)/shard_map/ppermute | solution.py:355
  57.2 1.4 collective-permute-start.16
  57.9 0.7 collective-permute-start.18
  58.6 60.1 %copy-start.6 = (bf16[64,64]{1,0:T(8,128)(2,1)S(1)}, bf16[64,64]{1,0:T(8,128)(2,1)}, u32[]{:S(2)}) copy-start(bf16[64,64]{1,0:T(8,128)(2,1)} %get-tuple-element.173.refs_17_) | copy-start | bytes 24580
  58.7 43.4 %collective-permute-start.22 = (bf16[24,2048]{1,0:T(8,128)(2,1)S(1)}, bf16[24,2048]{1,0:T(8,128)(2,1)S(1)}, u32[]{:S(2)}, u32[]{:S(2)}) collective-permute-start(bf16[24,2048]{1,0:T(8,128)(2,1)S(1)} %get-tuple-element.158), channel_id=1, source_target_pairs={{8,0},{9,1},{10,2},{11,3},{12,4},{13,5},{14,6},{15,7}} | collective-permute-start | bytes 294920 | tf_op jit(solution)/shard_map/ppermute | solution.py:355
  60.0 45.8 %collective-permute-start.23 = (bf16[24,2048]{1,0:T(8,128)(2,1)S(1)}, bf16[24,2048]{1,0:T(8,128)(2,1)S(1)}, u32[]{:S(2)}, u32[]{:S(2)}) collective-permute-start(bf16[24,2048]{1,0:T(8,128)(2,1)S(1)} %get-tuple-element.161), channel_id=1, source_target_pairs={{8,1},{9,0},{10,3},{11,2},{12,5},{13,4},{14,7},{15,6}} | collective-permute-start | bytes 294920 | tf_op jit(solution)/shard_map/ppermute | solution.py:355
  61.3 46.8 %collective-permute-start.25 = (bf16[24,2048]{1,0:T(8,128)(2,1)S(1)}, bf16[24,2048]{1,0:T(8,128)(2,1)S(1)}, u32[]{:S(2)}, u32[]{:S(2)}) collective-permute-start(bf16[24,2048]{1,0:T(8,128)(2,1)S(1)} %get-tuple-element.165), channel_id=1, source_target_pairs={{8,7},{9,6},{10,5},{11,4},{12,3},{13,2},{14,1},{15,0}} | collective-permute-start | bytes 294920 | tf_op jit(solution)/shard_map/ppermute | solution.py:355
  62.6 49.2 %collective-permute-start.28 = (bf16[24,2048]{1,0:T(8,128)(2,1)S(1)}, bf16[24,2048]{1,0:T(8,128)(2,1)S(1)}, u32[]{:S(2)}, u32[]{:S(2)}) collective-permute-start(bf16[24,2048]{1,0:T(8,128)(2,1)S(1)} %get-tuple-element.168), channel_id=1, source_target_pairs={{8,5},{9,4},{10,7},{11,6},{12,1},{13,0},{14,3},{15,2}} | collective-permute-start | bytes 294920 | tf_op jit(solution)/shard_map/ppermute | solution.py:355
  63.9 47.9 %collective-permute-start.29 = (bf16[24,2048]{1,0:T(8,128)(2,1)S(1)}, bf16[24,2048]{1,0:T(8,128)(2,1)S(1)}, u32[]{:S(2)}, u32[]{:S(2)}) collective-permute-start(bf16[24,2048]{1,0:T(8,128)(2,1)S(1)} %get-tuple-element.169), channel_id=1, source_target_pairs={{8,6},{9,7},{10,4},{11,5},{12,2},{13,3},{14,0},{15,1}} | collective-permute-start | bytes 294920 | tf_op jit(solution)/shard_map/ppermute | solution.py:355
  102.1 12.7 %collective-permute-start.27 = (bf16[24,2048]{1,0:T(8,128)(2,1)S(1)}, bf16[24,2048]{1,0:T(8,128)(2,1)S(1)}, u32[]{:S(2)}, u32[]{:S(2)}) collective-permute-start(bf16[24,2048]{1,0:T(8,128)(2,1)S(1)} %get-tuple-element.167), channel_id=1, source_target_pairs={{8,4},{9,5},{10,6},{11,7},{12,0},{13,1},{14,2},{15,3}} | collective-permute-start | bytes 294920 | tf_op jit(solution)/shard_map/ppermute | solution.py:355
  105.8 8.9 %collective-permute-start.24 = (bf16[24,2048]{1,0:T(8,128)(2,1)S(1)}, bf16[24,2048]{1,0:T(8,128)(2,1)S(1)}, u32[]{:S(2)}, u32[]{:S(2)}) collective-permute-start(bf16[24,2048]{1,0:T(8,128)(2,1)S(1)} %get-tuple-element.163), channel_id=1, source_target_pairs={{8,2},{9,3},{10,0},{11,1},{12,6},{13,7},{14,4},{15,5}} | collective-permute-start | bytes 294920 | tf_op jit(solution)/shard_map/ppermute | solution.py:355
  108.1 10.6 %collective-permute-start.26 = (bf16[24,2048]{1,0:T(8,128)(2,1)S(1)}, bf16[24,2048]{1,0:T(8,128)(2,1)S(1)}, u32[]{:S(2)}, u32[]{:S(2)}) collective-permute-start(bf16[24,2048]{1,0:T(8,128)(2,1)S(1)} %get-tuple-element.166), channel_id=1, source_target_pairs={{8,3},{9,2},{10,1},{11,0},{12,7},{13,6},{14,5},{15,4}} | collective-permute-start | bytes 294920 | tf_op jit(solution)/shard_map/ppermute | solution.py:355
  118.7 34.9 %copy-start.10 = (bf16[1,2048,64]{1,2,0:T(8,128)(2,1)S(1)}, bf16[1,2048,64]{1,2,0:T(8,128)(2,1)}, u32[]{:S(2)}) copy-start(bf16[1,2048,64]{1,2,0:T(8,128)(2,1)} %param.21) | copy-start | bytes 786436
  118.7 34.9 %copy-start.13 = (bf16[1,1536,64]{1,2,0:T(8,128)(2,1)S(1)}, bf16[1,1536,64]{1,2,0:T(8,128)(2,1)}, u32[]{:S(2)}) copy-start(bf16[1,1536,64]{1,2,0:T(8,128)(2,1)} %param.20) | copy-start | bytes 589828
  141.5 12.1 %all-to-all-start.10 = ((bf16[8,8,2048]{2,1,0:T(8,128)(2,1)}), bf16[8,8,2048]{2,1,0:T(8,128)(2,1)S(1)}, u32[]{:S(2)}, u32[]{:S(2)}) async-start(bf16[8,8,2048]{2,1,0:T(8,128)(2,1)} %bitcast.44), calls=%async_computation.10 | async-start | bytes 524288 | tf_op jit(solution)/shard_map/all_to_all | solution.py:458

commit v3 on v2

--- a/solution.py
+++ b/solution.py
@@ -14,6 +14,10 @@
 LANES = 128
 TILE = 256
 MOST_PERMUTES = 8
+NARROW = (1536, 1)
+WIDEN = (2048, 1)
+FORWARD = 512
+HALVES = 2
 
 F32 = jnp.float32
 BF16 = jnp.bfloat16
@@ -41,6 +45,19 @@
 
 def size_of(arrays):
     return sum(a.dtype.itemsize * a.size for a in arrays)
+
+
+def over_tiles(size, shape, body, start=0):
+    tile, together = math.gcd(size, shape[0]), shape[1]
+
+    def step(number, carry):
+        body(pl.ds(pl.multiple_of(start + number * tile, tile), tile))
+        return carry
+
+    if size == tile:
+        body(pl.ds(start, tile))
+        return
+    lax.fori_loop(0, size // tile, step, 0, unroll=math.gcd(size // tile, together))
 
 
 def call(kernel, out_shape, inputs, spec=VMEM, scratch=(), limit=12 << 20):
@@ -206,30 +223,28 @@
 
 
 def forward(
-    x_ref, gate_hbm, up_hbm, down_hbm, left_hbm, right_hbm,
-    to_gate_ref, to_up_ref, left_ref, gate_ref, up_ref, down_ref, left_map, right_map, sems,
+    x_ref, gate_hbm, up_hbm, left_hbm, to_gate_ref, to_up_ref, left_ref, gate_ref, up_ref, left_map, sems
 ):
-    hidden = gate_ref.shape[1]
-    tile = math.gcd(hidden, TILE)
-    pairs = [(left_hbm, left_map)]
-    for at in range(0, hidden, tile):
-        part = pl.ds(at, tile)
-        pairs.append((gate_hbm.at[:, part, :], gate_ref.at[:, part, :]))
-        pairs.append((up_hbm.at[:, part, :], up_ref.at[:, part, :]))
-    for at in range(0, hidden, tile):
-        part = pl.ds(at, tile)
-        pairs.append((down_hbm.at[:, part, :], down_ref.at[:, part, :]))
-    pairs.append((right_hbm, right_map))
-    copies = [pltpu.make_async_copy(a, b, sems.at[i]) for i, (a, b) in enumerate(pairs)]
-    for copy in copies:
-        copy.start()
-    copies.pop(0).wait()
+    hidden = to_gate_ref.shape[1]
+    tile = math.gcd(hidden, FORWARD)
+    first = pltpu.make_async_copy(left_hbm, left_map, sems.at[0])
+    first.start()
+    copies = []
+    for number in range(hidden // tile):
+        part = pl.ds(number * tile, tile)
+        for source, target in ((gate_hbm, gate_ref), (up_hbm, up_ref)):
+            sem = sems.at[len(copies) + 1]
+            copies.append(
+                pltpu.make_async_copy(source.at[:, part, :], target.at[:, part, :], sem)
+            )
+            copies[-1].start()
+    first.wait()
     left = jnp.zeros(left_ref.shape, F32)
-    for at in range(0, hidden, tile):
-        part = slice(at, at + tile)
-        copies.pop(0).wait()
+    for number in range(hidden // tile):
+        part = slice(number * tile, (number + 1) * tile)
+        copies[2 * number].wait()
         gate = contract(x_ref[...], gate_ref[0, part, :], 1, 1)
-        copies.pop(0).wait()
+        copies[2 * number + 1].wait()
         up = contract(x_ref[...], up_ref[0, part, :], 1, 1)
         sigmoid = jax.nn.sigmoid(gate)
         silu = gate * sigmoid
@@ -237,8 +252,6 @@
         to_gate_ref[:, part] = up * sigmoid * (1.0 + gate * (1.0 - sigmoid))
         left = left + contract((silu * up).astype(BF16), left_map[0, :, part], 1, 1)
     left_ref[...] = left.astype(BF16)
-    for copy in copies:
-        copy.wait()
 
 
 def layer(n_arrived, n_sent, n_before, stage, n_section, n_extra, *refs):
@@ -246,15 +259,28 @@
     take = lambda amount: [refs.pop(0) for _ in range(amount)]
     arrived = take(n_arrived)
     place = take(1)[0] if n_arrived > 1 else None
-    to_gate, to_up, down, gate, up, cols = take(6)
+    stored, cols = take(5), take(1)[0]
     comp = take(1)[0] if n_sent else None
     rows_before, part_before = take(2) if n_before else (None, None)
     if not n_sent:
         left_ref, right_proj, sketch = take(3)
     sent = take(n_sent)
     part_ref, rows_ref = take(2) if n_sent else take(1) + [None]
+    kept = stored if stage else take(5)
+    down, to_gate, to_up, gate, up = kept
     grad_gate, grad_up, rows_now = take(3)
     feat = rows_now.shape[1]
+    halves = [slice(0, feat)]
+    copies = []
+    if not stage:
+        halves = [slice(i * feat // HALVES, (i + 1) * feat // HALVES) for i in range(HALVES)]
+        pairs = [(stored[i], kept[i]) for i in range(3)]
+        for half in halves:
+            lanes = pl.ds(half.start, half.stop - half.start)
+            pairs += [(stored[i].at[:, :, lanes], kept[i].at[:, :, lanes]) for i in (3, 4)]
+        copies = [pltpu.make_async_copy(a, b, refs[0].at[i]) for i, (a, b) in enumerate(pairs)]
+        for copy in copies:
+            copy.start()
     live = lax.axis_index("section") == n_section - 1 - stage
 
     @pl.when(live)
@@ -265,19 +291,21 @@
         else:
             rows = arrived[0][...]
         rows_now[...] = rows
-        tile = math.gcd(grad_gate.shape[1], TILE)
-        for at in range(0, grad_gate.shape[1], tile):
-            part = slice(at, at + tile)
-            grad_hidden = contract(rows, down[0, part, :], 1, 1)
+        for copy in copies[:3]:
+            copy.wait()
+
+        def narrow(part):
+            grad_hidden = contract(rows_now[...], down[0, part, :], 1, 1)
             grad_gate[:, part] = (grad_hidden * to_gate[:, part]).astype(BF16)
             grad_up[:, part] = (grad_hidden * to_up[:, part]).astype(BF16)
-        weight, first = cols[:, 0:1], cols[:, 1:2]
-        for at in range(0, feat, TILE):
-            part = slice(at, at + TILE)
+
+        over_tiles(grad_gate.shape[1], NARROW, narrow)
+
+        def widen(part):
             total = contract(grad_gate[...], gate[0, :, part], 1, 0)
             total = total + contract(grad_up[...], up[0, :, part], 1, 0)
-            total = total * weight + rows[:, part].astype(F32) * first
-            total = total.astype(BF16)
+            kept = rows_now[:, part].astype(F32) * cols[:, 1:2]
+            total = (total * cols[:, 0:1] + kept).astype(BF16)
             part_ref[:, part] = total
             if n_sent:
                 chosen = contract(comp[...], total, 1, 0)
@@ -285,8 +313,15 @@
                 for turn in range(n_sent):
                     sent[turn][:, part] = chosen[turn * share : (turn + 1) * share].astype(BF16)
 
+        for number, half in enumerate(halves):
+            for copy in copies[3 + 2 * number : 5 + 2 * number]:
+                copy.wait()
+            over_tiles(half.stop - half.start, WIDEN, widen, half.start)
+
     @pl.when(jnp.logical_not(live))
     def _():
+        for copy in copies:
+            copy.wait()
         if n_before:
             rows_now[...] = rows_before[...]
             part_ref[...] = part_before[...]
@@ -306,12 +341,14 @@
     over_right = ones_where(axis == lane % size).astype(BF16)
     right = contract(high, over_right, 1, 0) + contract(low, over_right, 1, 0)
     for number in range(n_extra):
-        for at in range(0, feat, TILE):
-            part = slice(at, at + TILE)
-            over_left = ones_where(axis == (number * feat + at + lane) // size).astype(BF16)
-            outer = contract(left, over_left, 1, 0) * right
+
+        def add_terms(part, number=number):
+            over_left = ones_where(axis == (number * feat + part.start + lane) // size)
+            outer = contract(left, over_left.astype(BF16), 1, 0) * right
             terms = contract(sketch[number], outer.astype(BF16), 1, 0)
             part_ref[:, part] = (part_ref[:, part].astype(F32) + terms).astype(BF16)
+
+        over_tiles(feat, (TILE, 2), add_terms)
 
 
 def finish(n_expert, block, used, n_extra, q_dev, back_ref, slots_ref, grad_ref, sketch_ref):
@@ -451,6 +488,7 @@
         arrays,
         HBM,
         [pltpu.VMEM(a.shape, a.dtype) for a in arrays] + [pltpu.SemaphoreType.DMA((5,))],
+        60 << 20,
     )
 
     def exchange(rows):
@@ -469,27 +507,26 @@
         pairs = [(i, (i - turn) % n_section) for i in range(n_section)]
         around.append(lax.ppermute(fields, "section", pairs))
     top_rows = exchange(top_send)
-    kept = (
-        gate_weight,
-        up_weight,
-        down_weight,
-        left_proj.transpose(0, 2, 1),
-        right_proj.transpose(0, 2, 1),
-    )
-    kept, top_rows = lax.optimization_barrier((kept, top_rows))
-    to_gate, to_up, left, gate, up, down, left_map, right_map = pl.pallas_call(
+    tile = math.gcd(hidden, FORWARD)
+    weight = gate_weight.shape
+    left_map, right_map = left_proj.transpose(0, 2, 1), right_proj.transpose(0, 2, 1)
+    to_gate, to_up, left = pl.pallas_call(
         forward,
         out_shape=(
             shape(n_rows, hidden, dtype=F32),
             shape(n_rows, hidden, dtype=F32),
             shape(n_rows, sketch_dim),
-        )
-        + tuple(pltpu.VMEM(a.shape, a.dtype) for a in kept),
-        in_specs=[VMEM] + [HBM] * len(kept),
-        out_specs=(VMEM,) * (3 + len(kept)),
-        scratch_shapes=[pltpu.SemaphoreType.DMA((2 + 3 * (hidden // math.gcd(hidden, TILE)),))],
-        compiler_params=pltpu.CompilerParams(vmem_limit_bytes=40 << 20),
-    )(x_rows, *kept)
+        ),
+        in_specs=[VMEM, HBM, HBM, HBM],
+        out_specs=(VMEM,) * 3,
+        scratch_shapes=[
+            pltpu.VMEM(weight, BF16),
+            pltpu.VMEM(weight, BF16),
+            pltpu.VMEM(left_map.shape, BF16),
+            pltpu.SemaphoreType.DMA((1 + 2 * (hidden // tile),)),
+        ],
+        compiler_params=pltpu.CompilerParams(vmem_limit_bytes=58 << 20),
+    )(x_rows, gate_weight, up_weight, left_map)
     comp, place, cols, sketch, over = call(
         functools.partial(
             plan, n_section, n_expert, n_micro, tok_dev, top_k, block, share, q_dev
@@ -517,12 +554,12 @@
 
     rows, part = None, None
     arrived = [top_rows]
+    kept = (down_weight, to_gate, to_up, gate_weight, up_weight)
     for stage in range(n_section):
         last = stage == n_section - 1
-        inputs = list(arrived)
-        if stage > 0:
-            inputs += [place]
-        inputs += [to_gate, to_up, down, gate, up, cols]
+        inputs = list(arrived) + ([place] if stage > 0 else [])
+        specs = [VMEM] * len(inputs) + [VMEM if stage else HBM] * len(kept)
+        inputs += list(kept) + [cols]
         if last:
             inputs += [rows, part, left, right_map, sketch]
             out = (shape(n_rows, feat),)
@@ -530,33 +567,33 @@
             inputs += [comp] + ([rows, part] if stage > 0 else [])
             out = tuple(shape(share, feat) for _ in range(n_expert))
             out += (shape(n_rows, feat), shape(n_rows, feat))
-        kernel = functools.partial(
-            layer,
-            len(arrived),
-            0 if last else n_expert,
-            stage > 0,
-            stage,
-            n_section,
-            n_extra,
-        )
+        specs += [VMEM] * (len(inputs) - len(specs))
+        scratch = [
+            pltpu.VMEM((n_rows, hidden), BF16),
+            pltpu.VMEM((n_rows, hidden), BF16),
+            pltpu.VMEM((n_rows, feat), BF16),
+        ]
+        if stage == 0:
+            out += tuple(pltpu.VMEM(a.shape, a.dtype) for a in kept)
+            scratch.append(pltpu.SemaphoreType.DMA((3 + 2 * HALVES,)))
         results = pl.pallas_call(
-            kernel,
+            functools.partial(
+                layer, len(arrived), 0 if last else n_expert, stage > 0, stage, n_section, n_extra
+            ),
             out_shape=out,
-            in_specs=[VMEM] * len(inputs),
+            in_specs=specs,
             out_specs=tuple(VMEM for _ in out),
-            scratch_shapes=[
-                pltpu.VMEM((n_rows, hidden), BF16),
-                pltpu.VMEM((n_rows, hidden), BF16),
-                pltpu.VMEM((n_rows, feat), BF16),
-            ],
+            scratch_shapes=scratch,
             compiler_params=pltpu.CompilerParams(
-                vmem_limit_bytes=(12 << 20) + 2 * size_of(out) + 2 * size_of(arrived)
+                vmem_limit_bytes=(16 << 20) if stage else (38 << 20)
             ),
         )(*inputs)
         if last:
             back = exchange(results[0])
             break
-        part, rows = results[-2:]
+        part, rows = results[n_expert : n_expert + 2]
+        if stage == 0:
+            kept = results[n_expert + 2 :]
         arrived = send_down(results[:n_expert], n_section - 1 - stage, n_expert)
 
     def direct(*_):

time: 154 us -> 129 us (0.84); the launches traced: 155 us -> 128 us
  waiting for transfers between devices: 62.2 us -> 48.3 us
  Pallas kernels: 36.7 us -> 27.8 us
  local copies, waits for them, and re-layouts: 6.24 us -> 3.04 us
    ppermute x24, waiting for transfers between devices: 49.7 us -> 41.2 us  [send_down(): arrived[turn] = lax.ppermute(block, ('section', 'expert'), pairs)]
    pallas_call x4, Pallas kernels: 23.3 us -> 16.8 us  [on_device(): pl.pallas_call(functools.partial(layer, len(arrived), 0 if last else n_ex...]
    all_to_all x2, waiting for transfers between devices: 12.5 us -> 7.06 us  [exchange(): lax.all_to_all(blocks, 'expert', split_axis=0, concat_axis=0, tiled=True)]
    pallas_call x1, Pallas kernels: 10.7 us -> 7.29 us  [on_device(): pl.pallas_call(forward, out_shape=(shape(n_rows, hidden, dtype=F32), shap...]
    unnamed x26 -> x14, local copies, waits for them, and re-layouts: 5.73 us -> 2.53 us
  transfers between devices with their start and end apart: 29 -> 29, of which waited for: 8 -> 7; matrix products, arithmetic and copies ran while one was open for 0% -> 0% of each run, Pallas kernels for 7% -> 6%
where the time goes in v3:
time: 129 us; the launch traced here: 128 us
  waiting for transfers between devices  48.3 us (37%)
  starting transfers between devices  31.1 us (24%)
  Pallas kernels  27.8 us (22%)
  blocking collectives  16.2 us (13%)
  local copies, waits for them, and re-layouts  3.04 us (2%)
  between operations  1.74 us (1%)
    ppermute x24, waiting for transfers between devices, send_down(): arrived[turn] = lax.ppermute(block, ('section', 'expert'), pairs)  41.2 us
    ppermute x24, starting transfers between devices, send_down(): arrived[turn] = lax.ppermute(block, ('section', 'expert'), pairs)  21 us
    pallas_call x4, Pallas kernels, on_device(): pl.pallas_call(functools.partial(layer, len(arrived), 0 if last else n_ex...  16.8 us
    all_to_all x1, blocking collectives, exchange(): lax.all_to_all(blocks, 'expert', split_axis=0, concat_axis=0, tiled=True)  16.2 us
    pallas_call x1, Pallas kernels, on_device(): pl.pallas_call(forward, out_shape=(shape(n_rows, hidden, dtype=F32), shap...  7.29 us
    all_to_all x2, starting transfers between devices, exchange(): lax.all_to_all(blocks, 'expert', split_axis=0, concat_axis=0, tiled=True)  7.09 us
    all_to_all x2, waiting for transfers between devices, exchange(): lax.all_to_all(blocks, 'expert', split_axis=0, concat_axis=0, tiled=True)  7.06 us
    pallas_call x4, Pallas kernels, call(): pl.pallas_call(kernel, out_shape=out_shape, in_specs=[spec] * len(inputs)...  3.63 us
  transfers between devices with their start and end apart: 29, of which 7 were waited for; matrix products, arithmetic and copies ran while one was open for 0% of the time, Pallas kernels for 6%

profile of v3, /device:TPU:0, one launch (start us, length us, event | category | flops | bytes accessed | tf_op | source)
XLA Modules:
  0.0 128.1 jit_solution(4966504172384414489)
XLA Ops:
  0.6 2.2 %shard_map.117 = (bf16[64,2048]{1,0:T(8,128)(2,1)}, bf16[64,2048]{1,0:T(8,128)(2,1)}, bf16[64,16]{1,0:T(8,128)(2,1)S(1)}) custom-call(s32[1,2,2,8]{3,2,1,0:T(2,128)} %bitcast.213, bf16[1,2,2,8]{3,2,1,0:T(2,128)(2,1)} %bitcast.214, s32[2,8]{1,0:T(2,128)} %ex_hbm.1, bf16[1,2,8,2048]{3,2,1,0:T(8,128)(2,1)} %x_hbm.1, bf16[2,8,2048]{2,1,0:T(8,128)(2,1)} %top_hbm.1), custom_call_target="tpu_custom_call" | custom-call | tf_op jit(solution)/shard_map/pallas_call | solution.py:64
  2.9 16.2 %all_to_all.51 = bf16[8,8,2048]{2,1,0:T(8,128)(2,1)S(1)} all-to-all(bf16[8,8,2048]{2,1,0:T(8,128)(2,1)} %bitcast.211), channel_id=1, replica_groups=mesh['section'=4,'expert'=8] {'expert'}, dimensions={0} | all-to-all | bytes 524288 | tf_op jit(solution)/shard_map/all_to_all | solution.py:496
  19.1 3.6 %all-to-all-start.9 = ((bf16[8,8,2048]{2,1,0:T(8,128)(2,1)}), bf16[8,8,2048]{2,1,0:T(8,128)(2,1)S(1)}, u32[]{:S(2)}, u32[]{:S(2)}) async-start(bf16[8,8,2048]{2,1,0:T(8,128)(2,1)} %bitcast.210), calls=%async_computation.9 | async-start | bytes 524288 | tf_op jit(solution)/shard_map/all_to_all | solution.py:496
  22.7 0.1 collective-permute-start.5
  22.8 1.6 %collective-permute-start.4 = (f32[8,128]{1,0:T(8,128)S(1)}, f32[8,128]{1,0:T(8,128)S(1)}, u32[]{:S(2)}, u32[]{:S(2)}) collective-permute-start(f32[8,128]{1,0:T(8,128)S(1)} %shard_map.118.refs_0_), channel_id=1, source_target_pairs={{0,16},{8,24},{16,0},{24,8},{1,17},{9,25},{17,1},{25,9},{2,18},{10... | collective-permute-start | bytes 12296 | tf_op jit(solution)/shard_map/ppermute | solution.py:508
  24.3 1.4 %collective-permute-start.3 = (f32[8,128]{1,0:T(8,128)S(1)}, f32[8,128]{1,0:T(8,128)S(1)}, u32[]{:S(2)}, u32[]{:S(2)}) collective-permute-start(f32[8,128]{1,0:T(8,128)S(1)} %shard_map.118.refs_0_), channel_id=1, source_target_pairs={{0,24},{8,0},{16,8},{24,16},{1,25},{9,1},{17,9},{25,17},{2,26},{10... | collective-permute-start | bytes 12296 | tf_op jit(solution)/shard_map/ppermute | solution.py:508
  25.7 7.3 %shard_map.120 = (f32[64,1536]{1,0:T(8,128)}, f32[64,1536]{1,0:T(8,128)}, bf16[64,64]{1,0:T(8,128)(2,1)}) custom-call(bf16[64,2048]{1,0:T(8,128)(2,1)S(1)} %bitcast.206, bf16[1,1536,2048]{2,1,0:T(8,128)(2,1)} %refs_4_.1, bf16[1,1536,2048]{2,1,0:T(8,128)(2,1)} %refs_5_.1, bf16[1,64,1536]{2,1,0:T(8,128)(2,1)} %bitcast.212), custom_call_target="tpu_custom_call" | custom-call | tf_op jit(solution)/shard_map/pallas_call | solution.py:513
  33.0 0.0 collective-permute-done.3.refs_1_
  33.0 0.4 shard_map.119
  33.5 0.0 copy-start
  33.5 0.6 copy-done
  34.1 0.0 all-to-all-done.9
  34.1 8.6 %shard_map.121 = (bf16[24,2048]{1,0:T(8,128)(2,1)}, bf16[24,2048]{1,0:T(8,128)(2,1)}, bf16[24,2048]{1,0:T(8,128)(2,1)}, bf16[24,2048]{1,0:T(8,128)(2,1)}, bf16[2...) custom-call(bf16[64,2048]{1,0:T(8,128)(2,1)S(1)} %bitcast.203, ...), custom_call_target="tpu_custom_call" | custom-call | tf_op jit(solution)/shard_map/pallas_call | solution.py:579
  42.7 0.7 collective-permute-start.6
  43.4 0.7 collective-permute-start.7
  44.1 0.7 collective-permute-start.9
  44.8 0.7 collective-permute-start.12
  45.4 0.7 collective-permute-start.13
  46.1 0.0 collective-permute-done.6.refs_0_
  46.1 0.7 collective-permute-start.11
  46.8 0.0 collective-permute-done.7.refs_1_
  46.8 0.7 collective-permute-start.8
  47.5 0.0 collective-permute-done.9.refs_7_
  47.5 0.7 collective-permute-start.10
  48.2 0.0 collective-permute-done.11.refs_4_
  48.2 0.0 collective-permute-done.8.refs_2_
  48.2 0.9 copy-done.2
  49.2 0.9 copy-done.3
  50.1 0.1 shard_map.122
  50.2 0.7 collective-permute-start.14
  50.9 0.7 collective-permute-start.15
  51.5 0.7 collective-permute-start.17
  52.2 0.7 collective-permute-start.20
  52.9 0.7 collective-permute-start.21
  53.6 0.0 collective-permute-done.14.refs_0_
  53.6 0.7 collective-permute-start.19
  54.3 0.0 collective-permute-done.15.refs_1_
  54.3 0.7 collective-permute-start.16
  55.0 0.7 collective-permute-start.18
  55.6 0.0 collective-permute-done.21.refs_6_
  55.7 0.0 collective-permute-done.19.refs_4_
  55.7 0.0 collective-permute-done.18.refs_3_
  55.7 0.0 copy-start.5
  55.7 0.3 shard_map.123
  56.0 1.3 %collective-permute-start.22 = (bf16[24,2048]{1,0:T(8,128)(2,1)S(1)}, bf16[24,2048]{1,0:T(8,128)(2,1)S(1)}, u32[]{:S(2)}, u32[]{:S(2)}) collective-permute-start(bf16[24,2048]{1,0:T(8,128)(2,1)S(1)} %get-tuple-element.149), channel_id=1, source_target_pairs={{8,0},{9,1},{10,2},{11,3},{12,4},{13,5},{14,6},{15,7}} | collective-permute-start | bytes 294920 | tf_op jit(solution)/shard_map/ppermute | solution.py:392
  57.3 1.3 %collective-permute-start.23 = (bf16[24,2048]{1,0:T(8,128)(2,1)S(1)}, bf16[24,2048]{1,0:T(8,128)(2,1)S(1)}, u32[]{:S(2)}, u32[]{:S(2)}) collective-permute-start(bf16[24,2048]{1,0:T(8,128)(2,1)S(1)} %get-tuple-element.152), channel_id=1, source_target_pairs={{8,1},{9,0},{10,3},{11,2},{12,5},{13,4},{14,7},{15,6}} | collective-permute-start | bytes 294920 | tf_op jit(solution)/shard_map/ppermute | solution.py:392
  58.6 1.3 %collective-permute-start.25 = (bf16[24,2048]{1,0:T(8,128)(2,1)S(1)}, bf16[24,2048]{1,0:T(8,128)(2,1)S(1)}, u32[]{:S(2)}, u32[]{:S(2)}) collective-permute-start(bf16[24,2048]{1,0:T(8,128)(2,1)S(1)} %get-tuple-element.156), channel_id=1, source_target_pairs={{8,7},{9,6},{10,5},{11,4},{12,3},{13,2},{14,1},{15,0}} | collective-permute-start | bytes 294920 | tf_op jit(solution)/shard_map/ppermute | solution.py:392
  59.9 1.3 %collective-permute-start.28 = (bf16[24,2048]{1,0:T(8,128)(2,1)S(1)}, bf16[24,2048]{1,0:T(8,128)(2,1)S(1)}, u32[]{:S(2)}, u32[]{:S(2)}) collective-permute-start(bf16[24,2048]{1,0:T(8,128)(2,1)S(1)} %get-tuple-element.159), channel_id=1, source_target_pairs={{8,5},{9,4},{10,7},{11,6},{12,1},{13,0},{14,3},{15,2}} | collective-permute-start | bytes 294920 | tf_op jit(solution)/shard_map/ppermute | solution.py:392
  61.2 1.3 %collective-permute-start.29 = (bf16[24,2048]{1,0:T(8,128)(2,1)S(1)}, bf16[24,2048]{1,0:T(8,128)(2,1)S(1)}, u32[]{:S(2)}, u32[]{:S(2)}) collective-permute-start(bf16[24,2048]{1,0:T(8,128)(2,1)S(1)} %get-tuple-element.160), channel_id=1, source_target_pairs={{8,6},{9,7},{10,4},{11,5},{12,2},{13,3},{14,0},{15,1}} | collective-permute-start | bytes 294920 | tf_op jit(solution)/shard_map/ppermute | solution.py:392
  62.5 31.5 %collective-permute-done.22.refs_0_ = bf16[24,2048]{1,0:T(8,128)(2,1)S(1)} collective-permute-done((bf16[24,2048]{1,0:T(8,128)(2,1)S(1)}, bf16[24,2048]{1,0:T(8,128)(2,1)S(1)}, u32[]{:S(2)}, u32[]{:S(2)}) %collective-permute-start.22) | collective-permute-done | bytes 98336 | tf_op jit(solution)/shard_map/ppermute | solution.py:392
  94.0 1.3 collective-permute-start.27
  95.2 3.8 %collective-permute-done.23.refs_1_ = bf16[24,2048]{1,0:T(8,128)(2,1)S(1)} collective-permute-done((bf16[24,2048]{1,0:T(8,128)(2,1)S(1)}, bf16[24,2048]{1,0:T(8,128)(2,1)S(1)}, u32[]{:S(2)}, u32[]{:S(2)}) %collective-permute-start.23) | collective-permute-done | bytes 98336 | tf_op jit(solution)/shard_map/ppermute | solution.py:392
  99.0 1.3 collective-permute-start.24
  100.3 0.4 collective-permute-done.25.refs_7_
  100.7 1.3 collective-permute-start.26
  102.0 2.4 %collective-permute-done.27.refs_4_ = bf16[24,2048]{1,0:T(8,128)(2,1)S(1)} collective-permute-done((bf16[24,2048]{1,0:T(8,128)(2,1)S(1)}, bf16[24,2048]{1,0:T(8,128)(2,1)S(1)}, u32[]{:S(2)}, u32[]{:S(2)}) %collective-permute-start.27) | collective-permute-done | bytes 98336 | tf_op jit(solution)/shard_map/ppermute | solution.py:392
  104.4 1.0 collective-permute-done.24.refs_2_
  105.4 2.1 %collective-permute-done.26.refs_3_ = bf16[24,2048]{1,0:T(8,128)(2,1)S(1)} collective-permute-done((bf16[24,2048]{1,0:T(8,128)(2,1)S(1)}, bf16[24,2048]{1,0:T(8,128)(2,1)S(1)}, u32[]{:S(2)}, u32[]{:S(2)}) %collective-permute-start.26) | collective-permute-done | bytes 98336 | tf_op jit(solution)/shard_map/ppermute | solution.py:392
  107.5 7.9 %shard_map.124 = bf16[64,2048]{1,0:T(8,128)(2,1)} custom-call(bf16[24,2048]{1,0:T(8,128)(2,1)S(1)} %collective-permute-done.22.refs_0_, bf16[24,2048]{1,0:T(8,128)(2,1)S(1)} %collective-permute-done.23.refs_1_, bf16[24,2048]{1,0:T(8,128)(2,1)S(1)} %collective-permute-done.24.refs_2_, bf16[24,2048]{1,0:T(8,128)(2,1)S(1)} %collective-permute-done.26.refs_3_, ...), custom_call_target="tpu_custom_call" | custom-call | tf_op jit(solution)/shard_map/pallas_call | solution.py:579
  115.4 3.5 %all-to-all-start.10 = ((bf16[8,8,2048]{2,1,0:T(8,128)(2,1)}), bf16[8,8,2048]{2,1,0:T(8,128)(2,1)S(1)}, u32[]{:S(2)}, u32[]{:S(2)}) async-start(bf16[8,8,2048]{2,1,0:T(8,128)(2,1)} %bitcast.44), calls=%async_computation.10 | async-start | bytes 524288 | tf_op jit(solution)/shard_map/all_to_all | solution.py:496
  118.9 0.5 slice.30
  120.1 7.1 %all-to-all-done.10 = bf16[8,8,2048]{2,1,0:T(8,128)(2,1)S(1)} async-done(((bf16[8,8,2048]{2,1,0:T(8,128)(2,1)}), bf16[8,8,2048]{2,1,0:T(8,128)(2,1)S(1)}, u32[]{:S(2)}, u32[]{:S(2)}) %all-to-all-start.10) | async-done | bytes 262176 | tf_op jit(solution)/shard_map/all_to_all | solution.py:496
  127.1 0.9 conditional.1
  127.1 0.9 branch_0_fun.1
  (20 shorter events, 0.1 us)
Async XLA Ops:
  19.1 15.1 %all-to-all-start.9 = ((bf16[8,8,2048]{2,1,0:T(8,128)(2,1)}), bf16[8,8,2048]{2,1,0:T(8,128)(2,1)S(1)}, u32[]{:S(2)}, u32[]{:S(2)}) async-start(bf16[8,8,2048]{2,1,0:T(8,128)(2,1)} %bitcast.210), calls=%async_computation.9 | async-start | bytes 524288 | tf_op jit(solution)/shard_map/all_to_all | solution.py:496
  22.7 10.3 %collective-permute-start.5 = (f32[8,128]{1,0:T(8,128)S(1)}, f32[8,128]{1,0:T(8,128)S(1)}, u32[]{:S(2)}, u32[]{:S(2)}) collective-permute-start(f32[8,128]{1,0:T(8,128)S(1)} %shard_map.118.refs_0_), channel_id=1, source_target_pairs={{0,8},{8,16},{16,24},{24,0},{1,9},{9,17},{17,25},{25,1},{2,10},{10... | collective-permute-start | bytes 12296 | tf_op jit(solution)/shard_map/ppermute | solution.py:508
  22.8 10.3 %collective-permute-start.4 = (f32[8,128]{1,0:T(8,128)S(1)}, f32[8,128]{1,0:T(8,128)S(1)}, u32[]{:S(2)}, u32[]{:S(2)}) collective-permute-start(f32[8,128]{1,0:T(8,128)S(1)} %shard_map.118.refs_0_), channel_id=1, source_target_pairs={{0,16},{8,24},{16,0},{24,8},{1,17},{9,25},{17,1},{25,9},{2,18},{10... | collective-permute-start | bytes 12296 | tf_op jit(solution)/shard_map/ppermute | solution.py:508
  24.3 8.7 %collective-permute-start.3 = (f32[8,128]{1,0:T(8,128)S(1)}, f32[8,128]{1,0:T(8,128)S(1)}, u32[]{:S(2)}, u32[]{:S(2)}) collective-permute-start(f32[8,128]{1,0:T(8,128)S(1)} %shard_map.118.refs_0_), channel_id=1, source_target_pairs={{0,24},{8,0},{16,8},{24,16},{1,25},{9,1},{17,9},{25,17},{2,26},{10... | collective-permute-start | bytes 12296 | tf_op jit(solution)/shard_map/ppermute | solution.py:508
  33.5 0.6 copy-start
  34.1 14.1 %copy-start.1 = (bf16[192,64]{1,0:T(8,128)(2,1)S(1)}, bf16[192,64]{1,0:T(8,128)(2,1)}, u32[]{:S(2)}) copy-start(bf16[192,64]{1,0:T(8,128)(2,1)} %copy-done) | copy-start | bytes 73732
  42.7 3.4 %collective-permute-start.6 = (bf16[24,2048]{1,0:T(8,128)(2,1)}, bf16[24,2048]{1,0:T(8,128)(2,1)S(1)}, u32[]{:S(2)}, u32[]{:S(2)}) collective-permute-start(bf16[24,2048]{1,0:T(8,128)(2,1)} %get-tuple-element.111), channel_id=1, source_target_pairs={{24,16},{25,17},{26,18},{27,19},{28,20},{29,21},{30,22},{31,23}} | collective-permute-start | bytes 294920 | tf_op jit(solution)/shard_map/ppermute | solution.py:392
  43.4 3.4 %collective-permute-start.7 = (bf16[24,2048]{1,0:T(8,128)(2,1)}, bf16[24,2048]{1,0:T(8,128)(2,1)S(1)}, u32[]{:S(2)}, u32[]{:S(2)}) collective-permute-start(bf16[24,2048]{1,0:T(8,128)(2,1)} %get-tuple-element.114), channel_id=1, source_target_pairs={{24,17},{25,16},{26,19},{27,18},{28,21},{29,20},{30,23},{31,22}} | collective-permute-start | bytes 294920 | tf_op jit(solution)/shard_map/ppermute | solution.py:392
  44.1 3.4 %collective-permute-start.9 = (bf16[24,2048]{1,0:T(8,128)(2,1)}, bf16[24,2048]{1,0:T(8,128)(2,1)S(1)}, u32[]{:S(2)}, u32[]{:S(2)}) collective-permute-start(bf16[24,2048]{1,0:T(8,128)(2,1)} %get-tuple-element.118), channel_id=1, source_target_pairs={{24,23},{25,22},{26,21},{27,20},{28,19},{29,18},{30,17},{31,16}} | collective-permute-start | bytes 294920 | tf_op jit(solution)/shard_map/ppermute | solution.py:392
  44.8 3.4 %collective-permute-start.12 = (bf16[24,2048]{1,0:T(8,128)(2,1)}, bf16[24,2048]{1,0:T(8,128)(2,1)S(1)}, u32[]{:S(2)}, u32[]{:S(2)}) collective-permute-start(bf16[24,2048]{1,0:T(8,128)(2,1)} %get-tuple-element.121), channel_id=1, source_target_pairs={{24,21},{25,20},{26,23},{27,22},{28,17},{29,16},{30,19},{31,18}} | collective-permute-start | bytes 294920 | tf_op jit(solution)/shard_map/ppermute | solution.py:392
  45.4 2.7 %collective-permute-start.13 = (bf16[24,2048]{1,0:T(8,128)(2,1)}, bf16[24,2048]{1,0:T(8,128)(2,1)S(1)}, u32[]{:S(2)}, u32[]{:S(2)}) collective-permute-start(bf16[24,2048]{1,0:T(8,128)(2,1)} %get-tuple-element.122), channel_id=1, source_target_pairs={{24,22},{25,23},{26,20},{27,21},{28,18},{29,19},{30,16},{31,17}} | collective-permute-start | bytes 294920 | tf_op jit(solution)/shard_map/ppermute | solution.py:392
  46.1 2.1 %collective-permute-start.11 = (bf16[24,2048]{1,0:T(8,128)(2,1)}, bf16[24,2048]{1,0:T(8,128)(2,1)S(1)}, u32[]{:S(2)}, u32[]{:S(2)}) collective-permute-start(bf16[24,2048]{1,0:T(8,128)(2,1)} %get-tuple-element.120), channel_id=1, source_target_pairs={{24,20},{25,21},{26,22},{27,23},{28,16},{29,17},{30,18},{31,19}} | collective-permute-start | bytes 294920 | tf_op jit(solution)/shard_map/ppermute | solution.py:392
  46.8 1.4 %collective-permute-start.8 = (bf16[24,2048]{1,0:T(8,128)(2,1)}, bf16[24,2048]{1,0:T(8,128)(2,1)S(1)}, u32[]{:S(2)}, u32[]{:S(2)}) collective-permute-start(bf16[24,2048]{1,0:T(8,128)(2,1)} %get-tuple-element.116), channel_id=1, source_target_pairs={{24,18},{25,19},{26,16},{27,17},{28,22},{29,23},{30,20},{31,21}} | collective-permute-start | bytes 294920 | tf_op jit(solution)/shard_map/ppermute | solution.py:392
  47.5 0.7 collective-permute-start.10
  48.2 1.0 copy-start.2
  49.2 0.9 copy-start.3
  50.2 3.4 %collective-permute-start.14 = (bf16[24,2048]{1,0:T(8,128)(2,1)S(1)}, bf16[24,2048]{1,0:T(8,128)(2,1)S(1)}, u32[]{:S(2)}, u32[]{:S(2)}) collective-permute-start(bf16[24,2048]{1,0:T(8,128)(2,1)S(1)} %get-tuple-element.133), channel_id=1, source_target_pairs={{16,8},{17,9},{18,10},{19,11},{20,12},{21,13},{22,14},{23,15}} | collective-permute-start | bytes 294920 | tf_op jit(solution)/shard_map/ppermute | solution.py:392
  50.9 3.4 %collective-permute-start.15 = (bf16[24,2048]{1,0:T(8,128)(2,1)S(1)}, bf16[24,2048]{1,0:T(8,128)(2,1)S(1)}, u32[]{:S(2)}, u32[]{:S(2)}) collective-permute-start(bf16[24,2048]{1,0:T(8,128)(2,1)S(1)} %get-tuple-element.136), channel_id=1, source_target_pairs={{16,9},{17,8},{18,11},{19,10},{20,13},{21,12},{22,15},{23,14}} | collective-permute-start | bytes 294920 | tf_op jit(solution)/shard_map/ppermute | solution.py:392
  51.5 3.4 %collective-permute-start.17 = (bf16[24,2048]{1,0:T(8,128)(2,1)S(1)}, bf16[24,2048]{1,0:T(8,128)(2,1)S(1)}, u32[]{:S(2)}, u32[]{:S(2)}) collective-permute-start(bf16[24,2048]{1,0:T(8,128)(2,1)S(1)} %get-tuple-element.140), channel_id=1, source_target_pairs={{16,15},{17,14},{18,13},{19,12},{20,11},{21,10},{22,9},{23,8}} | collective-permute-start | bytes 294920 | tf_op jit(solution)/shard_map/ppermute | solution.py:392
  52.2 3.4 %collective-permute-start.20 = (bf16[24,2048]{1,0:T(8,128)(2,1)S(1)}, bf16[24,2048]{1,0:T(8,128)(2,1)S(1)}, u32[]{:S(2)}, u32[]{:S(2)}) collective-permute-start(bf16[24,2048]{1,0:T(8,128)(2,1)S(1)} %get-tuple-element.143), channel_id=1, source_target_pairs={{16,13},{17,12},{18,15},{19,14},{20,9},{21,8},{22,11},{23,10}} | collective-permute-start | bytes 294920 | tf_op jit(solution)/shard_map/ppermute | solution.py:392
  52.9 2.7 %collective-permute-start.21 = (bf16[24,2048]{1,0:T(8,128)(2,1)S(1)}, bf16[24,2048]{1,0:T(8,128)(2,1)S(1)}, u32[]{:S(2)}, u32[]{:S(2)}) collective-permute-start(bf16[24,2048]{1,0:T(8,128)(2,1)S(1)} %get-tuple-element.144), channel_id=1, source_target_pairs={{16,14},{17,15},{18,12},{19,13},{20,10},{21,11},{22,8},{23,9}} | collective-permute-start | bytes 294920 | tf_op jit(solution)/shard_map/ppermute | solution.py:392
  53.6 2.1 %collective-permute-start.19 = (bf16[24,2048]{1,0:T(8,128)(2,1)S(1)}, bf16[24,2048]{1,0:T(8,128)(2,1)S(1)}, u32[]{:S(2)}, u32[]{:S(2)}) collective-permute-start(bf16[24,2048]{1,0:T(8,128)(2,1)S(1)} %get-tuple-element.142), channel_id=1, source_target_pairs={{16,12},{17,13},{18,14},{19,15},{20,8},{21,9},{22,10},{23,11}} | collective-permute-start | bytes 294920 | tf_op jit(solution)/shard_map/ppermute | solution.py:392
  54.3 1.4 %collective-permute-start.16 = (bf16[24,2048]{1,0:T(8,128)(2,1)S(1)}, bf16[24,2048]{1,0:T(8,128)(2,1)S(1)}, u32[]{:S(2)}, u32[]{:S(2)}) collective-permute-start(bf16[24,2048]{1,0:T(8,128)(2,1)S(1)} %get-tuple-element.138), channel_id=1, source_target_pairs={{16,10},{17,11},{18,8},{19,9},{20,14},{21,15},{22,12},{23,13}} | collective-permute-start | bytes 294920 | tf_op jit(solution)/shard_map/ppermute | solution.py:392
  55.0 0.7 collective-permute-start.18
  55.7 51.8 %copy-start.4 = (bf16[64,64]{1,0:T(8,128)(2,1)S(1)}, bf16[64,64]{1,0:T(8,128)(2,1)}, u32[]{:S(2)}) copy-start(bf16[64,64]{1,0:T(8,128)(2,1)} %get-tuple-element.164.refs_17_) | copy-start | bytes 24580
  55.7 51.8 %copy-start.5 = (bf16[1,2048,64]{1,2,0:T(8,128)(2,1)S(1)}, bf16[1,2048,64]{1,2,0:T(8,128)(2,1)}, u32[]{:S(2)}) copy-start(bf16[1,2048,64]{1,2,0:T(8,128)(2,1)} %param.21) | copy-start | bytes 786436
  56.0 38.0 %collective-permute-start.22 = (bf16[24,2048]{1,0:T(8,128)(2,1)S(1)}, bf16[24,2048]{1,0:T(8,128)(2,1)S(1)}, u32[]{:S(2)}, u32[]{:S(2)}) collective-permute-start(bf16[24,2048]{1,0:T(8,128)(2,1)S(1)} %get-tuple-element.149), channel_id=1, source_target_pairs={{8,0},{9,1},{10,2},{11,3},{12,4},{13,5},{14,6},{15,7}} | collective-permute-start | bytes 294920 | tf_op jit(solution)/shard_map/ppermute | solution.py:392
  57.3 41.8 %collective-permute-start.23 = (bf16[24,2048]{1,0:T(8,128)(2,1)S(1)}, bf16[24,2048]{1,0:T(8,128)(2,1)S(1)}, u32[]{:S(2)}, u32[]{:S(2)}) collective-permute-start(bf16[24,2048]{1,0:T(8,128)(2,1)S(1)} %get-tuple-element.152), channel_id=1, source_target_pairs={{8,1},{9,0},{10,3},{11,2},{12,5},{13,4},{14,7},{15,6}} | collective-permute-start | bytes 294920 | tf_op jit(solution)/shard_map/ppermute | solution.py:392
  58.6 42.1 %collective-permute-start.25 = (bf16[24,2048]{1,0:T(8,128)(2,1)S(1)}, bf16[24,2048]{1,0:T(8,128)(2,1)S(1)}, u32[]{:S(2)}, u32[]{:S(2)}) collective-permute-start(bf16[24,2048]{1,0:T(8,128)(2,1)S(1)} %get-tuple-element.156), channel_id=1, source_target_pairs={{8,7},{9,6},{10,5},{11,4},{12,3},{13,2},{14,1},{15,0}} | collective-permute-start | bytes 294920 | tf_op jit(solution)/shard_map/ppermute | solution.py:392
  59.9 42.1 %collective-permute-start.28 = (bf16[24,2048]{1,0:T(8,128)(2,1)S(1)}, bf16[24,2048]{1,0:T(8,128)(2,1)S(1)}, u32[]{:S(2)}, u32[]{:S(2)}) collective-permute-start(bf16[24,2048]{1,0:T(8,128)(2,1)S(1)} %get-tuple-element.159), channel_id=1, source_target_pairs={{8,5},{9,4},{10,7},{11,6},{12,1},{13,0},{14,3},{15,2}} | collective-permute-start | bytes 294920 | tf_op jit(solution)/shard_map/ppermute | solution.py:392
  61.2 40.8 %collective-permute-start.29 = (bf16[24,2048]{1,0:T(8,128)(2,1)S(1)}, bf16[24,2048]{1,0:T(8,128)(2,1)S(1)}, u32[]{:S(2)}, u32[]{:S(2)}) collective-permute-start(bf16[24,2048]{1,0:T(8,128)(2,1)S(1)} %get-tuple-element.160), channel_id=1, source_target_pairs={{8,6},{9,7},{10,4},{11,5},{12,2},{13,3},{14,0},{15,1}} | collective-permute-start | bytes 294920 | tf_op jit(solution)/shard_map/ppermute | solution.py:392
  94.0 10.5 %collective-permute-start.27 = (bf16[24,2048]{1,0:T(8,128)(2,1)S(1)}, bf16[24,2048]{1,0:T(8,128)(2,1)S(1)}, u32[]{:S(2)}, u32[]{:S(2)}) collective-permute-start(bf16[24,2048]{1,0:T(8,128)(2,1)S(1)} %get-tuple-element.158), channel_id=1, source_target_pairs={{8,4},{9,5},{10,6},{11,7},{12,0},{13,1},{14,2},{15,3}} | collective-permute-start | bytes 294920 | tf_op jit(solution)/shard_map/ppermute | solution.py:392
  99.0 6.4 %collective-permute-start.24 = (bf16[24,2048]{1,0:T(8,128)(2,1)S(1)}, bf16[24,2048]{1,0:T(8,128)(2,1)S(1)}, u32[]{:S(2)}, u32[]{:S(2)}) collective-permute-start(bf16[24,2048]{1,0:T(8,128)(2,1)S(1)} %get-tuple-element.154), channel_id=1, source_target_pairs={{8,2},{9,3},{10,0},{11,1},{12,6},{13,7},{14,4},{15,5}} | collective-permute-start | bytes 294920 | tf_op jit(solution)/shard_map/ppermute | solution.py:392
  100.7 6.8 %collective-permute-start.26 = (bf16[24,2048]{1,0:T(8,128)(2,1)S(1)}, bf16[24,2048]{1,0:T(8,128)(2,1)S(1)}, u32[]{:S(2)}, u32[]{:S(2)}) collective-permute-start(bf16[24,2048]{1,0:T(8,128)(2,1)S(1)} %get-tuple-element.157), channel_id=1, source_target_pairs={{8,3},{9,2},{10,1},{11,0},{12,7},{13,6},{14,5},{15,4}} | collective-permute-start | bytes 294920 | tf_op jit(solution)/shard_map/ppermute | solution.py:392
  107.5 19.6 %copy-start.8 = (bf16[1,1536,64]{1,2,0:T(8,128)(2,1)S(1)}, bf16[1,1536,64]{1,2,0:T(8,128)(2,1)}, u32[]{:S(2)}) copy-start(bf16[1,1536,64]{1,2,0:T(8,128)(2,1)} %param.20) | copy-start | bytes 589828
  115.4 11.7 %all-to-all-start.10 = ((bf16[8,8,2048]{2,1,0:T(8,128)(2,1)}), bf16[8,8,2048]{2,1,0:T(8,128)(2,1)S(1)}, u32[]{:S(2)}, u32[]{:S(2)}) async-start(bf16[8,8,2048]{2,1,0:T(8,128)(2,1)} %bitcast.44), calls=%async_computation.10 | async-start | bytes 524288 | tf_op jit(solution)/shard_map/all_to_all | solution.py:496

commit v4 on v3

--- a/solution.py
+++ b/solution.py
@@ -12,12 +12,11 @@
 EXM = 4
 CAP = 3
 LANES = 128
-TILE = 256
 MOST_PERMUTES = 8
 NARROW = (1536, 1)
 WIDEN = (2048, 1)
 FORWARD = 512
-HALVES = 2
+SKETCH = (2048, 1)
 
 F32 = jnp.float32
 BF16 = jnp.bfloat16
@@ -47,15 +46,15 @@
     return sum(a.dtype.itemsize * a.size for a in arrays)
 
 
-def over_tiles(size, shape, body, start=0):
+def over_tiles(size, shape, body):
     tile, together = math.gcd(size, shape[0]), shape[1]
 
     def step(number, carry):
-        body(pl.ds(pl.multiple_of(start + number * tile, tile), tile))
+        body(pl.ds(pl.multiple_of(number * tile, tile), tile))
         return carry
 
     if size == tile:
-        body(pl.ds(start, tile))
+        body(pl.ds(0, tile))
         return
     lax.fori_loop(0, size // tile, step, 0, unroll=math.gcd(size // tile, together))
 
@@ -88,8 +87,8 @@
 
 
 def prepare(n_section, n_expert, block, ids_hbm, w_hbm, ex_hbm, x_hbm, top_hbm, *refs):
-    saved_ref, top_send_ref, slots_ref = refs[:3]
-    ids_ref, w_ref, ex_ref, x_ref, top_ref, sems = refs[3:]
+    send_ref, slots_ref = refs[:2]
+    ids_ref, w_ref, ex_ref, x_ref, top_ref, sems = refs[2:]
     from_hbm = (ids_hbm, w_hbm, ex_hbm, x_hbm, top_hbm)
     copy_all(list(zip(from_hbm, (ids_ref, w_ref, ex_ref, x_ref, top_ref))), sems)
     n_micro, top_k, tok_dev = ids_ref.shape[1:]
@@ -112,26 +111,31 @@
         local = local + contract(fields, ones_where(here), 1, 0)
         there = me * tokens + m * tok_dev + iota((tok_dev, n_all), 0)
         packed = packed + contract(fields, ones_where(iota((tok_dev, n_all), 1) == there), 1, 0)
-    rows = n_expert * block
-    group = (iota((rows, tokens), 0) // (block * (n_expert // EXPERTS))).astype(F32)
-    hit = names(local, top_k, group)
     early, late = iota((tokens, tokens), 0), iota((tokens, tokens), 1)
     before = ones_where((early // tok_dev == late // tok_dev) & (early < late))
-    position = contract(hit, before, 1, 0)
-    slot = iota((rows, tokens), 0) % block - CAP * (iota((rows, tokens), 1) // tok_dev)
-    fits = (hit > 0.5) & (slot >= 0) & (slot < CAP) & (position == slot.astype(F32))
-    slots = ones_where(fits).astype(BF16)
-    slots_ref[...] = slots
+
+    def slots_in(height):
+        at = (n_expert * height, tokens)
+        group = (iota(at, 0) // (height * (n_expert // EXPERTS))).astype(F32)
+        hit = names(local, top_k, group)
+        position = contract(hit, before, 1, 0)
+        slot = iota(at, 0) % block - CAP * (iota(at, 1) // tok_dev)
+        fits = (hit > 0.5) & (slot >= 0) & (slot < CAP) & (position == slot.astype(F32))
+        return ones_where(fits)
+
+    slots_ref[...] = slots_in(block).astype(BF16)
+    both = slots_in(2 * block)
+    second = iota(both.shape, 0) % (2 * block) >= block
+    for_saved = jnp.where(second, 0.0, both).astype(BF16)
+    for_top = jnp.where(second & (section == n_section - 1), both, 0.0).astype(BF16)
     saved = jnp.concatenate([x_ref[0, m] for m in range(n_micro)], axis=0)
-    saved_ref[...] = contract(slots, saved, 1, 0).astype(BF16)
+    top = jnp.concatenate([top_ref[m] for m in range(n_micro)], axis=0)
+    send_ref[...] = (contract(for_saved, saved, 1, 0) + contract(for_top, top, 1, 0)).astype(BF16)
+    spare_at = iota((2 * n_expert * block, n_all), 0) % (2 * block)
     for number, (at_row, lanes) in enumerate(field_places(n_fields, n_all, feat, n_micro * CAP)):
-        spare = iota((rows, n_all), 0) % block == at_row
-        field = jnp.broadcast_to(packed[number : number + 1, :], (rows, n_all))
-        kept = saved_ref[:, lanes].astype(F32)
-        saved_ref[:, lanes] = jnp.where(spare, field, kept).astype(BF16)
-    top = jnp.concatenate([top_ref[m] for m in range(n_micro)], axis=0)
-    used = jnp.where(section == n_section - 1, slots, jnp.zeros_like(slots))
-    top_send_ref[...] = contract(used, top, 1, 0).astype(BF16)
+        field = jnp.broadcast_to(packed[number : number + 1, :], spare_at.shape)
+        kept = send_ref[:, lanes].astype(F32)
+        send_ref[:, lanes] = jnp.where(spare_at == at_row, field, kept).astype(BF16)
 
 
 def field_places(n_fields, n_all, feat, first_row):
@@ -146,7 +150,7 @@
     rows, feat = x_ref.shape
     total = jnp.zeros(fields_ref.shape, F32)
     for number, (at_row, lanes) in enumerate(field_places(n_fields, n_all, feat, used)):
-        spare = iota((rows, n_all), 0) % block == at_row
+        spare = iota((rows, n_all), 0) % (2 * block) == at_row
         kept = jnp.where(spare, x_ref[:, lanes].astype(F32), 0.0)
         field = jnp.sum(kept, axis=0, keepdims=True)
         total = jnp.where(iota(fields_ref.shape, 0) == number, field, total)
@@ -223,35 +227,40 @@
 
 
 def forward(
-    x_ref, gate_hbm, up_hbm, left_hbm, to_gate_ref, to_up_ref, left_ref, gate_ref, up_ref, left_map, sems
+    block, both_ref, gate_hbm, up_hbm, down_hbm, left_hbm, right_hbm,
+    to_gate_ref, to_up_ref, left_ref, top_ref, gate_ref, up_ref, down_ref, right_map, left_map, sems,
 ):
-    hidden = to_gate_ref.shape[1]
+    n_rows, hidden = to_gate_ref.shape
+    feat = top_ref.shape[1]
     tile = math.gcd(hidden, FORWARD)
-    first = pltpu.make_async_copy(left_hbm, left_map, sems.at[0])
-    first.start()
-    copies = []
+    pairs = [(left_hbm, left_map)]
     for number in range(hidden // tile):
         part = pl.ds(number * tile, tile)
-        for source, target in ((gate_hbm, gate_ref), (up_hbm, up_ref)):
-            sem = sems.at[len(copies) + 1]
-            copies.append(
-                pltpu.make_async_copy(source.at[:, part, :], target.at[:, part, :], sem)
-            )
-            copies[-1].start()
-    first.wait()
+        pairs.append((gate_hbm.at[:, part, :], gate_ref.at[:, part, :]))
+        pairs.append((up_hbm.at[:, part, :], up_ref.at[:, part, :]))
+    pairs += [(down_hbm, down_ref), (right_hbm, right_map)]
+    copies = [pltpu.make_async_copy(a, b, sems.at[i]) for i, (a, b) in enumerate(pairs)]
+    for copy in copies:
+        copy.start()
+    both = both_ref[...].astype(F32).reshape(n_rows // block, 2 * block, feat)
+    top_ref[...] = both[:, block:].reshape(n_rows, feat).astype(BF16)
+    x = both[:, :block].reshape(n_rows, feat).astype(BF16)
+    copies[0].wait()
     left = jnp.zeros(left_ref.shape, F32)
     for number in range(hidden // tile):
         part = slice(number * tile, (number + 1) * tile)
-        copies[2 * number].wait()
-        gate = contract(x_ref[...], gate_ref[0, part, :], 1, 1)
         copies[2 * number + 1].wait()
-        up = contract(x_ref[...], up_ref[0, part, :], 1, 1)
+        gate = contract(x, gate_ref[0, part, :], 1, 1)
+        copies[2 * number + 2].wait()
+        up = contract(x, up_ref[0, part, :], 1, 1)
         sigmoid = jax.nn.sigmoid(gate)
         silu = gate * sigmoid
         to_up_ref[:, part] = silu
         to_gate_ref[:, part] = up * sigmoid * (1.0 + gate * (1.0 - sigmoid))
         left = left + contract((silu * up).astype(BF16), left_map[0, :, part], 1, 1)
     left_ref[...] = left.astype(BF16)
+    for copy in copies[-2:]:
+        copy.wait()
 
 
 def layer(n_arrived, n_sent, n_before, stage, n_section, n_extra, *refs):
@@ -259,28 +268,15 @@
     take = lambda amount: [refs.pop(0) for _ in range(amount)]
     arrived = take(n_arrived)
     place = take(1)[0] if n_arrived > 1 else None
-    stored, cols = take(5), take(1)[0]
+    down, to_gate, to_up, gate, up, cols = take(6)
     comp = take(1)[0] if n_sent else None
     rows_before, part_before = take(2) if n_before else (None, None)
     if not n_sent:
         left_ref, right_proj, sketch = take(3)
     sent = take(n_sent)
     part_ref, rows_ref = take(2) if n_sent else take(1) + [None]
-    kept = stored if stage else take(5)
-    down, to_gate, to_up, gate, up = kept
-    grad_gate, grad_up, rows_now = take(3)
+    grad_gate, grad_up, rows_now = refs
     feat = rows_now.shape[1]
-    halves = [slice(0, feat)]
-    copies = []
-    if not stage:
-        halves = [slice(i * feat // HALVES, (i + 1) * feat // HALVES) for i in range(HALVES)]
-        pairs = [(stored[i], kept[i]) for i in range(3)]
-        for half in halves:
-            lanes = pl.ds(half.start, half.stop - half.start)
-            pairs += [(stored[i].at[:, :, lanes], kept[i].at[:, :, lanes]) for i in (3, 4)]
-        copies = [pltpu.make_async_copy(a, b, refs[0].at[i]) for i, (a, b) in enumerate(pairs)]
-        for copy in copies:
-            copy.start()
     live = lax.axis_index("section") == n_section - 1 - stage
 
     @pl.when(live)
@@ -291,9 +287,6 @@
         else:
             rows = arrived[0][...]
         rows_now[...] = rows
-        for copy in copies[:3]:
-            copy.wait()
-
         def narrow(part):
             grad_hidden = contract(rows_now[...], down[0, part, :], 1, 1)
             grad_gate[:, part] = (grad_hidden * to_gate[:, part]).astype(BF16)
@@ -313,15 +306,10 @@
                 for turn in range(n_sent):
                     sent[turn][:, part] = chosen[turn * share : (turn + 1) * share].astype(BF16)
 
-        for number, half in enumerate(halves):
-            for copy in copies[3 + 2 * number : 5 + 2 * number]:
-                copy.wait()
-            over_tiles(half.stop - half.start, WIDEN, widen, half.start)
+        over_tiles(feat, WIDEN, widen)
 
     @pl.when(jnp.logical_not(live))
     def _():
-        for copy in copies:
-            copy.wait()
         if n_before:
             rows_now[...] = rows_before[...]
             part_ref[...] = part_before[...]
@@ -337,7 +325,8 @@
     low = (right - high.astype(F32)).astype(BF16)
     left = left_ref[...]
     size = left.shape[1]
-    lane, axis = iota((size, TILE), 1), iota((size, TILE), 0)
+    tile = math.gcd(feat, SKETCH[0])
+    lane, axis = iota((size, tile), 1), iota((size, tile), 0)
     over_right = ones_where(axis == lane % size).astype(BF16)
     right = contract(high, over_right, 1, 0) + contract(low, over_right, 1, 0)
     for number in range(n_extra):
@@ -348,7 +337,7 @@
             terms = contract(sketch[number], outer.astype(BF16), 1, 0)
             part_ref[:, part] = (part_ref[:, part].astype(F32) + terms).astype(BF16)
 
-        over_tiles(feat, (TILE, 2), add_terms)
+        over_tiles(feat, SKETCH, add_terms)
 
 
 def finish(n_expert, block, used, n_extra, q_dev, back_ref, slots_ref, grad_ref, sketch_ref):
@@ -371,14 +360,9 @@
 
 def send_down(blocks, section, n_expert):
     window = 5
-    far, near = list(range(n_expert - 1, n_expert // 2 - 1, -1)), list(range(n_expert // 2))
-    near[0:2] = near[1::-1]
-    order = []
-    while far or near:
-        for some, amount in ((far, 1), (near, 1), (far, 1), (near, 1), (far, 2), (near, 2)):
-            order += some[:amount]
-            del some[:amount]
-    freed = [3, 1, 0, 2, 4] + list(range(5, n_expert))
+    quick, far = [0, n_expert // 4, 1], [n_expert // 2 + 1, n_expert // 2]
+    late = [turn for turn in reversed(range(n_expert)) if turn not in quick + far]
+    order = quick + far + late
     arrived = [None] * n_expert
     for place, turn in enumerate(order):
         pairs = [
@@ -387,7 +371,7 @@
         ]
         block = blocks[turn]
         if place >= window:
-            earlier = order[freed[place - window]]
+            earlier = order[place - window]
             block, arrived[earlier] = lax.optimization_barrier((block, arrived[earlier]))
         arrived[turn] = lax.ppermute(block, ("section", "expert"), pairs)
     return arrived
@@ -482,9 +466,9 @@
         saved_inputs,
         top_grad,
     )
-    saved_send, top_send, slots = call(
+    send, slots = call(
         functools.partial(prepare, n_section, n_expert, block),
-        (shape(n_rows, feat), shape(n_rows, feat), shape(n_rows, tokens)),
+        (shape(2 * n_rows, feat), shape(n_rows, tokens)),
         arrays,
         HBM,
         [pltpu.VMEM(a.shape, a.dtype) for a in arrays] + [pltpu.SemaphoreType.DMA((5,))],
@@ -492,41 +476,40 @@
     )
 
     def exchange(rows):
-        blocks = rows.reshape(n_expert, block, feat)
+        blocks = rows.reshape(n_expert, rows.shape[0] // n_expert, feat)
         blocks = lax.all_to_all(blocks, "expert", split_axis=0, concat_axis=0, tiled=True)
-        return blocks.reshape(n_rows, feat)
-
-    x_rows = exchange(saved_send)
+        return blocks.reshape(rows.shape)
+
+    both = exchange(send)
     (fields,) = call(
         functools.partial(collect, block, used, 2 * top_k + 1),
         (shape(-(-(2 * top_k + 1) // 8) * 8, n_expert * tokens, dtype=F32),),
-        (x_rows,),
+        (both,),
     )
     around = [fields]
     for turn in range(1, n_section):
         pairs = [(i, (i - turn) % n_section) for i in range(n_section)]
         around.append(lax.ppermute(fields, "section", pairs))
-    top_rows = exchange(top_send)
     tile = math.gcd(hidden, FORWARD)
-    weight = gate_weight.shape
     left_map, right_map = left_proj.transpose(0, 2, 1), right_proj.transpose(0, 2, 1)
-    to_gate, to_up, left = pl.pallas_call(
-        forward,
+    stored = (gate_weight, up_weight, down_weight, left_map, right_map)
+    to_gate, to_up, left, top_rows, gate, up, down, right_map = pl.pallas_call(
+        functools.partial(forward, block),
         out_shape=(
-            shape(n_rows, hidden, dtype=F32),
-            shape(n_rows, hidden, dtype=F32),
+            pltpu.VMEM((n_rows, hidden), F32),
+            pltpu.VMEM((n_rows, hidden), F32),
             shape(n_rows, sketch_dim),
-        ),
-        in_specs=[VMEM, HBM, HBM, HBM],
-        out_specs=(VMEM,) * 3,
+            shape(n_rows, feat),
+        )
+        + tuple(pltpu.VMEM(stored[i].shape, BF16) for i in (0, 1, 2, 4)),
+        in_specs=[VMEM] + [HBM] * len(stored),
+        out_specs=(VMEM,) * 8,
         scratch_shapes=[
-            pltpu.VMEM(weight, BF16),
-            pltpu.VMEM(weight, BF16),
             pltpu.VMEM(left_map.shape, BF16),
-            pltpu.SemaphoreType.DMA((1 + 2 * (hidden // tile),)),
+            pltpu.SemaphoreType.DMA((3 + 2 * (hidden // tile),)),
         ],
-        compiler_params=pltpu.CompilerParams(vmem_limit_bytes=58 << 20),
-    )(x_rows, gate_weight, up_weight, left_map)
+        compiler_params=pltpu.CompilerParams(vmem_limit_bytes=38 << 20),
+    )(both, *stored)
     comp, place, cols, sketch, over = call(
         functools.partial(
             plan, n_section, n_expert, n_micro, tok_dev, top_k, block, share, q_dev
@@ -545,6 +528,7 @@
     raw = (top_grad, gate_weight, up_weight, down_weight, left_proj, right_proj)
 
     def crowded(*_):
+        x_rows = both.reshape(n_expert, 2 * block, feat)[:, :block].reshape(n_rows, feat)
         return by_owners(
             block, used, n_extra, q_dev, raw, slots, x_rows, top_rows, cols, sketch
         )
@@ -554,12 +538,10 @@
 
     rows, part = None, None
     arrived = [top_rows]
-    kept = (down_weight, to_gate, to_up, gate_weight, up_weight)
     for stage in range(n_section):
         last = stage == n_section - 1
         inputs = list(arrived) + ([place] if stage > 0 else [])
-        specs = [VMEM] * len(inputs) + [VMEM if stage else HBM] * len(kept)
-        inputs += list(kept) + [cols]
+        inputs += [down, to_gate, to_up, gate, up, cols]
         if last:
             inputs += [rows, part, left, right_map, sketch]
             out = (shape(n_rows, feat),)
@@ -567,33 +549,23 @@
             inputs += [comp] + ([rows, part] if stage > 0 else [])
             out = tuple(shape(share, feat) for _ in range(n_expert))
             out += (shape(n_rows, feat), shape(n_rows, feat))
-        specs += [VMEM] * (len(inputs) - len(specs))
-        scratch = [
-            pltpu.VMEM((n_rows, hidden), BF16),
-            pltpu.VMEM((n_rows, hidden), BF16),
-            pltpu.VMEM((n_rows, feat), BF16),
-        ]
-        if stage == 0:
-            out += tuple(pltpu.VMEM(a.shape, a.dtype) for a in kept)
-            scratch.append(pltpu.SemaphoreType.DMA((3 + 2 * HALVES,)))
-        results = pl.pallas_call(
+        results = call(
             functools.partial(
                 layer, len(arrived), 0 if last else n_expert, stage > 0, stage, n_section, n_extra
             ),
-            out_shape=out,
-            in_specs=specs,
-            out_specs=tuple(VMEM for _ in out),
-            scratch_shapes=scratch,
-            compiler_params=pltpu.CompilerParams(
-                vmem_limit_bytes=(16 << 20) if stage else (38 << 20)
-            ),
-        )(*inputs)
+            out,
+            inputs,
+            scratch=[
+                pltpu.VMEM((n_rows, hidden), BF16),
+                pltpu.VMEM((n_rows, hidden), BF16),
+                pltpu.VMEM((n_rows, feat), BF16),
+            ],
+            limit=16 << 20,
+        )
         if last:
             back = exchange(results[0])
             break
-        part, rows = results[n_expert : n_expert + 2]
-        if stage == 0:
-            kept = results[n_expert + 2 :]
+        part, rows = results[n_expert:]
         arrived = send_down(results[:n_expert], n_section - 1 - stage, n_expert)
 
     def direct(*_):

time: 129 us -> 117 us (0.907)
  Pallas kernels: 27.8 us -> 17.6 us
  blocking collectives: 16.2 us -> 21.8 us
  starting transfers between devices: 31.1 us -> 27.4 us
  local copies, waits for them, and re-layouts: 3.04 us -> 0.53 us
    pallas_call x5 -> x1, Pallas kernels: 24.1 us -> 7.24 us  [on_device(): pl.pallas_call(functools.partial(forward, block), out_shape=(pltpu.VMEM((...]
    pallas_call x4 -> x8, Pallas kernels: 3.63 us -> 10.3 us  [call(): pl.pallas_call(kernel, out_shape=out_shape, in_specs=[spec] * len(inputs)...]
    all_to_all x1, blocking collectives: 16.2 us -> 21.8 us  [exchange(): lax.all_to_all(blocks, 'expert', split_axis=0, concat_axis=0, tiled=True)]
    all_to_all x2 -> x1, starting transfers between devices: 7.09 us -> 3.41 us  [exchange(): lax.all_to_all(blocks, 'expert', split_axis=0, concat_axis=0, tiled=True)]
    unnamed x14 -> x6, local copies, waits for them, and re-layouts: 2.53 us -> 0.01 us
    all_to_all x2 -> x1, waiting for transfers between devices: 7.06 us -> 6.99 us  [exchange(): lax.all_to_all(blocks, 'expert', split_axis=0, concat_axis=0, tiled=True)]
  transfers between devices with their start and end apart: 29 -> 28, of which waited for: 7 -> 8; matrix products, arithmetic and copies ran while one was open for 0% -> 0% of each run, Pallas kernels for 6% -> 6%
where the time goes in v4:
time: 117 us; the launch traced here: 116 us
  waiting for transfers between devices  47.3 us (40%)
  starting transfers between devices  27.4 us (23%)
  blocking collectives  21.8 us (19%)
  Pallas kernels  17.6 us (15%)
  between operations  1.71 us (1%)
    ppermute x24, waiting for transfers between devices, send_down(): arrived[turn] = lax.ppermute(block, ('section', 'expert'), pairs)  40.3 us
    all_to_all x1, blocking collectives, exchange(): lax.all_to_all(blocks, 'expert', split_axis=0, concat_axis=0, tiled=True)  21.8 us
    ppermute x24, starting transfers between devices, send_down(): arrived[turn] = lax.ppermute(block, ('section', 'expert'), pairs)  21 us
    pallas_call x8, Pallas kernels, call(): pl.pallas_call(kernel, out_shape=out_shape, in_specs=[spec] * len(inputs)...  10.3 us
    pallas_call x1, Pallas kernels, on_device(): pl.pallas_call(functools.partial(forward, block), out_shape=(pltpu.VMEM((...  7.24 us
    all_to_all x1, waiting for transfers between devices, exchange(): lax.all_to_all(blocks, 'expert', split_axis=0, concat_axis=0, tiled=True)  6.99 us
    all_to_all x1, starting transfers between devices, exchange(): lax.all_to_all(blocks, 'expert', split_axis=0, concat_axis=0, tiled=True)  3.41 us
    ppermute x3, starting transfers between devices, on_device(): around.append(lax.ppermute(fields, 'section', pairs))  3.03 us
  transfers between devices with their start and end apart: 28, of which 8 were waited for; matrix products, arithmetic and copies ran while one was open for 0% of the time, Pallas kernels for 6%

profile of v4, /device:TPU:0, one launch (start us, length us, event | category | flops | bytes accessed | tf_op | source)
XLA Modules:
  0.0 116.3 jit_solution(9506396655891069852)
XLA Ops:
  0.6 2.5 %shard_map.117 = (bf16[128,2048]{1,0:T(8,128)(2,1)}, bf16[64,16]{1,0:T(8,128)(2,1)S(1)}) custom-call(s32[1,2,2,8]{3,2,1,0:T(2,128)} %bitcast.208, bf16[1,2,2,8]{3,2,1,0:T(2,128)(2,1)} %bitcast.209, s32[2,8]{1,0:T(2,128)} %ex_hbm.1, bf16[1,2,8,2048]{3,2,1,0:T(8,128)(2,1)} %x_hbm.1, bf16[2,8,2048]{2,1,0:T(8,128)(2,1)} %top_hbm.1), custom_call_target="tpu_custom_call" | custom-call | tf_op jit(solution)/shard_map/pallas_call | solution.py:63
  3.1 21.8 %all_to_all.46 = bf16[8,16,2048]{2,1,0:T(8,128)(2,1)S(1)} all-to-all(bf16[8,16,2048]{2,1,0:T(8,128)(2,1)} %bitcast.205), channel_id=1, replica_groups=mesh['section'=4,'expert'=8] {'expert'}, dimensions={0} | all-to-all | bytes 1048576 | tf_op jit(solution)/shard_map/all_to_all | solution.py:480
  24.9 0.1 collective-permute-start.5
  25.0 1.6 %collective-permute-start.4 = (f32[8,128]{1,0:T(8,128)S(1)}, f32[8,128]{1,0:T(8,128)S(1)}, u32[]{:S(2)}, u32[]{:S(2)}) collective-permute-start(f32[8,128]{1,0:T(8,128)S(1)} %shard_map.118.refs_0_), channel_id=1, source_target_pairs={{0,16},{8,24},{16,0},{24,8},{1,17},{9,25},{17,1},{25,9},{2,18},{10... | collective-permute-start | bytes 12296 | tf_op jit(solution)/shard_map/ppermute | solution.py:492
  26.6 1.4 %collective-permute-start.3 = (f32[8,128]{1,0:T(8,128)S(1)}, f32[8,128]{1,0:T(8,128)S(1)}, u32[]{:S(2)}, u32[]{:S(2)}) collective-permute-start(f32[8,128]{1,0:T(8,128)S(1)} %shard_map.118.refs_0_), channel_id=1, source_target_pairs={{0,24},{8,0},{16,8},{24,16},{1,25},{9,1},{17,9},{25,17},{2,26},{10... | collective-permute-start | bytes 12296 | tf_op jit(solution)/shard_map/ppermute | solution.py:492
  28.0 7.2 %shard_map.120 = (f32[64,1536]{1,0:T(8,128)S(1)}, f32[64,1536]{1,0:T(8,128)S(1)}, bf16[64,64]{1,0:T(8,128)(2,1)}, bf16[64,2048]{1,0:T(8,128)(2,1)S(1)}, bf16[1,1...) custom-call(bf16[128,2048]{1,0:T(8,128)(2,1)S(1)} %bitcast.202, ...), custom_call_target="tpu_custom_call" | custom-call | tf_op jit(solution)/shard_map/pallas_call | solution.py:496
  35.2 0.0 collective-permute-done.5.refs_3_
  35.2 0.0 collective-permute-done.4.refs_2_
  35.2 0.0 collective-permute-done.3.refs_1_
  35.2 0.4 shard_map.119
  35.7 0.1 shard_map.121
  35.8 0.7 collective-permute-start.6
  36.4 0.7 collective-permute-start.7
  37.1 0.7 collective-permute-start.8
  37.8 0.7 collective-permute-start.10
  38.4 0.7 collective-permute-start.11
  39.1 0.0 collective-permute-done.6.refs_0_
  39.1 0.7 collective-permute-start.13
  39.8 0.0 collective-permute-done.7.refs_1_
  39.8 0.7 collective-permute-start.9
  40.5 0.0 collective-permute-done.8.refs_2_
  40.5 0.7 collective-permute-start.12
  41.2 0.0 collective-permute-done.10.refs_4_
  41.2 0.0 collective-permute-done.11.refs_5_
  41.2 0.0 collective-permute-done.13.refs_7_
  41.2 0.0 collective-permute-done.12.refs_6_
  41.2 0.1 shard_map.122
  41.3 0.7 collective-permute-start.14
  42.0 0.7 collective-permute-start.15
  42.7 0.7 collective-permute-start.16
  43.4 0.7 collective-permute-start.18
  44.0 0.7 collective-permute-start.19
  44.7 0.0 collective-permute-done.14.refs_0_
  44.7 0.7 collective-permute-start.21
  45.4 0.0 collective-permute-done.15.refs_1_
  45.4 0.7 collective-permute-start.17
  46.1 0.0 collective-permute-done.16.refs_2_
  46.1 0.7 collective-permute-start.20
  46.8 0.0 collective-permute-done.21.refs_7_
  46.8 0.0 collective-permute-done.17.refs_3_
  46.8 0.0 copy-start
  46.8 0.3 shard_map.123
  47.1 1.3 %collective-permute-start.22 = (bf16[24,2048]{1,0:T(8,128)(2,1)S(1)}, bf16[24,2048]{1,0:T(8,128)(2,1)S(1)}, u32[]{:S(2)}, u32[]{:S(2)}) collective-permute-start(bf16[24,2048]{1,0:T(8,128)(2,1)S(1)} %get-tuple-element.146), channel_id=1, source_target_pairs={{8,0},{9,1},{10,2},{11,3},{12,4},{13,5},{14,6},{15,7}} | collective-permute-start | bytes 294920 | tf_op jit(solution)/shard_map/ppermute | solution.py:376
  48.4 1.3 %collective-permute-start.23 = (bf16[24,2048]{1,0:T(8,128)(2,1)S(1)}, bf16[24,2048]{1,0:T(8,128)(2,1)S(1)}, u32[]{:S(2)}, u32[]{:S(2)}) collective-permute-start(bf16[24,2048]{1,0:T(8,128)(2,1)S(1)} %get-tuple-element.149), channel_id=1, source_target_pairs={{8,1},{9,0},{10,3},{11,2},{12,5},{13,4},{14,7},{15,6}} | collective-permute-start | bytes 294920 | tf_op jit(solution)/shard_map/ppermute | solution.py:376
  49.7 1.3 %collective-permute-start.24 = (bf16[24,2048]{1,0:T(8,128)(2,1)S(1)}, bf16[24,2048]{1,0:T(8,128)(2,1)S(1)}, u32[]{:S(2)}, u32[]{:S(2)}) collective-permute-start(bf16[24,2048]{1,0:T(8,128)(2,1)S(1)} %get-tuple-element.152), channel_id=1, source_target_pairs={{8,2},{9,3},{10,0},{11,1},{12,6},{13,7},{14,4},{15,5}} | collective-permute-start | bytes 294920 | tf_op jit(solution)/shard_map/ppermute | solution.py:376
  51.0 1.3 %collective-permute-start.26 = (bf16[24,2048]{1,0:T(8,128)(2,1)S(1)}, bf16[24,2048]{1,0:T(8,128)(2,1)S(1)}, u32[]{:S(2)}, u32[]{:S(2)}) collective-permute-start(bf16[24,2048]{1,0:T(8,128)(2,1)S(1)} %get-tuple-element.155), channel_id=1, source_target_pairs={{8,4},{9,5},{10,6},{11,7},{12,0},{13,1},{14,2},{15,3}} | collective-permute-start | bytes 294920 | tf_op jit(solution)/shard_map/ppermute | solution.py:376
  52.3 1.3 %collective-permute-start.27 = (bf16[24,2048]{1,0:T(8,128)(2,1)S(1)}, bf16[24,2048]{1,0:T(8,128)(2,1)S(1)}, u32[]{:S(2)}, u32[]{:S(2)}) collective-permute-start(bf16[24,2048]{1,0:T(8,128)(2,1)S(1)} %get-tuple-element.156), channel_id=1, source_target_pairs={{8,5},{9,4},{10,7},{11,6},{12,1},{13,0},{14,3},{15,2}} | collective-permute-start | bytes 294920 | tf_op jit(solution)/shard_map/ppermute | solution.py:376
  53.6 30.4 %collective-permute-done.22.refs_0_ = bf16[24,2048]{1,0:T(8,128)(2,1)S(1)} collective-permute-done((bf16[24,2048]{1,0:T(8,128)(2,1)S(1)}, bf16[24,2048]{1,0:T(8,128)(2,1)S(1)}, u32[]{:S(2)}, u32[]{:S(2)}) %collective-permute-start.22) | collective-permute-done | bytes 98336 | tf_op jit(solution)/shard_map/ppermute | solution.py:376
  84.0 1.3 %collective-permute-start.29 = (bf16[24,2048]{1,0:T(8,128)(2,1)S(1)}, bf16[24,2048]{1,0:T(8,128)(2,1)S(1)}, u32[]{:S(2)}, u32[]{:S(2)}) collective-permute-start(bf16[24,2048]{1,0:T(8,128)(2,1)S(1)} %get-tuple-element.158), channel_id=1, source_target_pairs={{8,7},{9,6},{10,5},{11,4},{12,3},{13,2},{14,1},{15,0}} | collective-permute-start | bytes 294920 | tf_op jit(solution)/shard_map/ppermute | solution.py:376
  85.3 1.9 %collective-permute-done.23.refs_1_ = bf16[24,2048]{1,0:T(8,128)(2,1)S(1)} collective-permute-done((bf16[24,2048]{1,0:T(8,128)(2,1)S(1)}, bf16[24,2048]{1,0:T(8,128)(2,1)S(1)}, u32[]{:S(2)}, u32[]{:S(2)}) %collective-permute-start.23) | collective-permute-done | bytes 98336 | tf_op jit(solution)/shard_map/ppermute | solution.py:376
  87.2 1.3 %collective-permute-start.25 = (bf16[24,2048]{1,0:T(8,128)(2,1)S(1)}, bf16[24,2048]{1,0:T(8,128)(2,1)S(1)}, u32[]{:S(2)}, u32[]{:S(2)}) collective-permute-start(bf16[24,2048]{1,0:T(8,128)(2,1)S(1)} %get-tuple-element.154), channel_id=1, source_target_pairs={{8,3},{9,2},{10,1},{11,0},{12,7},{13,6},{14,5},{15,4}} | collective-permute-start | bytes 294920 | tf_op jit(solution)/shard_map/ppermute | solution.py:376
  88.5 1.3 %collective-permute-done.24.refs_2_ = bf16[24,2048]{1,0:T(8,128)(2,1)S(1)} collective-permute-done((bf16[24,2048]{1,0:T(8,128)(2,1)S(1)}, bf16[24,2048]{1,0:T(8,128)(2,1)S(1)}, u32[]{:S(2)}, u32[]{:S(2)}) %collective-permute-start.24) | collective-permute-done | bytes 98336 | tf_op jit(solution)/shard_map/ppermute | solution.py:376
  89.9 1.3 %collective-permute-start.28 = (bf16[24,2048]{1,0:T(8,128)(2,1)S(1)}, bf16[24,2048]{1,0:T(8,128)(2,1)S(1)}, u32[]{:S(2)}, u32[]{:S(2)}) collective-permute-start(bf16[24,2048]{1,0:T(8,128)(2,1)S(1)} %get-tuple-element.157), channel_id=1, source_target_pairs={{8,6},{9,7},{10,4},{11,5},{12,2},{13,3},{14,0},{15,1}} | collective-permute-start | bytes 294920 | tf_op jit(solution)/shard_map/ppermute | solution.py:376
  91.2 3.2 %collective-permute-done.26.refs_4_ = bf16[24,2048]{1,0:T(8,128)(2,1)S(1)} collective-permute-done((bf16[24,2048]{1,0:T(8,128)(2,1)S(1)}, bf16[24,2048]{1,0:T(8,128)(2,1)S(1)}, u32[]{:S(2)}, u32[]{:S(2)}) %collective-permute-start.26) | collective-permute-done | bytes 98336 | tf_op jit(solution)/shard_map/ppermute | solution.py:376
  94.3 1.3 %collective-permute-done.27.refs_5_ = bf16[24,2048]{1,0:T(8,128)(2,1)S(1)} collective-permute-done((bf16[24,2048]{1,0:T(8,128)(2,1)S(1)}, bf16[24,2048]{1,0:T(8,128)(2,1)S(1)}, u32[]{:S(2)}, u32[]{:S(2)}) %collective-permute-start.27) | collective-permute-done | bytes 98336 | tf_op jit(solution)/shard_map/ppermute | solution.py:376
  95.6 0.0 collective-permute-done.29.refs_7_
  95.6 1.0 collective-permute-done.25.refs_3_
  96.6 1.1 collective-permute-done.28.refs_6_
  97.7 6.1 %shard_map.124 = bf16[64,2048]{1,0:T(8,128)(2,1)} custom-call(bf16[24,2048]{1,0:T(8,128)(2,1)S(1)} %collective-permute-done.22.refs_0_, bf16[24,2048]{1,0:T(8,128)(2,1)S(1)} %collective-permute-done.23.refs_1_, bf16[24,2048]{1,0:T(8,128)(2,1)S(1)} %collective-permute-done.24.refs_2_, bf16[24,2048]{1,0:T(8,128)(2,1)S(1)} %collective-permute-done.25.refs_3_, ...), custom_call_target="tpu_custom_call" | custom-call | tf_op jit(solution)/shard_map/pallas_call | solution.py:63
  103.8 3.4 %all-to-all-start.9 = ((bf16[8,8,2048]{2,1,0:T(8,128)(2,1)}), bf16[8,8,2048]{2,1,0:T(8,128)(2,1)S(1)}, u32[]{:S(2)}, u32[]{:S(2)}) async-start(bf16[8,8,2048]{2,1,0:T(8,128)(2,1)} %bitcast.43), calls=%async_computation.9 | async-start | bytes 524288 | tf_op jit(solution)/shard_map/all_to_all | solution.py:480
  107.2 0.5 slice.33
  108.4 7.0 %all-to-all-done.9 = bf16[8,8,2048]{2,1,0:T(8,128)(2,1)S(1)} async-done(((bf16[8,8,2048]{2,1,0:T(8,128)(2,1)}), bf16[8,8,2048]{2,1,0:T(8,128)(2,1)S(1)}, u32[]{:S(2)}, u32[]{:S(2)}) %all-to-all-start.9) | async-done | bytes 262176 | tf_op jit(solution)/shard_map/all_to_all | solution.py:480
  115.4 0.9 conditional.1
  115.4 0.9 branch_0_fun.1
  (10 shorter events, 0.1 us)
Async XLA Ops:
  24.9 10.3 %collective-permute-start.5 = (f32[8,128]{1,0:T(8,128)S(1)}, f32[8,128]{1,0:T(8,128)S(1)}, u32[]{:S(2)}, u32[]{:S(2)}) collective-permute-start(f32[8,128]{1,0:T(8,128)S(1)} %shard_map.118.refs_0_), channel_id=1, source_target_pairs={{0,8},{8,16},{16,24},{24,0},{1,9},{9,17},{17,25},{25,1},{2,10},{10... | collective-permute-start | bytes 12296 | tf_op jit(solution)/shard_map/ppermute | solution.py:492
  25.0 10.2 %collective-permute-start.4 = (f32[8,128]{1,0:T(8,128)S(1)}, f32[8,128]{1,0:T(8,128)S(1)}, u32[]{:S(2)}, u32[]{:S(2)}) collective-permute-start(f32[8,128]{1,0:T(8,128)S(1)} %shard_map.118.refs_0_), channel_id=1, source_target_pairs={{0,16},{8,24},{16,0},{24,8},{1,17},{9,25},{17,1},{25,9},{2,18},{10... | collective-permute-start | bytes 12296 | tf_op jit(solution)/shard_map/ppermute | solution.py:492
  26.6 8.7 %collective-permute-start.3 = (f32[8,128]{1,0:T(8,128)S(1)}, f32[8,128]{1,0:T(8,128)S(1)}, u32[]{:S(2)}, u32[]{:S(2)}) collective-permute-start(f32[8,128]{1,0:T(8,128)S(1)} %shard_map.118.refs_0_), channel_id=1, source_target_pairs={{0,24},{8,0},{16,8},{24,16},{1,25},{9,1},{17,9},{25,17},{2,26},{10... | collective-permute-start | bytes 12296 | tf_op jit(solution)/shard_map/ppermute | solution.py:492
  35.8 3.4 %collective-permute-start.6 = (bf16[24,2048]{1,0:T(8,128)(2,1)S(1)}, bf16[24,2048]{1,0:T(8,128)(2,1)S(1)}, u32[]{:S(2)}, u32[]{:S(2)}) collective-permute-start(bf16[24,2048]{1,0:T(8,128)(2,1)S(1)} %get-tuple-element.113), channel_id=1, source_target_pairs={{24,16},{25,17},{26,18},{27,19},{28,20},{29,21},{30,22},{31,23}} | collective-permute-start | bytes 294920 | tf_op jit(solution)/shard_map/ppermute | solution.py:376
  36.4 3.4 %collective-permute-start.7 = (bf16[24,2048]{1,0:T(8,128)(2,1)S(1)}, bf16[24,2048]{1,0:T(8,128)(2,1)S(1)}, u32[]{:S(2)}, u32[]{:S(2)}) collective-permute-start(bf16[24,2048]{1,0:T(8,128)(2,1)S(1)} %get-tuple-element.116), channel_id=1, source_target_pairs={{24,17},{25,16},{26,19},{27,18},{28,21},{29,20},{30,23},{31,22}} | collective-permute-start | bytes 294920 | tf_op jit(solution)/shard_map/ppermute | solution.py:376
  37.1 3.4 %collective-permute-start.8 = (bf16[24,2048]{1,0:T(8,128)(2,1)S(1)}, bf16[24,2048]{1,0:T(8,128)(2,1)S(1)}, u32[]{:S(2)}, u32[]{:S(2)}) collective-permute-start(bf16[24,2048]{1,0:T(8,128)(2,1)S(1)} %get-tuple-element.119), channel_id=1, source_target_pairs={{24,18},{25,19},{26,16},{27,17},{28,22},{29,23},{30,20},{31,21}} | collective-permute-start | bytes 294920 | tf_op jit(solution)/shard_map/ppermute | solution.py:376
  37.8 3.4 %collective-permute-start.10 = (bf16[24,2048]{1,0:T(8,128)(2,1)S(1)}, bf16[24,2048]{1,0:T(8,128)(2,1)S(1)}, u32[]{:S(2)}, u32[]{:S(2)}) collective-permute-start(bf16[24,2048]{1,0:T(8,128)(2,1)S(1)} %get-tuple-element.122), channel_id=1, source_target_pairs={{24,20},{25,21},{26,22},{27,23},{28,16},{29,17},{30,18},{31,19}} | collective-permute-start | bytes 294920 | tf_op jit(solution)/shard_map/ppermute | solution.py:376
  38.4 2.7 %collective-permute-start.11 = (bf16[24,2048]{1,0:T(8,128)(2,1)S(1)}, bf16[24,2048]{1,0:T(8,128)(2,1)S(1)}, u32[]{:S(2)}, u32[]{:S(2)}) collective-permute-start(bf16[24,2048]{1,0:T(8,128)(2,1)S(1)} %get-tuple-element.123), channel_id=1, source_target_pairs={{24,21},{25,20},{26,23},{27,22},{28,17},{29,16},{30,19},{31,18}} | collective-permute-start | bytes 294920 | tf_op jit(solution)/shard_map/ppermute | solution.py:376
  39.1 2.1 %collective-permute-start.13 = (bf16[24,2048]{1,0:T(8,128)(2,1)S(1)}, bf16[24,2048]{1,0:T(8,128)(2,1)S(1)}, u32[]{:S(2)}, u32[]{:S(2)}) collective-permute-start(bf16[24,2048]{1,0:T(8,128)(2,1)S(1)} %get-tuple-element.125), channel_id=1, source_target_pairs={{24,23},{25,22},{26,21},{27,20},{28,19},{29,18},{30,17},{31,16}} | collective-permute-start | bytes 294920 | tf_op jit(solution)/shard_map/ppermute | solution.py:376
  39.8 1.4 %collective-permute-start.9 = (bf16[24,2048]{1,0:T(8,128)(2,1)S(1)}, bf16[24,2048]{1,0:T(8,128)(2,1)S(1)}, u32[]{:S(2)}, u32[]{:S(2)}) collective-permute-start(bf16[24,2048]{1,0:T(8,128)(2,1)S(1)} %get-tuple-element.121), channel_id=1, source_target_pairs={{24,19},{25,18},{26,17},{27,16},{28,23},{29,22},{30,21},{31,20}} | collective-permute-start | bytes 294920 | tf_op jit(solution)/shard_map/ppermute | solution.py:376
  40.5 0.7 collective-permute-start.12
  41.3 3.4 %collective-permute-start.14 = (bf16[24,2048]{1,0:T(8,128)(2,1)S(1)}, bf16[24,2048]{1,0:T(8,128)(2,1)S(1)}, u32[]{:S(2)}, u32[]{:S(2)}) collective-permute-start(bf16[24,2048]{1,0:T(8,128)(2,1)S(1)} %get-tuple-element.130), channel_id=1, source_target_pairs={{16,8},{17,9},{18,10},{19,11},{20,12},{21,13},{22,14},{23,15}} | collective-permute-start | bytes 294920 | tf_op jit(solution)/shard_map/ppermute | solution.py:376
  42.0 3.4 %collective-permute-start.15 = (bf16[24,2048]{1,0:T(8,128)(2,1)S(1)}, bf16[24,2048]{1,0:T(8,128)(2,1)S(1)}, u32[]{:S(2)}, u32[]{:S(2)}) collective-permute-start(bf16[24,2048]{1,0:T(8,128)(2,1)S(1)} %get-tuple-element.133), channel_id=1, source_target_pairs={{16,9},{17,8},{18,11},{19,10},{20,13},{21,12},{22,15},{23,14}} | collective-permute-start | bytes 294920 | tf_op jit(solution)/shard_map/ppermute | solution.py:376
  42.7 3.4 %collective-permute-start.16 = (bf16[24,2048]{1,0:T(8,128)(2,1)S(1)}, bf16[24,2048]{1,0:T(8,128)(2,1)S(1)}, u32[]{:S(2)}, u32[]{:S(2)}) collective-permute-start(bf16[24,2048]{1,0:T(8,128)(2,1)S(1)} %get-tuple-element.136), channel_id=1, source_target_pairs={{16,10},{17,11},{18,8},{19,9},{20,14},{21,15},{22,12},{23,13}} | collective-permute-start | bytes 294920 | tf_op jit(solution)/shard_map/ppermute | solution.py:376
  43.4 3.4 %collective-permute-start.18 = (bf16[24,2048]{1,0:T(8,128)(2,1)S(1)}, bf16[24,2048]{1,0:T(8,128)(2,1)S(1)}, u32[]{:S(2)}, u32[]{:S(2)}) collective-permute-start(bf16[24,2048]{1,0:T(8,128)(2,1)S(1)} %get-tuple-element.139), channel_id=1, source_target_pairs={{16,12},{17,13},{18,14},{19,15},{20,8},{21,9},{22,10},{23,11}} | collective-permute-start | bytes 294920 | tf_op jit(solution)/shard_map/ppermute | solution.py:376
  44.0 2.7 %collective-permute-start.19 = (bf16[24,2048]{1,0:T(8,128)(2,1)S(1)}, bf16[24,2048]{1,0:T(8,128)(2,1)S(1)}, u32[]{:S(2)}, u32[]{:S(2)}) collective-permute-start(bf16[24,2048]{1,0:T(8,128)(2,1)S(1)} %get-tuple-element.140), channel_id=1, source_target_pairs={{16,13},{17,12},{18,15},{19,14},{20,9},{21,8},{22,11},{23,10}} | collective-permute-start | bytes 294920 | tf_op jit(solution)/shard_map/ppermute | solution.py:376
  44.7 2.1 %collective-permute-start.21 = (bf16[24,2048]{1,0:T(8,128)(2,1)S(1)}, bf16[24,2048]{1,0:T(8,128)(2,1)S(1)}, u32[]{:S(2)}, u32[]{:S(2)}) collective-permute-start(bf16[24,2048]{1,0:T(8,128)(2,1)S(1)} %get-tuple-element.142), channel_id=1, source_target_pairs={{16,15},{17,14},{18,13},{19,12},{20,11},{21,10},{22,9},{23,8}} | collective-permute-start | bytes 294920 | tf_op jit(solution)/shard_map/ppermute | solution.py:376
  45.4 1.4 %collective-permute-start.17 = (bf16[24,2048]{1,0:T(8,128)(2,1)S(1)}, bf16[24,2048]{1,0:T(8,128)(2,1)S(1)}, u32[]{:S(2)}, u32[]{:S(2)}) collective-permute-start(bf16[24,2048]{1,0:T(8,128)(2,1)S(1)} %get-tuple-element.138), channel_id=1, source_target_pairs={{16,11},{17,10},{18,9},{19,8},{20,15},{21,14},{22,13},{23,12}} | collective-permute-start | bytes 294920 | tf_op jit(solution)/shard_map/ppermute | solution.py:376
  46.1 0.7 collective-permute-start.20
  46.8 50.9 %copy-start = (bf16[64,64]{1,0:T(8,128)(2,1)S(1)}, bf16[64,64]{1,0:T(8,128)(2,1)}, u32[]{:S(2)}) copy-start(bf16[64,64]{1,0:T(8,128)(2,1)} %get-tuple-element.161.refs_17_) | copy-start | bytes 24580
  47.1 36.9 %collective-permute-start.22 = (bf16[24,2048]{1,0:T(8,128)(2,1)S(1)}, bf16[24,2048]{1,0:T(8,128)(2,1)S(1)}, u32[]{:S(2)}, u32[]{:S(2)}) collective-permute-start(bf16[24,2048]{1,0:T(8,128)(2,1)S(1)} %get-tuple-element.146), channel_id=1, source_target_pairs={{8,0},{9,1},{10,2},{11,3},{12,4},{13,5},{14,6},{15,7}} | collective-permute-start | bytes 294920 | tf_op jit(solution)/shard_map/ppermute | solution.py:376
  48.4 38.8 %collective-permute-start.23 = (bf16[24,2048]{1,0:T(8,128)(2,1)S(1)}, bf16[24,2048]{1,0:T(8,128)(2,1)S(1)}, u32[]{:S(2)}, u32[]{:S(2)}) collective-permute-start(bf16[24,2048]{1,0:T(8,128)(2,1)S(1)} %get-tuple-element.149), channel_id=1, source_target_pairs={{8,1},{9,0},{10,3},{11,2},{12,5},{13,4},{14,7},{15,6}} | collective-permute-start | bytes 294920 | tf_op jit(solution)/shard_map/ppermute | solution.py:376
  49.7 40.2 %collective-permute-start.24 = (bf16[24,2048]{1,0:T(8,128)(2,1)S(1)}, bf16[24,2048]{1,0:T(8,128)(2,1)S(1)}, u32[]{:S(2)}, u32[]{:S(2)}) collective-permute-start(bf16[24,2048]{1,0:T(8,128)(2,1)S(1)} %get-tuple-element.152), channel_id=1, source_target_pairs={{8,2},{9,3},{10,0},{11,1},{12,6},{13,7},{14,4},{15,5}} | collective-permute-start | bytes 294920 | tf_op jit(solution)/shard_map/ppermute | solution.py:376
  51.0 43.3 %collective-permute-start.26 = (bf16[24,2048]{1,0:T(8,128)(2,1)S(1)}, bf16[24,2048]{1,0:T(8,128)(2,1)S(1)}, u32[]{:S(2)}, u32[]{:S(2)}) collective-permute-start(bf16[24,2048]{1,0:T(8,128)(2,1)S(1)} %get-tuple-element.155), channel_id=1, source_target_pairs={{8,4},{9,5},{10,6},{11,7},{12,0},{13,1},{14,2},{15,3}} | collective-permute-start | bytes 294920 | tf_op jit(solution)/shard_map/ppermute | solution.py:376
  52.3 43.3 %collective-permute-start.27 = (bf16[24,2048]{1,0:T(8,128)(2,1)S(1)}, bf16[24,2048]{1,0:T(8,128)(2,1)S(1)}, u32[]{:S(2)}, u32[]{:S(2)}) collective-permute-start(bf16[24,2048]{1,0:T(8,128)(2,1)S(1)} %get-tuple-element.156), channel_id=1, source_target_pairs={{8,5},{9,4},{10,7},{11,6},{12,1},{13,0},{14,3},{15,2}} | collective-permute-start | bytes 294920 | tf_op jit(solution)/shard_map/ppermute | solution.py:376
  84.0 11.6 %collective-permute-start.29 = (bf16[24,2048]{1,0:T(8,128)(2,1)S(1)}, bf16[24,2048]{1,0:T(8,128)(2,1)S(1)}, u32[]{:S(2)}, u32[]{:S(2)}) collective-permute-start(bf16[24,2048]{1,0:T(8,128)(2,1)S(1)} %get-tuple-element.158), channel_id=1, source_target_pairs={{8,7},{9,6},{10,5},{11,4},{12,3},{13,2},{14,1},{15,0}} | collective-permute-start | bytes 294920 | tf_op jit(solution)/shard_map/ppermute | solution.py:376
  87.2 9.3 %collective-permute-start.25 = (bf16[24,2048]{1,0:T(8,128)(2,1)S(1)}, bf16[24,2048]{1,0:T(8,128)(2,1)S(1)}, u32[]{:S(2)}, u32[]{:S(2)}) collective-permute-start(bf16[24,2048]{1,0:T(8,128)(2,1)S(1)} %get-tuple-element.154), channel_id=1, source_target_pairs={{8,3},{9,2},{10,1},{11,0},{12,7},{13,6},{14,5},{15,4}} | collective-permute-start | bytes 294920 | tf_op jit(solution)/shard_map/ppermute | solution.py:376
  89.9 7.8 %collective-permute-start.28 = (bf16[24,2048]{1,0:T(8,128)(2,1)S(1)}, bf16[24,2048]{1,0:T(8,128)(2,1)S(1)}, u32[]{:S(2)}, u32[]{:S(2)}) collective-permute-start(bf16[24,2048]{1,0:T(8,128)(2,1)S(1)} %get-tuple-element.157), channel_id=1, source_target_pairs={{8,6},{9,7},{10,4},{11,5},{12,2},{13,3},{14,0},{15,1}} | collective-permute-start | bytes 294920 | tf_op jit(solution)/shard_map/ppermute | solution.py:376
  97.7 17.7 %copy-start.3 = (bf16[1,2048,64]{1,2,0:T(8,128)(2,1)S(1)}, bf16[1,2048,64]{1,2,0:T(8,128)(2,1)}, u32[]{:S(2)}) copy-start(bf16[1,2048,64]{1,2,0:T(8,128)(2,1)} %param.21) | copy-start | bytes 786436
  97.7 17.7 %copy-start.10 = (bf16[1,1536,64]{1,2,0:T(8,128)(2,1)S(1)}, bf16[1,1536,64]{1,2,0:T(8,128)(2,1)}, u32[]{:S(2)}) copy-start(bf16[1,1536,64]{1,2,0:T(8,128)(2,1)} %param.20) | copy-start | bytes 589828
  103.8 11.6 %all-to-all-start.9 = ((bf16[8,8,2048]{2,1,0:T(8,128)(2,1)}), bf16[8,8,2048]{2,1,0:T(8,128)(2,1)S(1)}, u32[]{:S(2)}, u32[]{:S(2)}) async-start(bf16[8,8,2048]{2,1,0:T(8,128)(2,1)} %bitcast.43), calls=%async_computation.9 | async-start | bytes 524288 | tf_op jit(solution)/shard_map/all_to_all | solution.py:480

commit v5 on v4

--- a/solution.py
+++ b/solution.py
@@ -16,7 +16,6 @@
 NARROW = (1536, 1)
 WIDEN = (2048, 1)
 FORWARD = 512
-SKETCH = (2048, 1)
 
 F32 = jnp.float32
 BF16 = jnp.bfloat16
@@ -246,7 +245,8 @@
     top_ref[...] = both[:, block:].reshape(n_rows, feat).astype(BF16)
     x = both[:, :block].reshape(n_rows, feat).astype(BF16)
     copies[0].wait()
-    left = jnp.zeros(left_ref.shape, F32)
+    size = left_map.shape[1]
+    left = jnp.zeros((n_rows, size), F32)
     for number in range(hidden // tile):
         part = slice(number * tile, (number + 1) * tile)
         copies[2 * number + 1].wait()
@@ -258,7 +258,11 @@
         to_up_ref[:, part] = silu
         to_gate_ref[:, part] = up * sigmoid * (1.0 + gate * (1.0 - sigmoid))
         left = left + contract((silu * up).astype(BF16), left_map[0, :, part], 1, 1)
-    left_ref[...] = left.astype(BF16)
+    left = left.astype(BF16)
+    for at in range(0, left_ref.shape[1], feat):
+        lane, axis = at + iota((size, feat), 1), iota((size, feat), 0)
+        over_left = ones_where(axis == lane // size).astype(BF16)
+        left_ref[:, at : at + feat] = contract(left, over_left, 1, 0).astype(BF16)
     for copy in copies[-2:]:
         copy.wait()
 
@@ -323,21 +327,17 @@
     right = contract(rows_now[...], right_proj[0], 1, 1)
     high = right.astype(BF16)
     low = (right - high.astype(F32)).astype(BF16)
-    left = left_ref[...]
-    size = left.shape[1]
-    tile = math.gcd(feat, SKETCH[0])
-    lane, axis = iota((size, tile), 1), iota((size, tile), 0)
-    over_right = ones_where(axis == lane % size).astype(BF16)
+    size = right.shape[1]
+    width = math.gcd(feat, 2 * LANES)
+    over_right = iota((size, width), 0) == iota((size, width), 1) % size
+    over_right = ones_where(over_right).astype(BF16)
     right = contract(high, over_right, 1, 0) + contract(low, over_right, 1, 0)
+    right = jnp.concatenate([right] * (feat // width), axis=1)
     for number in range(n_extra):
-
-        def add_terms(part, number=number):
-            over_left = ones_where(axis == (number * feat + part.start + lane) // size)
-            outer = contract(left, over_left.astype(BF16), 1, 0) * right
-            terms = contract(sketch[number], outer.astype(BF16), 1, 0)
-            part_ref[:, part] = (part_ref[:, part].astype(F32) + terms).astype(BF16)
-
-        over_tiles(feat, SKETCH, add_terms)
+        part = slice(number * feat, (number + 1) * feat)
+        outer = left_ref[:, part].astype(F32) * right
+        terms = contract(sketch[number], outer.astype(BF16), 1, 0)
+        part_ref[...] = (part_ref[...].astype(F32) + terms).astype(BF16)
 
 
 def finish(n_expert, block, used, n_extra, q_dev, back_ref, slots_ref, grad_ref, sketch_ref):
@@ -468,11 +468,11 @@
     )
     send, slots = call(
         functools.partial(prepare, n_section, n_expert, block),
-        (shape(2 * n_rows, feat), shape(n_rows, tokens)),
+        (pltpu.VMEM((2 * n_rows, feat), BF16), shape(n_rows, tokens)),
         arrays,
         HBM,
         [pltpu.VMEM(a.shape, a.dtype) for a in arrays] + [pltpu.SemaphoreType.DMA((5,))],
-        60 << 20,
+        58 << 20,
     )
 
     def exchange(rows):
@@ -498,7 +498,7 @@
         out_shape=(
             pltpu.VMEM((n_rows, hidden), F32),
             pltpu.VMEM((n_rows, hidden), F32),
-            shape(n_rows, sketch_dim),
+            pltpu.VMEM((n_rows, n_extra * feat), BF16),
             shape(n_rows, feat),
         )
         + tuple(pltpu.VMEM(stored[i].shape, BF16) for i in (0, 1, 2, 4)),
@@ -544,7 +544,7 @@
         inputs += [down, to_gate, to_up, gate, up, cols]
         if last:
             inputs += [rows, part, left, right_map, sketch]
-            out = (shape(n_rows, feat),)
+            out = (pltpu.VMEM((n_rows, feat), BF16),)
         else:
             inputs += [comp] + ([rows, part] if stage > 0 else [])
             out = tuple(shape(share, feat) for _ in range(n_expert))

time: 117 us -> 115 us (0.983)
  Pallas kernels: 17.6 us -> 16.2 us
where the time goes in v5:
time: 115 us
  waiting for transfers between devices  47.3 us (41%)
  starting transfers between devices  27.4 us (24%)
  blocking collectives  21.6 us (19%)
  Pallas kernels  16.2 us (14%)
  between operations  1.71 us (1%)
    ppermute x24, waiting for transfers between devices, send_down(): arrived[turn] = lax.ppermute(block, ('section', 'expert'), pairs)  40.3 us
    all_to_all x1, blocking collectives, exchange(): lax.all_to_all(blocks, 'expert', split_axis=0, concat_axis=0, tiled=True)  21.6 us
    ppermute x24, starting transfers between devices, send_down(): arrived[turn] = lax.ppermute(block, ('section', 'expert'), pairs)  21 us
    pallas_call x8, Pallas kernels, call(): pl.pallas_call(kernel, out_shape=out_shape, in_specs=[spec] * len(inputs)...  9.32 us
    all_to_all x1, waiting for transfers between devices, exchange(): lax.all_to_all(blocks, 'expert', split_axis=0, concat_axis=0, tiled=True)  6.99 us
    pallas_call x1, Pallas kernels, on_device(): pl.pallas_call(functools.partial(forward, block), out_shape=(pltpu.VMEM((...  6.84 us
    all_to_all x1, starting transfers between devices, exchange(): lax.all_to_all(blocks, 'expert', split_axis=0, concat_axis=0, tiled=True)  3.41 us
    ppermute x3, starting transfers between devices, on_device(): around.append(lax.ppermute(fields, 'section', pairs))  3.03 us
  transfers between devices with their start and end apart: 28, of which 8 were waited for; matrix products, arithmetic and copies ran while one was open for 0% of the time, Pallas kernels for 6%

profile of v5, /device:TPU:0, one launch (start us, length us, event | category | flops | bytes accessed | tf_op | source)
XLA Modules:
  0.0 114.7 jit_solution(10176523352873088249)
XLA Ops:
  0.6 1.7 %shard_map.117 = (bf16[128,2048]{1,0:T(8,128)(2,1)S(1)}, bf16[64,16]{1,0:T(8,128)(2,1)S(1)}) custom-call(s32[1,2,2,8]{3,2,1,0:T(2,128)} %bitcast.208, bf16[1,2,2,8]{3,2,1,0:T(2,128)(2,1)} %bitcast.209, s32[2,8]{1,0:T(2,128)} %ex_hbm.1, bf16[1,2,8,2048]{3,2,1,0:T(8,128)(2,1)} %x_hbm.1, bf16[2,8,2048]{2,1,0:T(8,128)(2,1)} %top_hbm.1), custom_call_target="tpu_custom_call" | custom-call | tf_op jit(solution)/shard_map/pallas_call | solution.py:62
  2.3 21.6 %all_to_all.46 = bf16[8,16,2048]{2,1,0:T(8,128)(2,1)S(1)} all-to-all(bf16[8,16,2048]{2,1,0:T(8,128)(2,1)S(1)} %bitcast.199), channel_id=1, replica_groups=mesh['section'=4,'expert'=8] {'expert'}, dimensions={0} | all-to-all | bytes 1048576 | tf_op jit(solution)/shard_map/all_to_all | solution.py:480
  23.9 0.1 collective-permute-start.5
  24.0 1.6 %collective-permute-start.4 = (f32[8,128]{1,0:T(8,128)S(1)}, f32[8,128]{1,0:T(8,128)S(1)}, u32[]{:S(2)}, u32[]{:S(2)}) collective-permute-start(f32[8,128]{1,0:T(8,128)S(1)} %shard_map.118.refs_0_), channel_id=1, source_target_pairs={{0,16},{8,24},{16,0},{24,8},{1,17},{9,25},{17,1},{25,9},{2,18},{10... | collective-permute-start | bytes 12296 | tf_op jit(solution)/shard_map/ppermute | solution.py:492
  25.6 1.4 %collective-permute-start.3 = (f32[8,128]{1,0:T(8,128)S(1)}, f32[8,128]{1,0:T(8,128)S(1)}, u32[]{:S(2)}, u32[]{:S(2)}) collective-permute-start(f32[8,128]{1,0:T(8,128)S(1)} %shard_map.118.refs_0_), channel_id=1, source_target_pairs={{0,24},{8,0},{16,8},{24,16},{1,25},{9,1},{17,9},{25,17},{2,26},{10... | collective-permute-start | bytes 12296 | tf_op jit(solution)/shard_map/ppermute | solution.py:492
  26.9 6.8 %shard_map.120 = (f32[64,1536]{1,0:T(8,128)S(1)}, f32[64,1536]{1,0:T(8,128)S(1)}, bf16[64,4096]{1,0:T(8,128)(2,1)S(1)}, bf16[64,2048]{1,0:T(8,128)(2,1)S(1)}, bf...) custom-call(bf16[128,2048]{1,0:T(8,128)(2,1)S(1)} %bitcast.203, ...), custom_call_target="tpu_custom_call" | custom-call | tf_op jit(solution)/shard_map/pallas_call | solution.py:496
  33.8 0.0 collective-permute-done.5.refs_3_
  33.8 0.0 collective-permute-done.4.refs_2_
  33.8 0.0 collective-permute-done.3.refs_1_
  33.8 0.4 shard_map.119
  34.3 0.1 shard_map.121
  34.3 0.7 collective-permute-start.6
  35.0 0.7 collective-permute-start.7
  35.7 0.7 collective-permute-start.8
  36.4 0.7 collective-permute-start.10
  37.0 0.7 collective-permute-start.11
  37.7 0.0 collective-permute-done.6.refs_0_
  37.7 0.7 collective-permute-start.13
  38.4 0.0 collective-permute-done.7.refs_1_
  38.4 0.7 collective-permute-start.9
  39.1 0.0 collective-permute-done.8.refs_2_
  39.1 0.7 collective-permute-start.12
  39.8 0.0 collective-permute-done.10.refs_4_
  39.8 0.0 collective-permute-done.11.refs_5_
  39.8 0.0 collective-permute-done.13.refs_7_
  39.8 0.0 collective-permute-done.9.refs_3_
  39.8 0.0 collective-permute-done.12.refs_6_
  39.8 0.1 shard_map.122
  39.9 0.7 collective-permute-start.14
  40.6 0.7 collective-permute-start.15
  41.3 0.7 collective-permute-start.16
  41.9 0.7 collective-permute-start.18
  42.6 0.7 collective-permute-start.19
  43.3 0.0 collective-permute-done.14.refs_0_
  43.3 0.7 collective-permute-start.21
  44.0 0.0 collective-permute-done.15.refs_1_
  44.0 0.7 collective-permute-start.17
  44.7 0.7 collective-permute-start.20
  45.4 0.0 collective-permute-done.18.refs_4_
  45.4 0.0 collective-permute-done.19.refs_5_
  45.4 0.0 collective-permute-done.17.refs_3_
  45.4 0.0 collective-permute-done.20.refs_6_
  45.4 0.3 shard_map.123
  45.7 1.3 %collective-permute-start.22 = (bf16[24,2048]{1,0:T(8,128)(2,1)S(1)}, bf16[24,2048]{1,0:T(8,128)(2,1)S(1)}, u32[]{:S(2)}, u32[]{:S(2)}) collective-permute-start(bf16[24,2048]{1,0:T(8,128)(2,1)S(1)} %get-tuple-element.146), channel_id=1, source_target_pairs={{8,0},{9,1},{10,2},{11,3},{12,4},{13,5},{14,6},{15,7}} | collective-permute-start | bytes 294920 | tf_op jit(solution)/shard_map/ppermute | solution.py:376
  47.0 1.3 %collective-permute-start.23 = (bf16[24,2048]{1,0:T(8,128)(2,1)S(1)}, bf16[24,2048]{1,0:T(8,128)(2,1)S(1)}, u32[]{:S(2)}, u32[]{:S(2)}) collective-permute-start(bf16[24,2048]{1,0:T(8,128)(2,1)S(1)} %get-tuple-element.149), channel_id=1, source_target_pairs={{8,1},{9,0},{10,3},{11,2},{12,5},{13,4},{14,7},{15,6}} | collective-permute-start | bytes 294920 | tf_op jit(solution)/shard_map/ppermute | solution.py:376
  48.3 1.3 %collective-permute-start.24 = (bf16[24,2048]{1,0:T(8,128)(2,1)S(1)}, bf16[24,2048]{1,0:T(8,128)(2,1)S(1)}, u32[]{:S(2)}, u32[]{:S(2)}) collective-permute-start(bf16[24,2048]{1,0:T(8,128)(2,1)S(1)} %get-tuple-element.152), channel_id=1, source_target_pairs={{8,2},{9,3},{10,0},{11,1},{12,6},{13,7},{14,4},{15,5}} | collective-permute-start | bytes 294920 | tf_op jit(solution)/shard_map/ppermute | solution.py:376
  49.6 1.3 %collective-permute-start.26 = (bf16[24,2048]{1,0:T(8,128)(2,1)S(1)}, bf16[24,2048]{1,0:T(8,128)(2,1)S(1)}, u32[]{:S(2)}, u32[]{:S(2)}) collective-permute-start(bf16[24,2048]{1,0:T(8,128)(2,1)S(1)} %get-tuple-element.155), channel_id=1, source_target_pairs={{8,4},{9,5},{10,6},{11,7},{12,0},{13,1},{14,2},{15,3}} | collective-permute-start | bytes 294920 | tf_op jit(solution)/shard_map/ppermute | solution.py:376
  50.9 1.3 %collective-permute-start.27 = (bf16[24,2048]{1,0:T(8,128)(2,1)S(1)}, bf16[24,2048]{1,0:T(8,128)(2,1)S(1)}, u32[]{:S(2)}, u32[]{:S(2)}) collective-permute-start(bf16[24,2048]{1,0:T(8,128)(2,1)S(1)} %get-tuple-element.156), channel_id=1, source_target_pairs={{8,5},{9,4},{10,7},{11,6},{12,1},{13,0},{14,3},{15,2}} | collective-permute-start | bytes 294920 | tf_op jit(solution)/shard_map/ppermute | solution.py:376
  52.2 30.6 %collective-permute-done.22.refs_0_ = bf16[24,2048]{1,0:T(8,128)(2,1)S(1)} collective-permute-done((bf16[24,2048]{1,0:T(8,128)(2,1)S(1)}, bf16[24,2048]{1,0:T(8,128)(2,1)S(1)}, u32[]{:S(2)}, u32[]{:S(2)}) %collective-permute-start.22) | collective-permute-done | bytes 98336 | tf_op jit(solution)/shard_map/ppermute | solution.py:376
  82.8 1.3 %collective-permute-start.29 = (bf16[24,2048]{1,0:T(8,128)(2,1)S(1)}, bf16[24,2048]{1,0:T(8,128)(2,1)S(1)}, u32[]{:S(2)}, u32[]{:S(2)}) collective-permute-start(bf16[24,2048]{1,0:T(8,128)(2,1)S(1)} %get-tuple-element.158), channel_id=1, source_target_pairs={{8,7},{9,6},{10,5},{11,4},{12,3},{13,2},{14,1},{15,0}} | collective-permute-start | bytes 294920 | tf_op jit(solution)/shard_map/ppermute | solution.py:376
  84.1 1.9 %collective-permute-done.23.refs_1_ = bf16[24,2048]{1,0:T(8,128)(2,1)S(1)} collective-permute-done((bf16[24,2048]{1,0:T(8,128)(2,1)S(1)}, bf16[24,2048]{1,0:T(8,128)(2,1)S(1)}, u32[]{:S(2)}, u32[]{:S(2)}) %collective-permute-start.23) | collective-permute-done | bytes 98336 | tf_op jit(solution)/shard_map/ppermute | solution.py:376
  86.0 1.3 %collective-permute-start.25 = (bf16[24,2048]{1,0:T(8,128)(2,1)S(1)}, bf16[24,2048]{1,0:T(8,128)(2,1)S(1)}, u32[]{:S(2)}, u32[]{:S(2)}) collective-permute-start(bf16[24,2048]{1,0:T(8,128)(2,1)S(1)} %get-tuple-element.154), channel_id=1, source_target_pairs={{8,3},{9,2},{10,1},{11,0},{12,7},{13,6},{14,5},{15,4}} | collective-permute-start | bytes 294920 | tf_op jit(solution)/shard_map/ppermute | solution.py:376
  87.3 1.2 %collective-permute-done.24.refs_2_ = bf16[24,2048]{1,0:T(8,128)(2,1)S(1)} collective-permute-done((bf16[24,2048]{1,0:T(8,128)(2,1)S(1)}, bf16[24,2048]{1,0:T(8,128)(2,1)S(1)}, u32[]{:S(2)}, u32[]{:S(2)}) %collective-permute-start.24) | collective-permute-done | bytes 98336 | tf_op jit(solution)/shard_map/ppermute | solution.py:376
  88.5 1.3 %collective-permute-start.28 = (bf16[24,2048]{1,0:T(8,128)(2,1)S(1)}, bf16[24,2048]{1,0:T(8,128)(2,1)S(1)}, u32[]{:S(2)}, u32[]{:S(2)}) collective-permute-start(bf16[24,2048]{1,0:T(8,128)(2,1)S(1)} %get-tuple-element.157), channel_id=1, source_target_pairs={{8,6},{9,7},{10,4},{11,5},{12,2},{13,3},{14,0},{15,1}} | collective-permute-start | bytes 294920 | tf_op jit(solution)/shard_map/ppermute | solution.py:376
  89.7 2.9 %collective-permute-done.26.refs_4_ = bf16[24,2048]{1,0:T(8,128)(2,1)S(1)} collective-permute-done((bf16[24,2048]{1,0:T(8,128)(2,1)S(1)}, bf16[24,2048]{1,0:T(8,128)(2,1)S(1)}, u32[]{:S(2)}, u32[]{:S(2)}) %collective-permute-start.26) | collective-permute-done | bytes 98336 | tf_op jit(solution)/shard_map/ppermute | solution.py:376
  92.6 1.3 %collective-permute-done.27.refs_5_ = bf16[24,2048]{1,0:T(8,128)(2,1)S(1)} collective-permute-done((bf16[24,2048]{1,0:T(8,128)(2,1)S(1)}, bf16[24,2048]{1,0:T(8,128)(2,1)S(1)}, u32[]{:S(2)}, u32[]{:S(2)}) %collective-permute-start.27) | collective-permute-done | bytes 98336 | tf_op jit(solution)/shard_map/ppermute | solution.py:376
  94.0 1.0 collective-permute-done.25.refs_3_
  94.9 1.4 %collective-permute-done.28.refs_6_ = bf16[24,2048]{1,0:T(8,128)(2,1)S(1)} collective-permute-done((bf16[24,2048]{1,0:T(8,128)(2,1)S(1)}, bf16[24,2048]{1,0:T(8,128)(2,1)S(1)}, u32[]{:S(2)}, u32[]{:S(2)}) %collective-permute-start.28) | collective-permute-done | bytes 98336 | tf_op jit(solution)/shard_map/ppermute | solution.py:376
  96.3 5.8 %shard_map.124 = bf16[64,2048]{1,0:T(8,128)(2,1)} custom-call(bf16[24,2048]{1,0:T(8,128)(2,1)S(1)} %collective-permute-done.22.refs_0_, bf16[24,2048]{1,0:T(8,128)(2,1)S(1)} %collective-permute-done.23.refs_1_, bf16[24,2048]{1,0:T(8,128)(2,1)S(1)} %collective-permute-done.24.refs_2_, bf16[24,2048]{1,0:T(8,128)(2,1)S(1)} %collective-permute-done.25.refs_3_, ...), custom_call_target="tpu_custom_call" | custom-call | tf_op jit(solution)/shard_map/pallas_call | solution.py:62
  102.1 3.4 %all-to-all-start.9 = ((bf16[8,8,2048]{2,1,0:T(8,128)(2,1)}), bf16[8,8,2048]{2,1,0:T(8,128)(2,1)S(1)}, u32[]{:S(2)}, u32[]{:S(2)}) async-start(bf16[8,8,2048]{2,1,0:T(8,128)(2,1)} %bitcast.43), calls=%async_computation.9 | async-start | bytes 524288 | tf_op jit(solution)/shard_map/all_to_all | solution.py:480
  105.6 0.5 slice.33
  106.7 7.0 %all-to-all-done.9 = bf16[8,8,2048]{2,1,0:T(8,128)(2,1)S(1)} async-done(((bf16[8,8,2048]{2,1,0:T(8,128)(2,1)}), bf16[8,8,2048]{2,1,0:T(8,128)(2,1)S(1)}, u32[]{:S(2)}, u32[]{:S(2)}) %all-to-all-start.9) | async-done | bytes 262176 | tf_op jit(solution)/shard_map/all_to_all | solution.py:480
  113.7 0.9 conditional.1
  113.7 0.9 branch_0_fun.1
  (10 shorter events, 0.1 us)
Async XLA Ops:
  23.9 9.9 %collective-permute-start.5 = (f32[8,128]{1,0:T(8,128)S(1)}, f32[8,128]{1,0:T(8,128)S(1)}, u32[]{:S(2)}, u32[]{:S(2)}) collective-permute-start(f32[8,128]{1,0:T(8,128)S(1)} %shard_map.118.refs_0_), channel_id=1, source_target_pairs={{0,8},{8,16},{16,24},{24,0},{1,9},{9,17},{17,25},{25,1},{2,10},{10... | collective-permute-start | bytes 12296 | tf_op jit(solution)/shard_map/ppermute | solution.py:492
  24.0 9.8 %collective-permute-start.4 = (f32[8,128]{1,0:T(8,128)S(1)}, f32[8,128]{1,0:T(8,128)S(1)}, u32[]{:S(2)}, u32[]{:S(2)}) collective-permute-start(f32[8,128]{1,0:T(8,128)S(1)} %shard_map.118.refs_0_), channel_id=1, source_target_pairs={{0,16},{8,24},{16,0},{24,8},{1,17},{9,25},{17,1},{25,9},{2,18},{10... | collective-permute-start | bytes 12296 | tf_op jit(solution)/shard_map/ppermute | solution.py:492
  25.6 8.3 %collective-permute-start.3 = (f32[8,128]{1,0:T(8,128)S(1)}, f32[8,128]{1,0:T(8,128)S(1)}, u32[]{:S(2)}, u32[]{:S(2)}) collective-permute-start(f32[8,128]{1,0:T(8,128)S(1)} %shard_map.118.refs_0_), channel_id=1, source_target_pairs={{0,24},{8,0},{16,8},{24,16},{1,25},{9,1},{17,9},{25,17},{2,26},{10... | collective-permute-start | bytes 12296 | tf_op jit(solution)/shard_map/ppermute | solution.py:492
  34.3 62.0 %copy-start.10 = (bf16[2,64,64]{2,1,0:T(8,128)(2,1)}, bf16[2,64,64]{2,1,0:T(8,128)(2,1)S(1)}, u32[]{:S(2)}) copy-start(bf16[2,64,64]{2,1,0:T(8,128)(2,1)S(1)} %get-tuple-element.163.refs_19_) | copy-start | bytes 49156
  34.3 3.4 %collective-permute-start.6 = (bf16[24,2048]{1,0:T(8,128)(2,1)S(1)}, bf16[24,2048]{1,0:T(8,128)(2,1)S(1)}, u32[]{:S(2)}, u32[]{:S(2)}) collective-permute-start(bf16[24,2048]{1,0:T(8,128)(2,1)S(1)} %get-tuple-element.113), channel_id=1, source_target_pairs={{24,16},{25,17},{26,18},{27,19},{28,20},{29,21},{30,22},{31,23}} | collective-permute-start | bytes 294920 | tf_op jit(solution)/shard_map/ppermute | solution.py:376
  35.0 3.4 %collective-permute-start.7 = (bf16[24,2048]{1,0:T(8,128)(2,1)S(1)}, bf16[24,2048]{1,0:T(8,128)(2,1)S(1)}, u32[]{:S(2)}, u32[]{:S(2)}) collective-permute-start(bf16[24,2048]{1,0:T(8,128)(2,1)S(1)} %get-tuple-element.116), channel_id=1, source_target_pairs={{24,17},{25,16},{26,19},{27,18},{28,21},{29,20},{30,23},{31,22}} | collective-permute-start | bytes 294920 | tf_op jit(solution)/shard_map/ppermute | solution.py:376
  35.7 3.4 %collective-permute-start.8 = (bf16[24,2048]{1,0:T(8,128)(2,1)S(1)}, bf16[24,2048]{1,0:T(8,128)(2,1)S(1)}, u32[]{:S(2)}, u32[]{:S(2)}) collective-permute-start(bf16[24,2048]{1,0:T(8,128)(2,1)S(1)} %get-tuple-element.119), channel_id=1, source_target_pairs={{24,18},{25,19},{26,16},{27,17},{28,22},{29,23},{30,20},{31,21}} | collective-permute-start | bytes 294920 | tf_op jit(solution)/shard_map/ppermute | solution.py:376
  36.4 3.4 %collective-permute-start.10 = (bf16[24,2048]{1,0:T(8,128)(2,1)S(1)}, bf16[24,2048]{1,0:T(8,128)(2,1)S(1)}, u32[]{:S(2)}, u32[]{:S(2)}) collective-permute-start(bf16[24,2048]{1,0:T(8,128)(2,1)S(1)} %get-tuple-element.122), channel_id=1, source_target_pairs={{24,20},{25,21},{26,22},{27,23},{28,16},{29,17},{30,18},{31,19}} | collective-permute-start | bytes 294920 | tf_op jit(solution)/shard_map/ppermute | solution.py:376
  37.0 2.7 %collective-permute-start.11 = (bf16[24,2048]{1,0:T(8,128)(2,1)S(1)}, bf16[24,2048]{1,0:T(8,128)(2,1)S(1)}, u32[]{:S(2)}, u32[]{:S(2)}) collective-permute-start(bf16[24,2048]{1,0:T(8,128)(2,1)S(1)} %get-tuple-element.123), channel_id=1, source_target_pairs={{24,21},{25,20},{26,23},{27,22},{28,17},{29,16},{30,19},{31,18}} | collective-permute-start | bytes 294920 | tf_op jit(solution)/shard_map/ppermute | solution.py:376
  37.7 2.1 %collective-permute-start.13 = (bf16[24,2048]{1,0:T(8,128)(2,1)S(1)}, bf16[24,2048]{1,0:T(8,128)(2,1)S(1)}, u32[]{:S(2)}, u32[]{:S(2)}) collective-permute-start(bf16[24,2048]{1,0:T(8,128)(2,1)S(1)} %get-tuple-element.125), channel_id=1, source_target_pairs={{24,23},{25,22},{26,21},{27,20},{28,19},{29,18},{30,17},{31,16}} | collective-permute-start | bytes 294920 | tf_op jit(solution)/shard_map/ppermute | solution.py:376
  38.4 1.4 %collective-permute-start.9 = (bf16[24,2048]{1,0:T(8,128)(2,1)S(1)}, bf16[24,2048]{1,0:T(8,128)(2,1)S(1)}, u32[]{:S(2)}, u32[]{:S(2)}) collective-permute-start(bf16[24,2048]{1,0:T(8,128)(2,1)S(1)} %get-tuple-element.121), channel_id=1, source_target_pairs={{24,19},{25,18},{26,17},{27,16},{28,23},{29,22},{30,21},{31,20}} | collective-permute-start | bytes 294920 | tf_op jit(solution)/shard_map/ppermute | solution.py:376
  39.1 0.7 collective-permute-start.12
  39.9 3.4 %collective-permute-start.14 = (bf16[24,2048]{1,0:T(8,128)(2,1)S(1)}, bf16[24,2048]{1,0:T(8,128)(2,1)S(1)}, u32[]{:S(2)}, u32[]{:S(2)}) collective-permute-start(bf16[24,2048]{1,0:T(8,128)(2,1)S(1)} %get-tuple-element.130), channel_id=1, source_target_pairs={{16,8},{17,9},{18,10},{19,11},{20,12},{21,13},{22,14},{23,15}} | collective-permute-start | bytes 294920 | tf_op jit(solution)/shard_map/ppermute | solution.py:376
  40.6 3.4 %collective-permute-start.15 = (bf16[24,2048]{1,0:T(8,128)(2,1)S(1)}, bf16[24,2048]{1,0:T(8,128)(2,1)S(1)}, u32[]{:S(2)}, u32[]{:S(2)}) collective-permute-start(bf16[24,2048]{1,0:T(8,128)(2,1)S(1)} %get-tuple-element.133), channel_id=1, source_target_pairs={{16,9},{17,8},{18,11},{19,10},{20,13},{21,12},{22,15},{23,14}} | collective-permute-start | bytes 294920 | tf_op jit(solution)/shard_map/ppermute | solution.py:376
  41.3 3.4 %collective-permute-start.16 = (bf16[24,2048]{1,0:T(8,128)(2,1)S(1)}, bf16[24,2048]{1,0:T(8,128)(2,1)S(1)}, u32[]{:S(2)}, u32[]{:S(2)}) collective-permute-start(bf16[24,2048]{1,0:T(8,128)(2,1)S(1)} %get-tuple-element.136), channel_id=1, source_target_pairs={{16,10},{17,11},{18,8},{19,9},{20,14},{21,15},{22,12},{23,13}} | collective-permute-start | bytes 294920 | tf_op jit(solution)/shard_map/ppermute | solution.py:376
  41.9 3.4 %collective-permute-start.18 = (bf16[24,2048]{1,0:T(8,128)(2,1)S(1)}, bf16[24,2048]{1,0:T(8,128)(2,1)S(1)}, u32[]{:S(2)}, u32[]{:S(2)}) collective-permute-start(bf16[24,2048]{1,0:T(8,128)(2,1)S(1)} %get-tuple-element.139), channel_id=1, source_target_pairs={{16,12},{17,13},{18,14},{19,15},{20,8},{21,9},{22,10},{23,11}} | collective-permute-start | bytes 294920 | tf_op jit(solution)/shard_map/ppermute | solution.py:376
  42.6 2.7 %collective-permute-start.19 = (bf16[24,2048]{1,0:T(8,128)(2,1)S(1)}, bf16[24,2048]{1,0:T(8,128)(2,1)S(1)}, u32[]{:S(2)}, u32[]{:S(2)}) collective-permute-start(bf16[24,2048]{1,0:T(8,128)(2,1)S(1)} %get-tuple-element.140), channel_id=1, source_target_pairs={{16,13},{17,12},{18,15},{19,14},{20,9},{21,8},{22,11},{23,10}} | collective-permute-start | bytes 294920 | tf_op jit(solution)/shard_map/ppermute | solution.py:376
  43.3 2.1 %collective-permute-start.21 = (bf16[24,2048]{1,0:T(8,128)(2,1)S(1)}, bf16[24,2048]{1,0:T(8,128)(2,1)S(1)}, u32[]{:S(2)}, u32[]{:S(2)}) collective-permute-start(bf16[24,2048]{1,0:T(8,128)(2,1)S(1)} %get-tuple-element.142), channel_id=1, source_target_pairs={{16,15},{17,14},{18,13},{19,12},{20,11},{21,10},{22,9},{23,8}} | collective-permute-start | bytes 294920 | tf_op jit(solution)/shard_map/ppermute | solution.py:376
  44.0 1.4 %collective-permute-start.17 = (bf16[24,2048]{1,0:T(8,128)(2,1)S(1)}, bf16[24,2048]{1,0:T(8,128)(2,1)S(1)}, u32[]{:S(2)}, u32[]{:S(2)}) collective-permute-start(bf16[24,2048]{1,0:T(8,128)(2,1)S(1)} %get-tuple-element.138), channel_id=1, source_target_pairs={{16,11},{17,10},{18,9},{19,8},{20,15},{21,14},{22,13},{23,12}} | collective-permute-start | bytes 294920 | tf_op jit(solution)/shard_map/ppermute | solution.py:376
  44.7 0.7 collective-permute-start.20
  45.7 37.1 %collective-permute-start.22 = (bf16[24,2048]{1,0:T(8,128)(2,1)S(1)}, bf16[24,2048]{1,0:T(8,128)(2,1)S(1)}, u32[]{:S(2)}, u32[]{:S(2)}) collective-permute-start(bf16[24,2048]{1,0:T(8,128)(2,1)S(1)} %get-tuple-element.146), channel_id=1, source_target_pairs={{8,0},{9,1},{10,2},{11,3},{12,4},{13,5},{14,6},{15,7}} | collective-permute-start | bytes 294920 | tf_op jit(solution)/shard_map/ppermute | solution.py:376
  47.0 39.0 %collective-permute-start.23 = (bf16[24,2048]{1,0:T(8,128)(2,1)S(1)}, bf16[24,2048]{1,0:T(8,128)(2,1)S(1)}, u32[]{:S(2)}, u32[]{:S(2)}) collective-permute-start(bf16[24,2048]{1,0:T(8,128)(2,1)S(1)} %get-tuple-element.149), channel_id=1, source_target_pairs={{8,1},{9,0},{10,3},{11,2},{12,5},{13,4},{14,7},{15,6}} | collective-permute-start | bytes 294920 | tf_op jit(solution)/shard_map/ppermute | solution.py:376
  48.3 40.2 %collective-permute-start.24 = (bf16[24,2048]{1,0:T(8,128)(2,1)S(1)}, bf16[24,2048]{1,0:T(8,128)(2,1)S(1)}, u32[]{:S(2)}, u32[]{:S(2)}) collective-permute-start(bf16[24,2048]{1,0:T(8,128)(2,1)S(1)} %get-tuple-element.152), channel_id=1, source_target_pairs={{8,2},{9,3},{10,0},{11,1},{12,6},{13,7},{14,4},{15,5}} | collective-permute-start | bytes 294920 | tf_op jit(solution)/shard_map/ppermute | solution.py:376
  49.6 43.0 %collective-permute-start.26 = (bf16[24,2048]{1,0:T(8,128)(2,1)S(1)}, bf16[24,2048]{1,0:T(8,128)(2,1)S(1)}, u32[]{:S(2)}, u32[]{:S(2)}) collective-permute-start(bf16[24,2048]{1,0:T(8,128)(2,1)S(1)} %get-tuple-element.155), channel_id=1, source_target_pairs={{8,4},{9,5},{10,6},{11,7},{12,0},{13,1},{14,2},{15,3}} | collective-permute-start | bytes 294920 | tf_op jit(solution)/shard_map/ppermute | solution.py:376
  50.9 43.1 %collective-permute-start.27 = (bf16[24,2048]{1,0:T(8,128)(2,1)S(1)}, bf16[24,2048]{1,0:T(8,128)(2,1)S(1)}, u32[]{:S(2)}, u32[]{:S(2)}) collective-permute-start(bf16[24,2048]{1,0:T(8,128)(2,1)S(1)} %get-tuple-element.156), channel_id=1, source_target_pairs={{8,5},{9,4},{10,7},{11,6},{12,1},{13,0},{14,3},{15,2}} | collective-permute-start | bytes 294920 | tf_op jit(solution)/shard_map/ppermute | solution.py:376
  82.8 11.2 %collective-permute-start.29 = (bf16[24,2048]{1,0:T(8,128)(2,1)S(1)}, bf16[24,2048]{1,0:T(8,128)(2,1)S(1)}, u32[]{:S(2)}, u32[]{:S(2)}) collective-permute-start(bf16[24,2048]{1,0:T(8,128)(2,1)S(1)} %get-tuple-element.158), channel_id=1, source_target_pairs={{8,7},{9,6},{10,5},{11,4},{12,3},{13,2},{14,1},{15,0}} | collective-permute-start | bytes 294920 | tf_op jit(solution)/shard_map/ppermute | solution.py:376
  86.0 9.0 %collective-permute-start.25 = (bf16[24,2048]{1,0:T(8,128)(2,1)S(1)}, bf16[24,2048]{1,0:T(8,128)(2,1)S(1)}, u32[]{:S(2)}, u32[]{:S(2)}) collective-permute-start(bf16[24,2048]{1,0:T(8,128)(2,1)S(1)} %get-tuple-element.154), channel_id=1, source_target_pairs={{8,3},{9,2},{10,1},{11,0},{12,7},{13,6},{14,5},{15,4}} | collective-permute-start | bytes 294920 | tf_op jit(solution)/shard_map/ppermute | solution.py:376
  88.5 7.8 %collective-permute-start.28 = (bf16[24,2048]{1,0:T(8,128)(2,1)S(1)}, bf16[24,2048]{1,0:T(8,128)(2,1)S(1)}, u32[]{:S(2)}, u32[]{:S(2)}) collective-permute-start(bf16[24,2048]{1,0:T(8,128)(2,1)S(1)} %get-tuple-element.157), channel_id=1, source_target_pairs={{8,6},{9,7},{10,4},{11,5},{12,2},{13,3},{14,0},{15,1}} | collective-permute-start | bytes 294920 | tf_op jit(solution)/shard_map/ppermute | solution.py:376
  96.3 17.4 %copy-start.2 = (bf16[1,2048,64]{1,2,0:T(8,128)(2,1)S(1)}, bf16[1,2048,64]{1,2,0:T(8,128)(2,1)}, u32[]{:S(2)}) copy-start(bf16[1,2048,64]{1,2,0:T(8,128)(2,1)} %param.21) | copy-start | bytes 786436
  96.3 17.4 %copy-start.9 = (bf16[1,1536,64]{1,2,0:T(8,128)(2,1)S(1)}, bf16[1,1536,64]{1,2,0:T(8,128)(2,1)}, u32[]{:S(2)}) copy-start(bf16[1,1536,64]{1,2,0:T(8,128)(2,1)} %param.20) | copy-start | bytes 589828
  102.1 11.6 %all-to-all-start.9 = ((bf16[8,8,2048]{2,1,0:T(8,128)(2,1)}), bf16[8,8,2048]{2,1,0:T(8,128)(2,1)S(1)}, u32[]{:S(2)}, u32[]{:S(2)}) async-start(bf16[8,8,2048]{2,1,0:T(8,128)(2,1)} %bitcast.43), calls=%async_computation.9 | async-start | bytes 524288 | tf_op jit(solution)/shard_map/all_to_all | solution.py:480

commit v6 on v5

--- a/solution.py
+++ b/solution.py
@@ -340,6 +340,13 @@
         part_ref[...] = (part_ref[...].astype(F32) + terms).astype(BF16)
 
 
+def plan_and_layer(planner, layers, n_around, *refs):
+    around, inputs, refs = refs[:n_around], refs[n_around : n_around + 6], refs[n_around + 6 :]
+    comp, place, cols, sketch, over = refs[:5]
+    planner(*around, comp, place, cols, sketch, over)
+    layers(*inputs, cols, comp, *refs[5:])
+
+
 def finish(n_expert, block, used, n_extra, q_dev, back_ref, slots_ref, grad_ref, sketch_ref):
     me = lax.axis_index("expert")
     hsplit = n_expert // EXPERTS
@@ -510,21 +517,6 @@
         ],
         compiler_params=pltpu.CompilerParams(vmem_limit_bytes=38 << 20),
     )(both, *stored)
-    comp, place, cols, sketch, over = call(
-        functools.partial(
-            plan, n_section, n_expert, n_micro, tok_dev, top_k, block, share, q_dev
-        ),
-        (
-            shape(n_picks, n_rows),
-            shape(n_rows, n_picks),
-            shape(n_rows, LANES, dtype=F32),
-            shape(n_extra, n_rows, n_rows),
-            shape(8, LANES, dtype=F32),
-        ),
-        around,
-        limit=(12 << 20) + 16 * n_rows * n_picks,
-    )
-
     raw = (top_grad, gate_weight, up_weight, down_weight, left_proj, right_proj)
 
     def crowded(*_):
@@ -533,7 +525,19 @@
             block, used, n_extra, q_dev, raw, slots, x_rows, top_rows, cols, sketch
         )
 
+    planner = functools.partial(
+        plan, n_section, n_expert, n_micro, tok_dev, top_k, block, share, q_dev
+    )
+    plan_out = (
+        shape(n_picks, n_rows),
+        shape(n_rows, n_picks),
+        shape(n_rows, LANES, dtype=F32),
+        shape(n_extra, n_rows, n_rows),
+        shape(8, LANES, dtype=F32),
+    )
     if n_expert > MOST_PERMUTES:
+        limit = (12 << 20) + 16 * n_rows * n_picks
+        _, _, cols, sketch, _ = call(planner, plan_out, around, limit=limit)
         return crowded()
 
     rows, part = None, None
@@ -541,18 +545,23 @@
     for stage in range(n_section):
         last = stage == n_section - 1
         inputs = list(arrived) + ([place] if stage > 0 else [])
-        inputs += [down, to_gate, to_up, gate, up, cols]
+        inputs += [down, to_gate, to_up, gate, up] + ([cols] if stage else [])
         if last:
             inputs += [rows, part, left, right_map, sketch]
             out = (pltpu.VMEM((n_rows, feat), BF16),)
         else:
-            inputs += [comp] + ([rows, part] if stage > 0 else [])
+            inputs += [comp, rows, part] if stage else []
             out = tuple(shape(share, feat) for _ in range(n_expert))
             out += (shape(n_rows, feat), shape(n_rows, feat))
+        kernel = functools.partial(
+            layer, len(arrived), 0 if last else n_expert, stage > 0, stage, n_section, n_extra
+        )
+        if not stage:
+            kernel = functools.partial(plan_and_layer, planner, kernel, n_section)
+            inputs = [*around, *arrived, down, to_gate, to_up, gate, up]
+            out = plan_out + out
         results = call(
-            functools.partial(
-                layer, len(arrived), 0 if last else n_expert, stage > 0, stage, n_section, n_extra
-            ),
+            kernel,
             out,
             inputs,
             scratch=[
@@ -562,6 +571,9 @@
             ],
             limit=16 << 20,
         )
+        if not stage:
+            comp, place, cols, sketch, over = results[:5]
+            results = results[5:]
         if last:
             back = exchange(results[0])
             break

time: 115 us -> 115 us (level)
    pallas_call x8 -> x7, Pallas kernels: 9.32 us -> 9.31 us  [call(): pl.pallas_call(kernel, out_shape=out_shape, in_specs=[spec] * len(inputs)...]
where the time goes in v6:
time: 115 us
  waiting for transfers between devices  47.3 us (41%)
  starting transfers between devices  27.4 us (24%)
  blocking collectives  21.6 us (19%)
  Pallas kernels  16.1 us (14%)
  between operations  1.7 us (1%)
    ppermute x24, waiting for transfers between devices, send_down(): arrived[turn] = lax.ppermute(block, ('section', 'expert'), pairs)  40.3 us
    all_to_all x1, blocking collectives, exchange(): lax.all_to_all(blocks, 'expert', split_axis=0, concat_axis=0, tiled=True)  21.6 us
    ppermute x24, starting transfers between devices, send_down(): arrived[turn] = lax.ppermute(block, ('section', 'expert'), pairs)  21 us
    pallas_call x7, Pallas kernels, call(): pl.pallas_call(kernel, out_shape=out_shape, in_specs=[spec] * len(inputs)...  9.31 us
    all_to_all x1, waiting for transfers between devices, exchange(): lax.all_to_all(blocks, 'expert', split_axis=0, concat_axis=0, tiled=True)  6.99 us
    pallas_call x1, Pallas kernels, on_device(): pl.pallas_call(functools.partial(forward, block), out_shape=(pltpu.VMEM((...  6.84 us
    all_to_all x1, starting transfers between devices, exchange(): lax.all_to_all(blocks, 'expert', split_axis=0, concat_axis=0, tiled=True)  3.41 us
    ppermute x3, starting transfers between devices, on_device(): around.append(lax.ppermute(fields, 'section', pairs))  3.03 us
  transfers between devices with their start and end apart: 28, of which 8 were waited for; matrix products, arithmetic and copies ran while one was open for 0% of the time, Pallas kernels for 6%

profile of v6, /device:TPU:0, one launch (start us, length us, event | category | flops | bytes accessed | tf_op | source)
XLA Modules:
  0.0 114.6 jit_solution(2140897732964107334)
XLA Ops:
  0.6 1.7 %shard_map.117 = (bf16[128,2048]{1,0:T(8,128)(2,1)S(1)}, bf16[64,16]{1,0:T(8,128)(2,1)S(1)}) custom-call(s32[1,2,2,8]{3,2,1,0:T(2,128)} %bitcast.208, bf16[1,2,2,8]{3,2,1,0:T(2,128)(2,1)} %bitcast.209, s32[2,8]{1,0:T(2,128)} %ex_hbm.1, bf16[1,2,8,2048]{3,2,1,0:T(8,128)(2,1)} %x_hbm.1, bf16[2,8,2048]{2,1,0:T(8,128)(2,1)} %top_hbm.1), custom_call_target="tpu_custom_call" | custom-call | tf_op jit(solution)/shard_map/pallas_call | solution.py:62
  2.3 21.6 %all_to_all.46 = bf16[8,16,2048]{2,1,0:T(8,128)(2,1)S(1)} all-to-all(bf16[8,16,2048]{2,1,0:T(8,128)(2,1)S(1)} %bitcast.199), channel_id=1, replica_groups=mesh['section'=4,'expert'=8] {'expert'}, dimensions={0} | all-to-all | bytes 1048576 | tf_op jit(solution)/shard_map/all_to_all | solution.py:487
  23.9 0.1 collective-permute-start.5
  24.0 1.6 %collective-permute-start.4 = (f32[8,128]{1,0:T(8,128)S(1)}, f32[8,128]{1,0:T(8,128)S(1)}, u32[]{:S(2)}, u32[]{:S(2)}) collective-permute-start(f32[8,128]{1,0:T(8,128)S(1)} %shard_map.118.refs_0_), channel_id=1, source_target_pairs={{0,16},{8,24},{16,0},{24,8},{1,17},{9,25},{17,1},{25,9},{2,18},{10... | collective-permute-start | bytes 12296 | tf_op jit(solution)/shard_map/ppermute | solution.py:499
  25.6 1.4 %collective-permute-start.3 = (f32[8,128]{1,0:T(8,128)S(1)}, f32[8,128]{1,0:T(8,128)S(1)}, u32[]{:S(2)}, u32[]{:S(2)}) collective-permute-start(f32[8,128]{1,0:T(8,128)S(1)} %shard_map.118.refs_0_), channel_id=1, source_target_pairs={{0,24},{8,0},{16,8},{24,16},{1,25},{9,1},{17,9},{25,17},{2,26},{10... | collective-permute-start | bytes 12296 | tf_op jit(solution)/shard_map/ppermute | solution.py:499
  26.9 6.8 %shard_map.119 = (f32[64,1536]{1,0:T(8,128)S(1)}, f32[64,1536]{1,0:T(8,128)S(1)}, bf16[64,4096]{1,0:T(8,128)(2,1)S(1)}, bf16[64,2048]{1,0:T(8,128)(2,1)S(1)}, bf...) custom-call(bf16[128,2048]{1,0:T(8,128)(2,1)S(1)} %bitcast.203, ...), custom_call_target="tpu_custom_call" | custom-call | tf_op jit(solution)/shard_map/pallas_call | solution.py:503
  33.8 0.0 collective-permute-done.5.refs_3_
  33.8 0.0 collective-permute-done.4.refs_2_
  33.8 0.0 collective-permute-done.3.refs_1_
  33.8 0.5 shard_map.120
  34.3 0.7 collective-permute-start.6
  35.0 0.7 collective-permute-start.7
  35.7 0.7 collective-permute-start.8
  36.3 0.7 collective-permute-start.10
  37.0 0.7 collective-permute-start.11
  37.7 0.0 collective-permute-done.6.refs_0_
  37.7 0.7 collective-permute-start.13
  38.4 0.0 collective-permute-done.7.refs_1_
  38.4 0.7 collective-permute-start.9
  39.1 0.0 collective-permute-done.8.refs_2_
  39.1 0.7 collective-permute-start.12
  39.8 0.0 collective-permute-done.10.refs_4_
  39.8 0.0 collective-permute-done.11.refs_5_
  39.8 0.0 collective-permute-done.13.refs_7_
  39.8 0.0 collective-permute-done.9.refs_3_
  39.8 0.0 collective-permute-done.12.refs_6_
  39.8 0.1 shard_map.121
  39.9 0.7 collective-permute-start.14
  40.6 0.7 collective-permute-start.15
  41.3 0.7 collective-permute-start.16
  41.9 0.7 collective-permute-start.18
  42.6 0.7 collective-permute-start.19
  43.3 0.0 collective-permute-done.14.refs_0_
  43.3 0.7 collective-permute-start.21
  44.0 0.0 collective-permute-done.15.refs_1_
  44.0 0.7 collective-permute-start.17
  44.6 0.0 collective-permute-done.16.refs_2_
  44.7 0.7 collective-permute-start.20
  45.3 0.0 collective-permute-done.18.refs_4_
  45.3 0.0 collective-permute-done.19.refs_5_
  45.4 0.0 collective-permute-done.21.refs_7_
  45.4 0.0 collective-permute-done.20.refs_6_
  45.4 0.3 shard_map.122
  45.7 1.3 %collective-permute-start.22 = (bf16[24,2048]{1,0:T(8,128)(2,1)S(1)}, bf16[24,2048]{1,0:T(8,128)(2,1)S(1)}, u32[]{:S(2)}, u32[]{:S(2)}) collective-permute-start(bf16[24,2048]{1,0:T(8,128)(2,1)S(1)} %get-tuple-element.146), channel_id=1, source_target_pairs={{8,0},{9,1},{10,2},{11,3},{12,4},{13,5},{14,6},{15,7}} | collective-permute-start | bytes 294920 | tf_op jit(solution)/shard_map/ppermute | solution.py:383
  47.0 1.3 %collective-permute-start.23 = (bf16[24,2048]{1,0:T(8,128)(2,1)S(1)}, bf16[24,2048]{1,0:T(8,128)(2,1)S(1)}, u32[]{:S(2)}, u32[]{:S(2)}) collective-permute-start(bf16[24,2048]{1,0:T(8,128)(2,1)S(1)} %get-tuple-element.149), channel_id=1, source_target_pairs={{8,1},{9,0},{10,3},{11,2},{12,5},{13,4},{14,7},{15,6}} | collective-permute-start | bytes 294920 | tf_op jit(solution)/shard_map/ppermute | solution.py:383
  48.3 1.3 %collective-permute-start.24 = (bf16[24,2048]{1,0:T(8,128)(2,1)S(1)}, bf16[24,2048]{1,0:T(8,128)(2,1)S(1)}, u32[]{:S(2)}, u32[]{:S(2)}) collective-permute-start(bf16[24,2048]{1,0:T(8,128)(2,1)S(1)} %get-tuple-element.152), channel_id=1, source_target_pairs={{8,2},{9,3},{10,0},{11,1},{12,6},{13,7},{14,4},{15,5}} | collective-permute-start | bytes 294920 | tf_op jit(solution)/shard_map/ppermute | solution.py:383
  49.6 1.3 %collective-permute-start.26 = (bf16[24,2048]{1,0:T(8,128)(2,1)S(1)}, bf16[24,2048]{1,0:T(8,128)(2,1)S(1)}, u32[]{:S(2)}, u32[]{:S(2)}) collective-permute-start(bf16[24,2048]{1,0:T(8,128)(2,1)S(1)} %get-tuple-element.155), channel_id=1, source_target_pairs={{8,4},{9,5},{10,6},{11,7},{12,0},{13,1},{14,2},{15,3}} | collective-permute-start | bytes 294920 | tf_op jit(solution)/shard_map/ppermute | solution.py:383
  50.9 1.3 %collective-permute-start.27 = (bf16[24,2048]{1,0:T(8,128)(2,1)S(1)}, bf16[24,2048]{1,0:T(8,128)(2,1)S(1)}, u32[]{:S(2)}, u32[]{:S(2)}) collective-permute-start(bf16[24,2048]{1,0:T(8,128)(2,1)S(1)} %get-tuple-element.156), channel_id=1, source_target_pairs={{8,5},{9,4},{10,7},{11,6},{12,1},{13,0},{14,3},{15,2}} | collective-permute-start | bytes 294920 | tf_op jit(solution)/shard_map/ppermute | solution.py:383
  52.2 30.6 %collective-permute-done.22.refs_0_ = bf16[24,2048]{1,0:T(8,128)(2,1)S(1)} collective-permute-done((bf16[24,2048]{1,0:T(8,128)(2,1)S(1)}, bf16[24,2048]{1,0:T(8,128)(2,1)S(1)}, u32[]{:S(2)}, u32[]{:S(2)}) %collective-permute-start.22) | collective-permute-done | bytes 98336 | tf_op jit(solution)/shard_map/ppermute | solution.py:383
  82.8 1.3 %collective-permute-start.29 = (bf16[24,2048]{1,0:T(8,128)(2,1)S(1)}, bf16[24,2048]{1,0:T(8,128)(2,1)S(1)}, u32[]{:S(2)}, u32[]{:S(2)}) collective-permute-start(bf16[24,2048]{1,0:T(8,128)(2,1)S(1)} %get-tuple-element.158), channel_id=1, source_target_pairs={{8,7},{9,6},{10,5},{11,4},{12,3},{13,2},{14,1},{15,0}} | collective-permute-start | bytes 294920 | tf_op jit(solution)/shard_map/ppermute | solution.py:383
  84.1 1.9 %collective-permute-done.23.refs_1_ = bf16[24,2048]{1,0:T(8,128)(2,1)S(1)} collective-permute-done((bf16[24,2048]{1,0:T(8,128)(2,1)S(1)}, bf16[24,2048]{1,0:T(8,128)(2,1)S(1)}, u32[]{:S(2)}, u32[]{:S(2)}) %collective-permute-start.23) | collective-permute-done | bytes 98336 | tf_op jit(solution)/shard_map/ppermute | solution.py:383
  85.9 1.3 %collective-permute-start.25 = (bf16[24,2048]{1,0:T(8,128)(2,1)S(1)}, bf16[24,2048]{1,0:T(8,128)(2,1)S(1)}, u32[]{:S(2)}, u32[]{:S(2)}) collective-permute-start(bf16[24,2048]{1,0:T(8,128)(2,1)S(1)} %get-tuple-element.154), channel_id=1, source_target_pairs={{8,3},{9,2},{10,1},{11,0},{12,7},{13,6},{14,5},{15,4}} | collective-permute-start | bytes 294920 | tf_op jit(solution)/shard_map/ppermute | solution.py:383
  87.2 1.2 %collective-permute-done.24.refs_2_ = bf16[24,2048]{1,0:T(8,128)(2,1)S(1)} collective-permute-done((bf16[24,2048]{1,0:T(8,128)(2,1)S(1)}, bf16[24,2048]{1,0:T(8,128)(2,1)S(1)}, u32[]{:S(2)}, u32[]{:S(2)}) %collective-permute-start.24) | collective-permute-done | bytes 98336 | tf_op jit(solution)/shard_map/ppermute | solution.py:383
  88.4 1.3 %collective-permute-start.28 = (bf16[24,2048]{1,0:T(8,128)(2,1)S(1)}, bf16[24,2048]{1,0:T(8,128)(2,1)S(1)}, u32[]{:S(2)}, u32[]{:S(2)}) collective-permute-start(bf16[24,2048]{1,0:T(8,128)(2,1)S(1)} %get-tuple-element.157), channel_id=1, source_target_pairs={{8,6},{9,7},{10,4},{11,5},{12,2},{13,3},{14,0},{15,1}} | collective-permute-start | bytes 294920 | tf_op jit(solution)/shard_map/ppermute | solution.py:383
  89.7 2.9 %collective-permute-done.26.refs_4_ = bf16[24,2048]{1,0:T(8,128)(2,1)S(1)} collective-permute-done((bf16[24,2048]{1,0:T(8,128)(2,1)S(1)}, bf16[24,2048]{1,0:T(8,128)(2,1)S(1)}, u32[]{:S(2)}, u32[]{:S(2)}) %collective-permute-start.26) | collective-permute-done | bytes 98336 | tf_op jit(solution)/shard_map/ppermute | solution.py:383
  92.6 1.3 %collective-permute-done.27.refs_5_ = bf16[24,2048]{1,0:T(8,128)(2,1)S(1)} collective-permute-done((bf16[24,2048]{1,0:T(8,128)(2,1)S(1)}, bf16[24,2048]{1,0:T(8,128)(2,1)S(1)}, u32[]{:S(2)}, u32[]{:S(2)}) %collective-permute-start.27) | collective-permute-done | bytes 98336 | tf_op jit(solution)/shard_map/ppermute | solution.py:383
  93.9 1.0 collective-permute-done.25.refs_3_
  94.9 1.4 %collective-permute-done.28.refs_6_ = bf16[24,2048]{1,0:T(8,128)(2,1)S(1)} collective-permute-done((bf16[24,2048]{1,0:T(8,128)(2,1)S(1)}, bf16[24,2048]{1,0:T(8,128)(2,1)S(1)}, u32[]{:S(2)}, u32[]{:S(2)}) %collective-permute-start.28) | collective-permute-done | bytes 98336 | tf_op jit(solution)/shard_map/ppermute | solution.py:383
  96.3 5.9 %shard_map.123 = bf16[64,2048]{1,0:T(8,128)(2,1)} custom-call(bf16[24,2048]{1,0:T(8,128)(2,1)S(1)} %collective-permute-done.22.refs_0_, bf16[24,2048]{1,0:T(8,128)(2,1)S(1)} %collective-permute-done.23.refs_1_, bf16[24,2048]{1,0:T(8,128)(2,1)S(1)} %collective-permute-done.24.refs_2_, bf16[24,2048]{1,0:T(8,128)(2,1)S(1)} %collective-permute-done.25.refs_3_, ...), custom_call_target="tpu_custom_call" | custom-call | tf_op jit(solution)/shard_map/pallas_call | solution.py:62
  102.1 3.4 %all-to-all-start.9 = ((bf16[8,8,2048]{2,1,0:T(8,128)(2,1)}), bf16[8,8,2048]{2,1,0:T(8,128)(2,1)S(1)}, u32[]{:S(2)}, u32[]{:S(2)}) async-start(bf16[8,8,2048]{2,1,0:T(8,128)(2,1)} %bitcast.43), calls=%async_computation.9 | async-start | bytes 524288 | tf_op jit(solution)/shard_map/all_to_all | solution.py:487
  105.5 0.5 slice.33
  106.7 7.0 %all-to-all-done.9 = bf16[8,8,2048]{2,1,0:T(8,128)(2,1)S(1)} async-done(((bf16[8,8,2048]{2,1,0:T(8,128)(2,1)}), bf16[8,8,2048]{2,1,0:T(8,128)(2,1)S(1)}, u32[]{:S(2)}, u32[]{:S(2)}) %all-to-all-start.9) | async-done | bytes 262176 | tf_op jit(solution)/shard_map/all_to_all | solution.py:487
  113.7 0.9 conditional.1
  113.7 0.9 branch_0_fun.1
  (9 shorter events, 0.0 us)
Async XLA Ops:
  23.9 9.9 %collective-permute-start.5 = (f32[8,128]{1,0:T(8,128)S(1)}, f32[8,128]{1,0:T(8,128)S(1)}, u32[]{:S(2)}, u32[]{:S(2)}) collective-permute-start(f32[8,128]{1,0:T(8,128)S(1)} %shard_map.118.refs_0_), channel_id=1, source_target_pairs={{0,8},{8,16},{16,24},{24,0},{1,9},{9,17},{17,25},{25,1},{2,10},{10... | collective-permute-start | bytes 12296 | tf_op jit(solution)/shard_map/ppermute | solution.py:499
  24.0 9.8 %collective-permute-start.4 = (f32[8,128]{1,0:T(8,128)S(1)}, f32[8,128]{1,0:T(8,128)S(1)}, u32[]{:S(2)}, u32[]{:S(2)}) collective-permute-start(f32[8,128]{1,0:T(8,128)S(1)} %shard_map.118.refs_0_), channel_id=1, source_target_pairs={{0,16},{8,24},{16,0},{24,8},{1,17},{9,25},{17,1},{25,9},{2,18},{10... | collective-permute-start | bytes 12296 | tf_op jit(solution)/shard_map/ppermute | solution.py:499
  25.6 8.3 %collective-permute-start.3 = (f32[8,128]{1,0:T(8,128)S(1)}, f32[8,128]{1,0:T(8,128)S(1)}, u32[]{:S(2)}, u32[]{:S(2)}) collective-permute-start(f32[8,128]{1,0:T(8,128)S(1)} %shard_map.118.refs_0_), channel_id=1, source_target_pairs={{0,24},{8,0},{16,8},{24,16},{1,25},{9,1},{17,9},{25,17},{2,26},{10... | collective-permute-start | bytes 12296 | tf_op jit(solution)/shard_map/ppermute | solution.py:499
  34.3 62.0 %copy-start.10 = (bf16[2,64,64]{2,1,0:T(8,128)(2,1)}, bf16[2,64,64]{2,1,0:T(8,128)(2,1)S(1)}, u32[]{:S(2)}) copy-start(bf16[2,64,64]{2,1,0:T(8,128)(2,1)S(1)} %get-tuple-element.163.refs_19_) | copy-start | bytes 49156
  34.3 3.4 %collective-permute-start.6 = (bf16[24,2048]{1,0:T(8,128)(2,1)S(1)}, bf16[24,2048]{1,0:T(8,128)(2,1)S(1)}, u32[]{:S(2)}, u32[]{:S(2)}) collective-permute-start(bf16[24,2048]{1,0:T(8,128)(2,1)S(1)} %get-tuple-element.111), channel_id=1, source_target_pairs={{24,16},{25,17},{26,18},{27,19},{28,20},{29,21},{30,22},{31,23}} | collective-permute-start | bytes 294920 | tf_op jit(solution)/shard_map/ppermute | solution.py:383
  35.0 3.4 %collective-permute-start.7 = (bf16[24,2048]{1,0:T(8,128)(2,1)S(1)}, bf16[24,2048]{1,0:T(8,128)(2,1)S(1)}, u32[]{:S(2)}, u32[]{:S(2)}) collective-permute-start(bf16[24,2048]{1,0:T(8,128)(2,1)S(1)} %get-tuple-element.114), channel_id=1, source_target_pairs={{24,17},{25,16},{26,19},{27,18},{28,21},{29,20},{30,23},{31,22}} | collective-permute-start | bytes 294920 | tf_op jit(solution)/shard_map/ppermute | solution.py:383
  35.7 3.4 %collective-permute-start.8 = (bf16[24,2048]{1,0:T(8,128)(2,1)S(1)}, bf16[24,2048]{1,0:T(8,128)(2,1)S(1)}, u32[]{:S(2)}, u32[]{:S(2)}) collective-permute-start(bf16[24,2048]{1,0:T(8,128)(2,1)S(1)} %get-tuple-element.117), channel_id=1, source_target_pairs={{24,18},{25,19},{26,16},{27,17},{28,22},{29,23},{30,20},{31,21}} | collective-permute-start | bytes 294920 | tf_op jit(solution)/shard_map/ppermute | solution.py:383
  36.3 3.4 %collective-permute-start.10 = (bf16[24,2048]{1,0:T(8,128)(2,1)S(1)}, bf16[24,2048]{1,0:T(8,128)(2,1)S(1)}, u32[]{:S(2)}, u32[]{:S(2)}) collective-permute-start(bf16[24,2048]{1,0:T(8,128)(2,1)S(1)} %get-tuple-element.120), channel_id=1, source_target_pairs={{24,20},{25,21},{26,22},{27,23},{28,16},{29,17},{30,18},{31,19}} | collective-permute-start | bytes 294920 | tf_op jit(solution)/shard_map/ppermute | solution.py:383
  37.0 2.7 %collective-permute-start.11 = (bf16[24,2048]{1,0:T(8,128)(2,1)S(1)}, bf16[24,2048]{1,0:T(8,128)(2,1)S(1)}, u32[]{:S(2)}, u32[]{:S(2)}) collective-permute-start(bf16[24,2048]{1,0:T(8,128)(2,1)S(1)} %get-tuple-element.121), channel_id=1, source_target_pairs={{24,21},{25,20},{26,23},{27,22},{28,17},{29,16},{30,19},{31,18}} | collective-permute-start | bytes 294920 | tf_op jit(solution)/shard_map/ppermute | solution.py:383
  37.7 2.1 %collective-permute-start.13 = (bf16[24,2048]{1,0:T(8,128)(2,1)S(1)}, bf16[24,2048]{1,0:T(8,128)(2,1)S(1)}, u32[]{:S(2)}, u32[]{:S(2)}) collective-permute-start(bf16[24,2048]{1,0:T(8,128)(2,1)S(1)} %get-tuple-element.123), channel_id=1, source_target_pairs={{24,23},{25,22},{26,21},{27,20},{28,19},{29,18},{30,17},{31,16}} | collective-permute-start | bytes 294920 | tf_op jit(solution)/shard_map/ppermute | solution.py:383
  38.4 1.4 %collective-permute-start.9 = (bf16[24,2048]{1,0:T(8,128)(2,1)S(1)}, bf16[24,2048]{1,0:T(8,128)(2,1)S(1)}, u32[]{:S(2)}, u32[]{:S(2)}) collective-permute-start(bf16[24,2048]{1,0:T(8,128)(2,1)S(1)} %get-tuple-element.119), channel_id=1, source_target_pairs={{24,19},{25,18},{26,17},{27,16},{28,23},{29,22},{30,21},{31,20}} | collective-permute-start | bytes 294920 | tf_op jit(solution)/shard_map/ppermute | solution.py:383
  39.1 0.7 collective-permute-start.12
  39.9 3.4 %collective-permute-start.14 = (bf16[24,2048]{1,0:T(8,128)(2,1)S(1)}, bf16[24,2048]{1,0:T(8,128)(2,1)S(1)}, u32[]{:S(2)}, u32[]{:S(2)}) collective-permute-start(bf16[24,2048]{1,0:T(8,128)(2,1)S(1)} %get-tuple-element.130), channel_id=1, source_target_pairs={{16,8},{17,9},{18,10},{19,11},{20,12},{21,13},{22,14},{23,15}} | collective-permute-start | bytes 294920 | tf_op jit(solution)/shard_map/ppermute | solution.py:383
  40.6 3.4 %collective-permute-start.15 = (bf16[24,2048]{1,0:T(8,128)(2,1)S(1)}, bf16[24,2048]{1,0:T(8,128)(2,1)S(1)}, u32[]{:S(2)}, u32[]{:S(2)}) collective-permute-start(bf16[24,2048]{1,0:T(8,128)(2,1)S(1)} %get-tuple-element.133), channel_id=1, source_target_pairs={{16,9},{17,8},{18,11},{19,10},{20,13},{21,12},{22,15},{23,14}} | collective-permute-start | bytes 294920 | tf_op jit(solution)/shard_map/ppermute | solution.py:383
  41.3 3.4 %collective-permute-start.16 = (bf16[24,2048]{1,0:T(8,128)(2,1)S(1)}, bf16[24,2048]{1,0:T(8,128)(2,1)S(1)}, u32[]{:S(2)}, u32[]{:S(2)}) collective-permute-start(bf16[24,2048]{1,0:T(8,128)(2,1)S(1)} %get-tuple-element.136), channel_id=1, source_target_pairs={{16,10},{17,11},{18,8},{19,9},{20,14},{21,15},{22,12},{23,13}} | collective-permute-start | bytes 294920 | tf_op jit(solution)/shard_map/ppermute | solution.py:383
  41.9 3.4 %collective-permute-start.18 = (bf16[24,2048]{1,0:T(8,128)(2,1)S(1)}, bf16[24,2048]{1,0:T(8,128)(2,1)S(1)}, u32[]{:S(2)}, u32[]{:S(2)}) collective-permute-start(bf16[24,2048]{1,0:T(8,128)(2,1)S(1)} %get-tuple-element.139), channel_id=1, source_target_pairs={{16,12},{17,13},{18,14},{19,15},{20,8},{21,9},{22,10},{23,11}} | collective-permute-start | bytes 294920 | tf_op jit(solution)/shard_map/ppermute | solution.py:383
  42.6 2.7 %collective-permute-start.19 = (bf16[24,2048]{1,0:T(8,128)(2,1)S(1)}, bf16[24,2048]{1,0:T(8,128)(2,1)S(1)}, u32[]{:S(2)}, u32[]{:S(2)}) collective-permute-start(bf16[24,2048]{1,0:T(8,128)(2,1)S(1)} %get-tuple-element.140), channel_id=1, source_target_pairs={{16,13},{17,12},{18,15},{19,14},{20,9},{21,8},{22,11},{23,10}} | collective-permute-start | bytes 294920 | tf_op jit(solution)/shard_map/ppermute | solution.py:383
  43.3 2.1 %collective-permute-start.21 = (bf16[24,2048]{1,0:T(8,128)(2,1)S(1)}, bf16[24,2048]{1,0:T(8,128)(2,1)S(1)}, u32[]{:S(2)}, u32[]{:S(2)}) collective-permute-start(bf16[24,2048]{1,0:T(8,128)(2,1)S(1)} %get-tuple-element.142), channel_id=1, source_target_pairs={{16,15},{17,14},{18,13},{19,12},{20,11},{21,10},{22,9},{23,8}} | collective-permute-start | bytes 294920 | tf_op jit(solution)/shard_map/ppermute | solution.py:383
  44.0 1.4 %collective-permute-start.17 = (bf16[24,2048]{1,0:T(8,128)(2,1)S(1)}, bf16[24,2048]{1,0:T(8,128)(2,1)S(1)}, u32[]{:S(2)}, u32[]{:S(2)}) collective-permute-start(bf16[24,2048]{1,0:T(8,128)(2,1)S(1)} %get-tuple-element.138), channel_id=1, source_target_pairs={{16,11},{17,10},{18,9},{19,8},{20,15},{21,14},{22,13},{23,12}} | collective-permute-start | bytes 294920 | tf_op jit(solution)/shard_map/ppermute | solution.py:383
  44.7 0.7 collective-permute-start.20
  45.7 37.1 %collective-permute-start.22 = (bf16[24,2048]{1,0:T(8,128)(2,1)S(1)}, bf16[24,2048]{1,0:T(8,128)(2,1)S(1)}, u32[]{:S(2)}, u32[]{:S(2)}) collective-permute-start(bf16[24,2048]{1,0:T(8,128)(2,1)S(1)} %get-tuple-element.146), channel_id=1, source_target_pairs={{8,0},{9,1},{10,2},{11,3},{12,4},{13,5},{14,6},{15,7}} | collective-permute-start | bytes 294920 | tf_op jit(solution)/shard_map/ppermute | solution.py:383
  47.0 39.0 %collective-permute-start.23 = (bf16[24,2048]{1,0:T(8,128)(2,1)S(1)}, bf16[24,2048]{1,0:T(8,128)(2,1)S(1)}, u32[]{:S(2)}, u32[]{:S(2)}) collective-permute-start(bf16[24,2048]{1,0:T(8,128)(2,1)S(1)} %get-tuple-element.149), channel_id=1, source_target_pairs={{8,1},{9,0},{10,3},{11,2},{12,5},{13,4},{14,7},{15,6}} | collective-permute-start | bytes 294920 | tf_op jit(solution)/shard_map/ppermute | solution.py:383
  48.3 40.2 %collective-permute-start.24 = (bf16[24,2048]{1,0:T(8,128)(2,1)S(1)}, bf16[24,2048]{1,0:T(8,128)(2,1)S(1)}, u32[]{:S(2)}, u32[]{:S(2)}) collective-permute-start(bf16[24,2048]{1,0:T(8,128)(2,1)S(1)} %get-tuple-element.152), channel_id=1, source_target_pairs={{8,2},{9,3},{10,0},{11,1},{12,6},{13,7},{14,4},{15,5}} | collective-permute-start | bytes 294920 | tf_op jit(solution)/shard_map/ppermute | solution.py:383
  49.6 43.1 %collective-permute-start.26 = (bf16[24,2048]{1,0:T(8,128)(2,1)S(1)}, bf16[24,2048]{1,0:T(8,128)(2,1)S(1)}, u32[]{:S(2)}, u32[]{:S(2)}) collective-permute-start(bf16[24,2048]{1,0:T(8,128)(2,1)S(1)} %get-tuple-element.155), channel_id=1, source_target_pairs={{8,4},{9,5},{10,6},{11,7},{12,0},{13,1},{14,2},{15,3}} | collective-permute-start | bytes 294920 | tf_op jit(solution)/shard_map/ppermute | solution.py:383
  50.9 43.1 %collective-permute-start.27 = (bf16[24,2048]{1,0:T(8,128)(2,1)S(1)}, bf16[24,2048]{1,0:T(8,128)(2,1)S(1)}, u32[]{:S(2)}, u32[]{:S(2)}) collective-permute-start(bf16[24,2048]{1,0:T(8,128)(2,1)S(1)} %get-tuple-element.156), channel_id=1, source_target_pairs={{8,5},{9,4},{10,7},{11,6},{12,1},{13,0},{14,3},{15,2}} | collective-permute-start | bytes 294920 | tf_op jit(solution)/shard_map/ppermute | solution.py:383
  82.8 11.2 %collective-permute-start.29 = (bf16[24,2048]{1,0:T(8,128)(2,1)S(1)}, bf16[24,2048]{1,0:T(8,128)(2,1)S(1)}, u32[]{:S(2)}, u32[]{:S(2)}) collective-permute-start(bf16[24,2048]{1,0:T(8,128)(2,1)S(1)} %get-tuple-element.158), channel_id=1, source_target_pairs={{8,7},{9,6},{10,5},{11,4},{12,3},{13,2},{14,1},{15,0}} | collective-permute-start | bytes 294920 | tf_op jit(solution)/shard_map/ppermute | solution.py:383
  85.9 9.0 %collective-permute-start.25 = (bf16[24,2048]{1,0:T(8,128)(2,1)S(1)}, bf16[24,2048]{1,0:T(8,128)(2,1)S(1)}, u32[]{:S(2)}, u32[]{:S(2)}) collective-permute-start(bf16[24,2048]{1,0:T(8,128)(2,1)S(1)} %get-tuple-element.154), channel_id=1, source_target_pairs={{8,3},{9,2},{10,1},{11,0},{12,7},{13,6},{14,5},{15,4}} | collective-permute-start | bytes 294920 | tf_op jit(solution)/shard_map/ppermute | solution.py:383
  88.4 7.8 %collective-permute-start.28 = (bf16[24,2048]{1,0:T(8,128)(2,1)S(1)}, bf16[24,2048]{1,0:T(8,128)(2,1)S(1)}, u32[]{:S(2)}, u32[]{:S(2)}) collective-permute-start(bf16[24,2048]{1,0:T(8,128)(2,1)S(1)} %get-tuple-element.157), channel_id=1, source_target_pairs={{8,6},{9,7},{10,4},{11,5},{12,2},{13,3},{14,0},{15,1}} | collective-permute-start | bytes 294920 | tf_op jit(solution)/shard_map/ppermute | solution.py:383
  96.3 17.4 %copy-start.2 = (bf16[1,2048,64]{1,2,0:T(8,128)(2,1)S(1)}, bf16[1,2048,64]{1,2,0:T(8,128)(2,1)}, u32[]{:S(2)}) copy-start(bf16[1,2048,64]{1,2,0:T(8,128)(2,1)} %param.21) | copy-start | bytes 786436
  96.3 17.4 %copy-start.9 = (bf16[1,1536,64]{1,2,0:T(8,128)(2,1)S(1)}, bf16[1,1536,64]{1,2,0:T(8,128)(2,1)}, u32[]{:S(2)}) copy-start(bf16[1,1536,64]{1,2,0:T(8,128)(2,1)} %param.20) | copy-start | bytes 589828
  102.1 11.6 %all-to-all-start.9 = ((bf16[8,8,2048]{2,1,0:T(8,128)(2,1)}), bf16[8,8,2048]{2,1,0:T(8,128)(2,1)S(1)}, u32[]{:S(2)}, u32[]{:S(2)}) async-start(bf16[8,8,2048]{2,1,0:T(8,128)(2,1)} %bitcast.43), calls=%async_computation.9 | async-start | bytes 524288 | tf_op jit(solution)/shard_map/all_to_all | solution.py:487
